TPU v7x, 32 devices: a whole 2x2x4 slice. The times are simulated.
32 devices in a mesh: tm: 8 (over z, x), height: 4 (over y, core).
Axes of the slice: x: 2, y: 2, z: 4, core: 2. Of those that a mesh axis runs over, the one named last changes fastest.
Arguments:
- latents: bfloat16 [16, 32, 104, 256], P('tm', 'height'), may hold values from -45 to 45
- first_gain: bfloat16 [256], replicated, may hold values from 0.099609375 to 1.8984375
- first_kernel: bfloat16 [3, 3, 3, 256, 256], replicated, may hold values from -0.078125 to 0.078125
- first_bias: bfloat16 [256], replicated, may hold values from -3 to 3
- second_gain: bfloat16 [256], replicated, may hold values from 0.099609375 to 1.8984375
- second_kernel: bfloat16 [3, 3, 3, 256, 256], replicated, may hold values from -0.078125 to 0.078125
- second_bias: bfloat16 [256], replicated, may hold values from -3 to 3
Outputs:
- decoded: bfloat16 [16, 32, 104, 256], P('tm', 'height')
All inputs are finite; a program needn't handle non-finite values.
Results may differ from a plain program's by a relative error of at most 0.0055.
Values may be sent and summed in bfloat16 or wider, within the bound.
No kernel may reach another device: no remote copies, remote signals or barrier semaphores. Data moves between devices by JAX's collectives and lax.ppermute only.
A program may use at most 64 MiB of HBM per device.

v0:
```python
import jax
import jax.numpy as jnp
from jax import lax
from jax.sharding import PartitionSpec as P

EPSILON = 1e-06


def shifted(block, axis, distance):
    devices = range(lax.axis_size(axis))
    route = [(i - distance, i) for i in devices if i - distance in devices]
    return lax.ppermute(block, axis, route)


def padded_2(array, sides, width):
    for axis, dim in sides:
        peers, length = (lax.axis_size(axis), array.shape[dim])
        up = [(i, (i + 1) % peers) for i in range(peers - 1)]
        down = [(j, i) for i, j in up]
        last = lax.slice_in_dim(array, length - width, length, axis=dim)
        initial = lax.slice_in_dim(array, 0, width, axis=dim)
        before = lax.ppermute(last, axis, up)
        after = lax.ppermute(initial, axis, down)
        array = jnp.concatenate([before, array, after], axis=dim)
    return array


def activate(field, gain):
    values = field.astype(jnp.float32)
    mean_power = jnp.mean(jnp.square(values), axis=-1, keepdims=True)
    normed = values * lax.rsqrt(mean_power + EPSILON) * gain.astype(jnp.float32)
    return jax.nn.silu(normed).astype(jnp.bfloat16)


def borders(block):
    cached = shifted(block, "tm", 1)
    longer = jnp.concatenate([cached, block], 0)
    return padded_2(longer, (("height", 1),), 1)


def causal_conv(widened, kernel, bias):
    frames = widened.shape[0] - 2
    rows = widened.shape[1] - 2
    cells = widened.shape[2]
    channels = widened.shape[3]
    padded = jnp.pad(widened, ((0, 0), (0, 0), (1, 1), (0, 0)))
    total = jnp.zeros((frames * rows * cells, channels), jnp.float32)
    for tap_time in range(3):
        for tap_row in range(3):
            columns = jnp.concatenate(
                [
                    padded[
                        tap_time : tap_time + frames,
                        tap_row : tap_row + rows,
                        tap_col : tap_col + cells,
                    ]
                    for tap_col in range(3)
                ],
                -1,
            )
            columns = columns.reshape(frames * rows * cells, 3 * channels)
            taps = kernel[tap_time, tap_row].reshape(3 * channels, channels)
            total = total + jnp.dot(columns, taps, preferred_element_type=jnp.float32)
    return total.reshape(frames, rows, cells, channels) + bias.astype(jnp.float32)


def section(block, gain, kernel, bias):
    widened = borders(activate(block, gain))
    return causal_conv(widened, kernel, bias)


def per_device(
    latents, first_gain, first_kernel, first_bias, second_gain, second_kernel, second_bias
):
    first_out = section(latents, first_gain, first_kernel, first_bias).astype(jnp.bfloat16)
    second_out = section(first_out, second_gain, second_kernel, second_bias)
    return (latents.astype(jnp.float32) + second_out).astype(jnp.bfloat16)


def solution(mesh):
    return jax.shard_map(
        per_device,
        mesh=mesh,
        in_specs=(P("tm", "height", None, None), P(), P(), P(), P(), P(), P()),
        out_specs=P("tm", "height", None, None),
        check_vma=False,
    )
```

profile of v0, /device:TPU:17, one launch (start us, length us, event | category | flops | bytes accessed | tf_op | source)
XLA Modules:
  0.0 113.1 jit_solution(9165984368340111341)
XLA Ops:
  0.0 1.6 %fusion.15 = f32[2,8,104]{2,1,0:T(8,128)S(1)} fusion(bf16[2,8,104,256]{3,2,1,0:T(8,128)(2,1)} %param.7), kind=kLoop, calls=%fused_computation.60 | loop fusion | flops 1276288 | bytes 858624 | tf_op jit(solution)/shard_map/reduce_sum | solution.py:30
  1.7 0.7 convert_element_type.41
  2.3 1.7 %fusion.22 = bf16[2,8,104,256]{3,2,1,0:T(8,128)(2,1)S(1)} fusion(bf16[2,8,104,256]{3,2,1,0:T(8,128)(2,1)} %param.7, f32[256]{0:T(256)S(1)} %convert_element_type.41, f32[2,8,104]{2,1,0:T(8,128)S(1)} %add_rsqrt_fusion.1), kind=kLoop, calls=%fused_computation.67 | loop fusion | flops 3407872 | bytes 1711616 | tf_op jit(solution)/shard_map/convert_element_type | solution.py:32
  4.1 3.1 %collective-permute-start = (bf16[2,8,104,256]{3,2,1,0:T(8,128)(2,1)S(1)}, bf16[2,8,104,256]{3,2,1,0:T(8,128)(2,1)S(1)}, u32[]{:S(2)}, u32[]{:S(2)}) collective-permute-start(bf16[2,8,104,256]{3,2,1,0:T(8,128)(2,1)S(1)} %fusion.22), channel_id=1, source_target_pairs={{0,4},{4,8},{8,12},{12,16},{16,20},{20,24},{24,28},{1,5},{5,9},{9,... | collective-permute-start | bytes 2555912 | tf_op jit(solution)/shard_map/ppermute | solution.py:12
  7.2 19.4 %collective-permute-done = bf16[2,8,104,256]{3,2,1,0:T(8,128)(2,1)S(1)} collective-permute-done((bf16[2,8,104,256]{3,2,1,0:T(8,128)(2,1)S(1)}, bf16[2,8,104,256]{3,2,1,0:T(8,128)(2,1)S(1)}, u32[]{:S(2)}, u32[]{:S(2)}) %collective-permute-start) | collective-permute-done | bytes 852000 | tf_op jit(solution)/shard_map/ppermute | solution.py:12
  26.7 4.6 %collective-permute-start.1 = (bf16[4,1,104,256]{3,2,1,0:T(8,128)(2,1)S(1)}, bf16[4,1,104,256]{3,2,1,0:T(8,128)(2,1)S(1)}, u32[]{:S(2)}, u32[]{:S(2)}) collective-permute-start(bf16[4,1,104,256]{3,2,1,0:T(8,128)(2,1)S(1)} %get-tuple-element.77), channel_id=1, source_target_pairs={{0,1},{1,2},{2,3},{4,5},{5,6},{6,7},{8,9},{9,10},{10,11},{12,13},{... | collective-permute-start | bytes 638984 | tf_op jit(solution)/shard_map/ppermute | solution.py:22
  31.3 1.9 %collective-permute-start.2 = (bf16[4,1,104,256]{3,2,1,0:T(8,128)(2,1)S(1)}, bf16[4,1,104,256]{3,2,1,0:T(8,128)(2,1)S(1)}, u32[]{:S(2)}, u32[]{:S(2)}) collective-permute-start(bf16[4,1,104,256]{3,2,1,0:T(8,128)(2,1)S(1)} %get-tuple-element.78), channel_id=1, source_target_pairs={{1,0},{2,1},{3,2},{5,4},{6,5},{7,6},{9,8},{10,9},{11,10},{13,12},{... | collective-permute-start | bytes 638984 | tf_op jit(solution)/shard_map/ppermute | solution.py:23
  33.2 1.7 %fusion.25 = (bf16[1,1,3,256,256]{4,3,2,1,0:T(8,128)(2,1)S(1)}, bf16[1,1,3,256,256]{4,3,2,1,0:T(8,128)(2,1)}, bf16[1,1,3,256,256]{4,3,2,1,0:T(8,128)(2,1)}, bf16...) fusion(bf16[3,3,3,256,256]{4,3,2,1,0:T(8,128)(2,1)S(1)} %copy-d, ...), kind=kLoop, calls=%fused_computation.80 | loop fusion | bytes 7077888 | tf_op jit(solution)/shard_map/slice | solution.py:62
  35.0 3.5 %collective-permute-done.2 = bf16[4,1,104,256]{3,2,1,0:T(8,128)(2,1)S(1)} collective-permute-done((bf16[4,1,104,256]{3,2,1,0:T(8,128)(2,1)S(1)}, bf16[4,1,104,256]{3,2,1,0:T(8,128)(2,1)S(1)}, u32[]{:S(2)}, u32[]{:S(2)}) %collective-permute-start.2) | collective-permute-done | bytes 213024 | tf_op jit(solution)/shard_map/ppermute | solution.py:23
  38.5 1.0 fusion.12
  39.4 5.5 %fusion.27 = (bf16[2,8,104,256]{3,2,1,0:T(8,128)(2,1)S(1)}, bf16[2,8,104,256]{3,2,1,0:T(8,128)(2,1)S(1)}, bf16[2,8,104,256]{3,2,1,0:T(8,128)(2,1)S(1)}, bf16[2,8...) fusion(bf16[4,10,106,256]{3,2,1,0:T(8,128)(2,1)S(1)} %fusion.12), kind=kLoop, calls=%fused_computation.82 | loop fusion | bytes 30670848 | tf_op jit(solution)/shard_map/slice | solution.py:52
  44.9 0.9 pad_maximum_fusion.18
  45.8 0.4 fusion.30
  46.3 0.2 pad_maximum_fusion.2
  46.5 0.8 copy-done.21
  47.3 0.8 fusion.32
  48.1 1.0 pad_maximum_fusion.8
  49.1 0.9 convolution_add_fusion.15
  50.0 0.2 pad_maximum_fusion.4
  50.2 0.8 copy-done.19
  51.0 0.8 convolution_add_fusion.14
  51.9 0.2 pad_maximum_fusion.5
  52.0 0.8 copy-done.18
  52.8 0.8 convolution_add_fusion.13
  53.8 0.9 convolution_add_fusion.12
  54.8 0.2 pad_maximum_fusion.6
  54.9 0.8 copy-done.15
  55.7 0.8 convolution_add_fusion.11
  56.6 0.2 pad_maximum_fusion.7
  56.8 0.8 copy-done.12
  57.6 0.8 convolution_add_fusion.10
  58.6 0.9 convolution_add_fusion.9
  59.5 0.2 pad_maximum_fusion.9
  59.7 0.9 multiply_reduce_fusion
  60.7 0.6 multiply_convert_fusion
  61.3 2.4 %collective-permute-start.3 = (bf16[2,8,104,256]{3,2,1,0:T(8,128)(2,1)S(1)}, bf16[2,8,104,256]{3,2,1,0:T(8,128)(2,1)S(1)}, u32[]{:S(2)}, u32[]{:S(2)}) collective-permute-start(bf16[2,8,104,256]{3,2,1,0:T(8,128)(2,1)S(1)} %multiply_convert_fusion), channel_id=1, source_target_pairs={{0,4},{4,8},{8,12},{12,16},{16,20},{20,24},{24,28},{1,5},{5,9},{9,... | collective-permute-start | bytes 2555912 | tf_op jit(solution)/shard_map/ppermute | solution.py:12
  63.7 17.9 %collective-permute-done.3 = bf16[2,8,104,256]{3,2,1,0:T(8,128)(2,1)S(1)} collective-permute-done((bf16[2,8,104,256]{3,2,1,0:T(8,128)(2,1)S(1)}, bf16[2,8,104,256]{3,2,1,0:T(8,128)(2,1)S(1)}, u32[]{:S(2)}, u32[]{:S(2)}) %collective-permute-start.3) | collective-permute-done | bytes 852000 | tf_op jit(solution)/shard_map/ppermute | solution.py:12
  81.6 2.5 %collective-permute-start.4 = (bf16[4,1,104,256]{3,2,1,0:T(8,128)(2,1)S(1)}, bf16[4,1,104,256]{3,2,1,0:T(8,128)(2,1)S(1)}, u32[]{:S(2)}, u32[]{:S(2)}) collective-permute-start(bf16[4,1,104,256]{3,2,1,0:T(8,128)(2,1)S(1)} %get-tuple-element.73), channel_id=1, source_target_pairs={{0,1},{1,2},{2,3},{4,5},{5,6},{6,7},{8,9},{9,10},{10,11},{12,13},{... | collective-permute-start | bytes 638984 | tf_op jit(solution)/shard_map/ppermute | solution.py:22
  84.0 1.9 %collective-permute-start.5 = (bf16[4,1,104,256]{3,2,1,0:T(8,128)(2,1)S(1)}, bf16[4,1,104,256]{3,2,1,0:T(8,128)(2,1)S(1)}, u32[]{:S(2)}, u32[]{:S(2)}) collective-permute-start(bf16[4,1,104,256]{3,2,1,0:T(8,128)(2,1)S(1)} %get-tuple-element.74), channel_id=1, source_target_pairs={{1,0},{2,1},{3,2},{5,4},{6,5},{7,6},{9,8},{10,9},{11,10},{13,12},{... | collective-permute-start | bytes 638984 | tf_op jit(solution)/shard_map/ppermute | solution.py:23
  86.0 1.6 %fusion.24 = (bf16[1,1,3,256,256]{4,3,2,1,0:T(8,128)(2,1)S(1)}, bf16[1,1,3,256,256]{4,3,2,1,0:T(8,128)(2,1)}, bf16[1,1,3,256,256]{4,3,2,1,0:T(8,128)(2,1)}, bf16...) fusion(bf16[3,3,3,256,256]{4,3,2,1,0:T(8,128)(2,1)S(1)} %copy-d, ...), kind=kLoop, calls=%fused_computation.79 | loop fusion | bytes 7077888 | tf_op jit(solution)/shard_map/slice | solution.py:62
  87.6 3.6 %collective-permute-done.5 = bf16[4,1,104,256]{3,2,1,0:T(8,128)(2,1)S(1)} collective-permute-done((bf16[4,1,104,256]{3,2,1,0:T(8,128)(2,1)S(1)}, bf16[4,1,104,256]{3,2,1,0:T(8,128)(2,1)S(1)}, u32[]{:S(2)}, u32[]{:S(2)}) %collective-permute-start.5) | collective-permute-done | bytes 213024 | tf_op jit(solution)/shard_map/ppermute | solution.py:23
  91.2 0.9 pad_maximum_fusion.19
  92.1 0.2 fusion.28
  92.3 1.0 select_maximum_fusion
  93.3 5.8 %fusion.26 = (bf16[2,8,104,256]{3,2,1,0:T(8,128)(2,1)}, bf16[2,8,104,256]{3,2,1,0:T(8,128)(2,1)S(1)}, bf16[2,8,104,256]{3,2,1,0:T(8,128)(2,1)S(1)}, bf16[2,8,104...) fusion(bf16[4,10,106,256]{3,2,1,0:T(8,128)(2,1)S(1)} %select_ma, ...), kind=kLoop, calls=%fused_computation.81 | loop fusion | bytes 30670848 | tf_op jit(solution)/shard_map/slice | solution.py:52
  99.3 0.2 pad_maximum_fusion.10
  99.5 0.8 fusion.33
  100.3 0.3 copy-done.5
  100.6 0.3 copy-done.6
  101.0 1.0 copy-done.3
  102.0 0.3 copy-done.4
  102.4 0.2 pad_maximum_fusion.14
  102.6 0.2 pad_maximum_fusion.13
  103.0 1.0 pad_maximum_fusion.16
  104.0 0.8 convolution_add_fusion.7
  105.0 0.8 convolution_add_fusion.6
  106.0 0.8 convolution_add_fusion.5
  107.0 0.8 convolution_add_fusion.4
  108.0 0.9 convolution_add_fusion.3
  109.0 0.9 convolution_add_fusion.2
  110.0 0.8 convolution_add_fusion.1
  110.9 0.9 convolution_add_fusion
  111.8 0.2 copy-done
  112.0 1.1 %fusion.23 = bf16[2,8,104,256]{3,2,1,0:T(8,128)(2,1)} fusion(bf16[2,8,104,256]{3,2,1,0:T(8,128)(2,1)S(1)} %copy-done, f32[2,8,104,256]{3,2,1,0:T(8,128)S(1)} %bitcast.93, f32[256]{0:T(256)S(1)} %convert_element_type.50), kind=kLoop, calls=%fused_computation.68 | loop fusion | flops 1703936 | bytes 3408896 | tf_op jit(solution)/shard_map/convert_element_type | solution.py:77
  (54 shorter events, 2.0 us)
Async XLA Ops:
  0.0 7.2 %copy-start.22 = (bf16[256]{0:T(256)(128)(2,1)S(1)}, bf16[256]{0:T(256)(128)(2,1)}, u32[]{:S(2)}) copy-start(bf16[256]{0:T(256)(128)(2,1)} %param.10) | copy-start | bytes 1540
  0.0 7.2 %copy-start.23 = (bf16[256]{0:T(256)(128)(2,1)S(1)}, bf16[256]{0:T(256)(128)(2,1)}, u32[]{:S(2)}) copy-start(bf16[256]{0:T(256)(128)(2,1)} %param.11) | copy-start | bytes 1540
  0.0 33.2 %copy-start.1 = (bf16[3,3,3,256,256]{4,3,2,1,0:T(8,128)(2,1)S(1)}, bf16[3,3,3,256,256]{4,3,2,1,0:T(8,128)(2,1)}, u32[]{:S(2)}) copy-start(bf16[3,3,3,256,256]{4,3,2,1,0:T(8,128)(2,1)} %param.9) | copy-start | bytes 10616836
  4.1 22.6 %collective-permute-start = (bf16[2,8,104,256]{3,2,1,0:T(8,128)(2,1)S(1)}, bf16[2,8,104,256]{3,2,1,0:T(8,128)(2,1)S(1)}, u32[]{:S(2)}, u32[]{:S(2)}) collective-permute-start(bf16[2,8,104,256]{3,2,1,0:T(8,128)(2,1)S(1)} %fusion.22), channel_id=1, source_target_pairs={{0,4},{4,8},{8,12},{12,16},{16,20},{20,24},{24,28},{1,5},{5,9},{9,... | collective-permute-start | bytes 2555912 | tf_op jit(solution)/shard_map/ppermute | solution.py:12
  26.7 8.2 %collective-permute-start.1 = (bf16[4,1,104,256]{3,2,1,0:T(8,128)(2,1)S(1)}, bf16[4,1,104,256]{3,2,1,0:T(8,128)(2,1)S(1)}, u32[]{:S(2)}, u32[]{:S(2)}) collective-permute-start(bf16[4,1,104,256]{3,2,1,0:T(8,128)(2,1)S(1)} %get-tuple-element.77), channel_id=1, source_target_pairs={{0,1},{1,2},{2,3},{4,5},{5,6},{6,7},{8,9},{9,10},{10,11},{12,13},{... | collective-permute-start | bytes 638984 | tf_op jit(solution)/shard_map/ppermute | solution.py:22
  31.3 7.2 %collective-permute-start.2 = (bf16[4,1,104,256]{3,2,1,0:T(8,128)(2,1)S(1)}, bf16[4,1,104,256]{3,2,1,0:T(8,128)(2,1)S(1)}, u32[]{:S(2)}, u32[]{:S(2)}) collective-permute-start(bf16[4,1,104,256]{3,2,1,0:T(8,128)(2,1)S(1)} %get-tuple-element.78), channel_id=1, source_target_pairs={{1,0},{2,1},{3,2},{5,4},{6,5},{7,6},{9,8},{10,9},{11,10},{13,12},{... | collective-permute-start | bytes 638984 | tf_op jit(solution)/shard_map/ppermute | solution.py:23
  46.3 1.0 copy-start.21
  48.1 1.0 copy-start.20
  50.0 1.0 copy-start.19
  51.8 1.0 copy-start.18
  52.8 1.0 copy-start.17
  54.7 1.0 copy-start.15
  56.6 1.0 copy-start.12
  57.6 1.0 copy-start.10
  60.6 3.1 %copy-start.24 = (bf16[256]{0:T(256)(128)(2,1)S(1)}, bf16[256]{0:T(256)(128)(2,1)}, u32[]{:S(2)}) copy-start(bf16[256]{0:T(256)(128)(2,1)} %param.13) | copy-start | bytes 1540
  60.7 25.3 %copy-start.2 = (bf16[3,3,3,256,256]{4,3,2,1,0:T(8,128)(2,1)S(1)}, bf16[3,3,3,256,256]{4,3,2,1,0:T(8,128)(2,1)}, u32[]{:S(2)}) copy-start(bf16[3,3,3,256,256]{4,3,2,1,0:T(8,128)(2,1)} %param.12) | copy-start | bytes 10616836
  61.3 20.3 %collective-permute-start.3 = (bf16[2,8,104,256]{3,2,1,0:T(8,128)(2,1)S(1)}, bf16[2,8,104,256]{3,2,1,0:T(8,128)(2,1)S(1)}, u32[]{:S(2)}, u32[]{:S(2)}) collective-permute-start(bf16[2,8,104,256]{3,2,1,0:T(8,128)(2,1)S(1)} %multiply_convert_fusion), channel_id=1, source_target_pairs={{0,4},{4,8},{8,12},{12,16},{16,20},{20,24},{24,28},{1,5},{5,9},{9,... | collective-permute-start | bytes 2555912 | tf_op jit(solution)/shard_map/ppermute | solution.py:12
  81.6 6.0 %collective-permute-start.4 = (bf16[4,1,104,256]{3,2,1,0:T(8,128)(2,1)S(1)}, bf16[4,1,104,256]{3,2,1,0:T(8,128)(2,1)S(1)}, u32[]{:S(2)}, u32[]{:S(2)}) collective-permute-start(bf16[4,1,104,256]{3,2,1,0:T(8,128)(2,1)S(1)} %get-tuple-element.73), channel_id=1, source_target_pairs={{0,1},{1,2},{2,3},{4,5},{5,6},{6,7},{8,9},{9,10},{10,11},{12,13},{... | collective-permute-start | bytes 638984 | tf_op jit(solution)/shard_map/ppermute | solution.py:22
  84.0 7.2 %collective-permute-start.5 = (bf16[4,1,104,256]{3,2,1,0:T(8,128)(2,1)S(1)}, bf16[4,1,104,256]{3,2,1,0:T(8,128)(2,1)S(1)}, u32[]{:S(2)}, u32[]{:S(2)}) collective-permute-start(bf16[4,1,104,256]{3,2,1,0:T(8,128)(2,1)S(1)} %get-tuple-element.74), channel_id=1, source_target_pairs={{1,0},{2,1},{3,2},{5,4},{6,5},{7,6},{9,8},{10,9},{11,10},{13,12},{... | collective-permute-start | bytes 638984 | tf_op jit(solution)/shard_map/ppermute | solution.py:23
  99.4 1.2 %copy-start.5 = (bf16[2,8,104,256]{3,2,1,0:T(8,128)(2,1)S(1)}, bf16[2,8,104,256]{3,2,1,0:T(8,128)(2,1)}, u32[]{:S(2)}) copy-start(bf16[2,8,104,256]{3,2,1,0:T(8,128)(2,1)} %get-tuple-element.23) | copy-start | bytes 2555908
  99.5 1.4 %copy-start.6 = (bf16[2,8,104,256]{3,2,1,0:T(8,128)(2,1)S(1)}, bf16[2,8,104,256]{3,2,1,0:T(8,128)(2,1)}, u32[]{:S(2)}) copy-start(bf16[2,8,104,256]{3,2,1,0:T(8,128)(2,1)} %get-tuple-element.40) | copy-start | bytes 2555908
  100.9 1.2 %copy-start.3 = (bf16[2,8,104,256]{3,2,1,0:T(8,128)(2,1)S(1)}, bf16[2,8,104,256]{3,2,1,0:T(8,128)(2,1)}, u32[]{:S(2)}) copy-start(bf16[2,8,104,256]{3,2,1,0:T(8,128)(2,1)} %get-tuple-element.26) | copy-start | bytes 2555908
  100.9 1.4 %copy-start.4 = (bf16[2,8,104,256]{3,2,1,0:T(8,128)(2,1)S(1)}, bf16[2,8,104,256]{3,2,1,0:T(8,128)(2,1)}, u32[]{:S(2)}) copy-start(bf16[2,8,104,256]{3,2,1,0:T(8,128)(2,1)} %get-tuple-element.27) | copy-start | bytes 2555908
  103.0 1.0 copy-start.16
  104.0 1.0 copy-start.14
  105.0 1.0 copy-start.13
  106.0 1.0 copy-start.11
  107.0 1.0 copy-start.9
  108.0 1.0 copy-start.8
  109.0 1.0 copy-start.7
  110.8 1.2 %copy-start = (bf16[2,8,104,256]{3,2,1,0:T(8,128)(2,1)S(1)}, bf16[2,8,104,256]{3,2,1,0:T(8,128)(2,1)}, u32[]{:S(2)}) copy-start(bf16[2,8,104,256]{3,2,1,0:T(8,128)(2,1)} %param.7) | copy-start | bytes 2555908
where the time goes:
time: 114 us; the launch traced here: 113 us
  waiting for transfers between devices  44.5 us (39%)
  local copies, waits for them, and re-layouts  22.7 us (20%)
  starting transfers between devices  16.3 us (14%)
  matrix products  15.5 us (14%)
  other arithmetic  13.5 us (12%)
    ppermute x2, waiting for transfers between devices, shifted(): return lax.ppermute(block, axis, route)  37.3 us
    dot_general x18, matrix products, causal_conv(): total = total + jnp.dot(columns, taps, preferred_element_type=jnp.float32)  15.5 us
    slice x5, local copies, waits for them, and re-layouts, causal_conv(): padded[tap_time:tap_time + frames, tap_row:tap_row + rows, tap_col:tap_co...  12.1 us
    unnamed x50, local copies, waits for them, and re-layouts  7.28 us
    ppermute x2, waiting for transfers between devices, padded_2(): after = lax.ppermute(initial, axis, down)  7.15 us
    ppermute x2, starting transfers between devices, padded_2(): before = lax.ppermute(last, axis, up)  7.03 us
    ppermute x2, starting transfers between devices, shifted(): return lax.ppermute(block, axis, route)  5.47 us
    concatenate x14, other arithmetic, causal_conv(): jnp.concatenate([padded[tap_time:tap_time + frames, tap_row:tap_row + row...  3.98 us
  transfers between devices with their start and end apart: 6, of which 4 were waited for; matrix products, arithmetic and copies ran while one was open for 3% of the time, Pallas kernels for 0%

commit v1 on v0

v1 whole, which is shorter than its diff:
```python
import functools

import jax
import jax.numpy as jnp
from jax import lax
from jax.experimental import pallas as pl
from jax.experimental.pallas import tpu as pltpu
from jax.sharding import PartitionSpec as P

EPSILON = 1e-06
BF16, F32 = jnp.bfloat16, jnp.float32
VMEM_LIMIT = 26 * 2**20
CHUNK = 2


def ring(axis, step):
    peers = lax.axis_size(axis)
    return [(i, (i + step) % peers) for i in range(peers)]


def activate_rows(get_row, gain, shifts, rows, cells):
    for r in range(rows):
        values, mask = get_row(r)
        values = values.astype(F32)
        mean_power = jnp.mean(values * values, axis=-1, keepdims=True)
        normed = values * lax.rsqrt(mean_power + EPSILON) * gain
        act = normed / (1.0 + jnp.exp(-normed))
        if mask is not None:
            act = act * mask
        cell = lax.broadcasted_iota(jnp.int32, act.shape, 0)
        here = slice(r * cells, (r + 1) * cells)
        shifts[0, here, :] = jnp.where(cell == 0, 0.0, pltpu.roll(act, 1, 0))
        shifts[1, here, :] = act
        shifts[2, here, :] = jnp.where(cell == cells - 1, 0.0, pltpu.roll(act, cells - 1, 0))


def pack(shifts, even, odd, rows, cells):
    channels = shifts.shape[-1]
    pair = 2 * cells
    for buf, first, count in ((even, 0, rows // 2), (odd, cells, rows // 2 - 1)):
        for k in range(count):
            for l in range(3):
                buf[k * pair : (k + 1) * pair, l * channels : (l + 1) * channels] = shifts[
                    l, first + k * pair : first + (k + 1) * pair, :
                ].astype(BF16)


def taps(even, odd, kernel, start, length, cells):
    dot = functools.partial(jnp.dot, preferred_element_type=F32)
    lower = 2 * cells + start
    return (
        dot(even[start : start + length], kernel[0, 0])
        + dot(odd[start : start + length], kernel[0, 1])
        + dot(even[lower : lower + length], kernel[0, 2])
    )


def masks():
    row_id, rows = lax.axis_index("height"), lax.axis_size("height")
    above = (row_id > 0).astype(F32)
    below = (row_id < rows - 1).astype(F32)
    before = (lax.axis_index("tm") > 0).astype(F32)
    return above, below, before


def load_frame(frame, up, down, gain, bufs, time_halo):
    shifts, even, odd = bufs
    rows, cells = frame.shape[0], frame.shape[1]
    above, below, before = masks()
    if time_halo:
        above, below = above * before, below * before

    def get_row(r):
        if r == 0:
            return up, above
        if r == rows + 1:
            return down, below
        return frame[r - 1], before if time_halo else None

    activate_rows(get_row, gain[...].astype(F32), shifts, rows + 2, cells)
    pack(shifts, even, odd, rows + 2, cells)


def chunks(rows, cells):
    step = 4 * cells if rows % 4 == 0 else 2 * cells
    return [(s, step) for s in range(0, rows * cells, step)]


def own_kernel(last_ref, first_ref, up, down, gain, k1, k2, acc_first, acc_last, *bufs):
    last, first = last_ref.at[0], first_ref.at[0]
    rows, cells = last.shape[0], last.shape[1]
    even, odd = bufs[1:]
    load_frame(last, up[1], down[1], gain, bufs, False)
    for s, n in chunks(rows, cells):
        acc_last[s : s + n] = taps(even, odd, k2, s, n, cells)
    load_frame(first, up[0], down[0], gain, bufs, False)
    for s, n in chunks(rows, cells):
        acc_last[s : s + n] += taps(even, odd, k1, s, n, cells)
        acc_first[s : s + n] = taps(even, odd, k2, s, n, cells)


def finish(total, bias, residual, out, s, n, cells):
    value = (total + bias[...].astype(F32)).reshape(n // cells, cells, -1)
    r = slice(s // cells, (s + n) // cells)
    if residual is not None:
        value = residual[0, r].astype(F32) + value
    out[0, r] = value.astype(BF16)


def before_kernel(residual, *refs):
    frame, up, down, gain, k0, k1, bias, acc_first, acc_last = refs[:9]
    refs = refs[9:]
    res = None
    if residual:
        res, refs = refs[0], refs[1:]
    out, acc_out = refs[:2]
    refs = refs[2:]
    edges = None
    if not residual:
        edges, refs = refs[0], refs[1:]
    bufs = refs
    frame = frame.at[0]
    rows, cells = frame.shape[0], frame.shape[1]
    even, odd = bufs[1:]
    load_frame(frame, up[0], down[0], gain, bufs, True)
    for s, n in chunks(rows, cells):
        total = acc_last[s : s + n] + taps(even, odd, k0, s, n, cells)
        finish(total, bias, res, out, s, n, cells)
    if edges is not None:
        edges[0, 0] = out[0, 0]
        edges[1, 0] = out[0, rows - 1]
    for s, n in chunks(rows, cells):
        acc_out[s : s + n] = acc_first[s : s + n] + taps(even, odd, k1, s, n, cells)


def earliest_kernel(residual, *refs):
    frame, up, down, gain, k0, bias, acc_first = refs[:7]
    refs = refs[7:]
    res = None
    if residual:
        res, refs = refs[0], refs[2:]
    out, refs = refs[0], refs[1:]
    edges = None
    if not residual:
        edges, refs = refs[0], refs[1:]
    bufs = refs
    frame = frame.at[0]
    rows, cells = frame.shape[0], frame.shape[1]
    even, odd = bufs[1:]
    load_frame(frame, up[0], down[0], gain, bufs, True)
    for s, n in chunks(rows, cells):
        total = acc_first[s : s + n] + taps(even, odd, k0, s, n, cells)
        finish(total, bias, res, out, s, n, cells)
    if edges is not None:
        edges[0, 0] = out[0, 0]
        edges[1, 0] = out[0, rows - 1]


def whole(shape):
    return pl.BlockSpec(tuple(shape), lambda i: (0,) * len(shape))


def part(shape, index):
    return pl.BlockSpec((1, *shape[1:]), lambda i: (index,) + (0,) * (len(shape) - 1))


def call(body, name, units, out_specs, out_shape, args, aliases=None):
    rows, cells, channels = call.block
    flat = (rows + 2) * cells
    arrays = [a for a, _ in args]
    flops = units * 2 * rows * cells * 9 * channels * channels
    return pl.pallas_call(
        body,
        grid=(1,),
        in_specs=[s for _, s in args],
        out_specs=out_specs,
        out_shape=out_shape,
        scratch_shapes=[
            pltpu.VMEM((3, flat, channels), F32),
            pltpu.VMEM((flat, 3 * channels), BF16),
            pltpu.VMEM((flat - 2 * cells, 3 * channels), BF16),
        ],
        input_output_aliases=aliases or {},
        compiler_params=pltpu.CompilerParams(vmem_limit_bytes=VMEM_LIMIT),
        cost_estimate=pl.CostEstimate(
            flops=flops, bytes_accessed=units * 2**21, transcendentals=2 * flat * channels
        ),
        name=name,
    )(*arrays)


def exchange_rows(top, bottom):
    up = lax.ppermute(bottom, "height", ring("height", 1))
    down = lax.ppermute(top, "height", ring("height", -1))
    return up, down


def w(array):
    return array, whole(array.shape)


def section(last, first, edges, gain, kernel, bias, residual):
    rows, cells, channels = call.block
    frame = (1, rows, cells, channels)
    last_frame, first_frame = (a if a.shape[0] == 1 else a[i : i + 1] for (a, _), i in ((last, 1), (first, 0)))
    before = lax.ppermute(last_frame, "tm", ring("tm", 1))
    earliest = lax.ppermute(first_frame, "tm", ring("tm", 1))
    up, down = exchange_rows(*edges)
    acc = jax.ShapeDtypeStruct((rows * cells, channels), F32)
    acc_spec = whole(acc.shape)
    y = jax.ShapeDtypeStruct(frame, BF16)
    edge = jax.ShapeDtypeStruct((2, 1, cells, channels), BF16)
    k = [(kernel, part(kernel.shape, i)) for i in range(3)]
    acc_first, acc_last = call(
        own_kernel, "own", 3, [acc_spec] * 2, [acc] * 2, [last, first, w(up), w(down), w(gain), k[1], k[2]]
    )
    up, down = exchange_rows(before[:, 0], before[:, rows - 1])
    args = [w(before), w(up), w(down), w(gain), k[0], k[1], w(bias), w(acc_first), w(acc_last)]
    body = functools.partial(before_kernel, residual is not None)
    if residual is None:
        y_last, acc_first, edge_last = call(
            body, "before", 2, [whole(frame), acc_spec, whole(edge.shape)], [y, acc, edge], args
        )
    else:
        out = jax.ShapeDtypeStruct(residual.shape, BF16)
        args.append((residual, part(residual.shape, 1)))
        half, acc_first = call(body, "before", 2, [part(out.shape, 1), acc_spec], [out, acc], args)
    up, down = exchange_rows(earliest[:, 0], earliest[:, rows - 1])
    args = [w(earliest), w(up), w(down), w(gain), k[0], w(bias), w(acc_first)]
    body = functools.partial(earliest_kernel, residual is not None)
    if residual is None:
        y_first, edge_first = call(body, "earliest", 1, [whole(frame), whole(edge.shape)], [y, edge], args)
        return y_last, y_first, edge_last, edge_first
    args += [(residual, part(residual.shape, 0)), (half, pl.BlockSpec(memory_space=pl.ANY))]
    return call(body, "earliest", 1, part(out.shape, 0), out, args, {len(args) - 1: 0})


def per_device(
    latents, first_gain, first_kernel, first_bias, second_gain, second_kernel, second_bias
):
    frames, rows, cells, channels = latents.shape
    call.block = (rows, cells, channels)

    def columns(kernel):
        return kernel.reshape(3, 3, 3 * channels, channels)

    edges = latents[:, 0], latents[:, rows - 1]
    lat = [(latents, part(latents.shape, i)) for i in range(2)]
    y_last, y_first, edge_last, edge_first = section(
        lat[1], lat[0], edges, first_gain[None], columns(first_kernel), first_bias[None], None
    )
    edges = [jnp.concatenate([edge_first[i], edge_last[i]]) for i in range(2)]
    return section(
        w(y_last), w(y_first), edges, second_gain[None], columns(second_kernel), second_bias[None], latents
    )


def solution(mesh):
    return jax.shard_map(
        per_device,
        mesh=mesh,
        in_specs=(P("tm", "height", None, None), P(), P(), P(), P(), P(), P()),
        out_specs=P("tm", "height", None, None),
        check_vma=False,
    )
```

time: 114 us -> 63.4 us (0.56)
  the two profiles are of different devices: /device:TPU:17 before, /device:TPU:0 now
where the time goes in v1:
time: 63.4 us; the launch traced here: 62.9 us
  waiting for transfers between devices  24.9 us (39%)
  Pallas kernels  16.5 us (26%)
  starting transfers between devices  14.5 us (23%)
  local copies, waits for them, and re-layouts  6.71 us (11%)
    pallas_call x6, Pallas kernels, call(): pl.pallas_call(body, grid=(1,), in_specs=[s for _, s in args], out_specs=...  16.5 us
    ppermute x2, waiting for transfers between devices, section(): earliest = lax.ppermute(first_frame, 'tm', ring('tm', 1))  12.8 us
    ppermute x6, starting transfers between devices, exchange_rows(): down = lax.ppermute(top, 'height', ring('height', -1))  7.93 us
    ppermute x2, waiting for transfers between devices, section(): before = lax.ppermute(last_frame, 'tm', ring('tm', 1))  7.84 us
    ppermute x6, waiting for transfers between devices, exchange_rows(): up = lax.ppermute(bottom, 'height', ring('height', 1))  3.31 us
    unnamed x14, local copies, waits for them, and re-layouts  3.18 us
    ppermute x2, starting transfers between devices, section(): before = lax.ppermute(last_frame, 'tm', ring('tm', 1))  2.99 us
    ppermute x2, starting transfers between devices, section(): earliest = lax.ppermute(first_frame, 'tm', ring('tm', 1))  2.75 us
  transfers between devices with their start and end apart: 16, of which 7 were waited for; matrix products, arithmetic and copies ran while one was open for 4% of the time, Pallas kernels for 20%

profile of v1, /device:TPU:0, one launch (start us, length us, event | category | flops | bytes accessed | tf_op | source)
XLA Modules:
  0.0 62.9 jit_solution(6982981248972077310)
XLA Ops:
  0.0 1.2 %fusion = (bf16[1,8,104,256]{3,2,1,0:T(8,128)(2,1)S(1)}, bf16[1,8,104,256]{3,2,1,0:T(8,128)(2,1)S(1)}) fusion(bf16[2,8,104,256]{3,2,1,0:T(8,128)(2,1)} %refs_7_.1), kind=kLoop, calls=%fused_computation.16 | loop fusion | bytes 1703936 | tf_op jit(solution)/shard_map/slice | solution.py:205
  1.2 3.0 %collective-permute-start.3 = (bf16[1,8,104,256]{3,2,1,0:T(8,128)(2,1)S(1)}, bf16[1,8,104,256]{3,2,1,0:T(8,128)(2,1)S(1)}, u32[]{:S(2)}, u32[]{:S(2)}) collective-permute-start(bf16[1,8,104,256]{3,2,1,0:T(8,128)(2,1)S(1)} %get-tuple-element.29), channel_id=1, source_target_pairs={{0,4},{4,8},{8,12},{12,16},{16,20},{20,24},{24,28},{28,0},{1,5},{5... | collective-permute-start | bytes 1277960 | tf_op jit(solution)/shard_map/ppermute | solution.py:206
  4.2 1.0 %slice_bitcast_fusion = (bf16[2,104,256]{2,1,0:T(8,128)(2,1)S(1)}, bf16[2,104,256]{2,1,0:T(8,128)(2,1)S(1)}) fusion(bf16[2,8,104,256]{3,2,1,0:T(8,128)(2,1)} %refs_7_.1), kind=kLoop, calls=%fused_computation.2 | loop fusion | bytes 425984 | tf_op jit(solution)/shard_map/squeeze | solution.py:247
  5.2 0.1 collective-permute-start.6
  5.2 1.7 %collective-permute-start.7 = (bf16[2,104,256]{2,1,0:T(8,128)(2,1)S(1)}, bf16[2,104,256]{2,1,0:T(8,128)(2,1)S(1)}, u32[]{:S(2)}, u32[]{:S(2)}) collective-permute-start(bf16[2,104,256]{2,1,0:T(8,128)(2,1)S(1)} %get-tuple-element.27), channel_id=1, source_target_pairs={{0,3},{1,0},{2,1},{3,2},{4,7},{5,4},{6,5},{7,6},{8,11},{9,8},{10,9... | collective-permute-start | bytes 319496 | tf_op jit(solution)/shard_map/ppermute | solution.py:194
  7.0 1.5 %collective-permute-start = (bf16[1,8,104,256]{3,2,1,0:T(8,128)(2,1)S(1)}, bf16[1,8,104,256]{3,2,1,0:T(8,128)(2,1)S(1)}, u32[]{:S(2)}, u32[]{:S(2)}) collective-permute-start(bf16[1,8,104,256]{3,2,1,0:T(8,128)(2,1)S(1)} %get-tuple-element.30), channel_id=1, source_target_pairs={{0,4},{4,8},{8,12},{12,16},{16,20},{20,24},{24,28},{28,0},{1,5},{5... | collective-permute-start | bytes 1277960 | tf_op jit(solution)/shard_map/ppermute | solution.py:207
  8.5 0.7 %broadcast_in_dim.12.gain.refs_3_ = bf16[1,256]{1,0:T(2,128)(2,1)S(1)} reshape(bf16[256]{0:T(256)(128)(2,1)} %param.8) | data formatting | bytes 1024 | tf_op jit(solution)/shard_map/broadcast_in_dim | solution.py:250
  9.2 0.7 %broadcast_in_dim.13.refs_6_.refs_5_ = bf16[1,256]{1,0:T(2,128)(2,1)S(1)} reshape(bf16[256]{0:T(256)(128)(2,1)} %param.10) | data formatting | bytes 1024 | tf_op jit(solution)/shard_map/broadcast_in_dim | solution.py:250
  9.8 0.0 collective-permute-done.6.up
  9.8 0.0 collective-permute-done.7.down
  9.8 0.0 copy-start
  9.8 2.0 %copy-done = bf16[3,3,3,256,256]{4,3,2,1,0:T(8,128)(2,1)S(1)} copy-done((bf16[3,3,3,256,256]{4,3,2,1,0:T(8,128)(2,1)S(1)}, bf16[3,3,3,256,256]{4,3,2,1,0:T(8,128)(2,1)}, u32[]{:S(2)}) %copy-start) | copy-done | bytes 3538968
  11.8 0.0 copy-start.3
  11.8 1.2 %copy-done.3 = bf16[2,8,104,256]{3,2,1,0:T(8,128)(2,1)S(1)} copy-done((bf16[2,8,104,256]{3,2,1,0:T(8,128)(2,1)S(1)}, bf16[2,8,104,256]{3,2,1,0:T(8,128)(2,1)}, u32[]{:S(2)}) %copy-start.3) | copy-done | bytes 851992
  13.0 0.0 copy-start.1
  13.0 3.5 %own.2 = (f32[832,256]{1,0:T(8,128)S(1)}, f32[832,256]{1,0:T(8,128)S(1)}) custom-call(bf16[2,8,104,256]{3,2,1,0:T(8,128)(2,1)S(1)} %copy-done.3, bf16[2,8,104,256]{3,2,1,0:T(8,128)(2,1)S(1)} %copy-done.3, bf16[2,104,256]{2,1,0:T(8,128)(2,1)S(1)} %collective-permute-done.6.up, bf16[2,104,256]{2,1,0:T(8,128)(2,1)S(1)} %collective-permute-done.7.down, ...), custom_call_target="tpu_custom_call" | custom-call | flops 2944401408 | bytes 6291456 | tf_op jit(solution)/shard_map/own/pallas_call | solution.py:172
  16.5 1.4 %collective-permute-done.3.refs_0_ = bf16[1,8,104,256]{3,2,1,0:T(8,128)(2,1)S(1)} collective-permute-done((bf16[1,8,104,256]{3,2,1,0:T(8,128)(2,1)S(1)}, bf16[1,8,104,256]{3,2,1,0:T(8,128)(2,1)S(1)}, u32[]{:S(2)}, u32[]{:S(2)}) %collective-permute-start.3) | collective-permute-done | bytes 426016 | tf_op jit(solution)/shard_map/ppermute | solution.py:206
  17.9 0.1 collective-permute-start.4
  18.0 1.7 %collective-permute-start.5 = (bf16[1,104,256]{2,1,0:T(8,128)(2,1)S(1)}, bf16[1,104,256]{2,1,0:T(8,128)(2,1)S(1)}, u32[]{:S(2)}, u32[]{:S(2)}) collective-permute-start(bf16[1,104,256]{2,1,0:T(8,128)(2,1)S(1)} %get-tuple-element.35), channel_id=1, source_target_pairs={{0,3},{1,0},{2,1},{3,2},{4,7},{5,4},{6,5},{7,6},{8,11},{9,8},{10,9... | collective-permute-start | bytes 159752 | tf_op jit(solution)/shard_map/ppermute | solution.py:194
  19.7 6.5 %collective-permute-done.refs_0_ = bf16[1,8,104,256]{3,2,1,0:T(8,128)(2,1)S(1)} collective-permute-done((bf16[1,8,104,256]{3,2,1,0:T(8,128)(2,1)S(1)}, bf16[1,8,104,256]{3,2,1,0:T(8,128)(2,1)S(1)}, u32[]{:S(2)}, u32[]{:S(2)}) %collective-permute-start) | collective-permute-done | bytes 426016 | tf_op jit(solution)/shard_map/ppermute | solution.py:207
  26.2 0.1 collective-permute-start.1
  26.2 1.7 %collective-permute-start.2 = (bf16[1,104,256]{2,1,0:T(8,128)(2,1)S(1)}, bf16[1,104,256]{2,1,0:T(8,128)(2,1)S(1)}, u32[]{:S(2)}, u32[]{:S(2)}) collective-permute-start(bf16[1,104,256]{2,1,0:T(8,128)(2,1)S(1)} %get-tuple-element.37), channel_id=1, source_target_pairs={{0,3},{1,0},{2,1},{3,2},{4,7},{5,4},{6,5},{7,6},{8,11},{9,8},{10,9... | collective-permute-start | bytes 159752 | tf_op jit(solution)/shard_map/ppermute | solution.py:194
  28.0 0.0 collective-permute-done.4.refs_1_
  28.0 0.0 collective-permute-done.5.refs_2_
  28.0 0.0 copy-done.1
  28.0 2.6 %before.2 = (bf16[1,8,104,256]{3,2,1,0:T(8,128)(2,1)S(1)}, f32[832,256]{1,0:T(8,128)S(1)}, bf16[2,1,104,256]{3,2,1,0:T(8,128)(2,1)S(1)}) custom-call(bf16[1,8,104,256]{3,2,1,0:T(8,128)(2,1)S(1)} %collective-permute-done.3.refs_0_, bf16[1,104,256]{2,1,0:T(8,128)(2,1)S(1)} %collective-permute-done.4.refs_1_, ...), custom_call_target="tpu_custom_call" | custom-call | flops 1962934272 | bytes 4194304 | tf_op jit(solution)/shard_map/before/pallas_call | solution.py:172
  30.6 0.0 copy-start.5
  30.6 0.0 copy-start.6
  30.6 0.0 copy-start.2
  30.6 0.0 collective-permute-done.1.refs_1_
  30.6 0.0 collective-permute-done.2.refs_2_
  30.6 1.5 %earliest.2 = (bf16[1,8,104,256]{3,2,1,0:T(8,128)(2,1)S(1)}, bf16[2,1,104,256]{3,2,1,0:T(8,128)(2,1)S(1)}) custom-call(bf16[1,8,104,256]{3,2,1,0:T(8,128)(2,1)S(1)} %collective-permute-done.refs_0_, bf16[1,104,256]{2,1,0:T(8,128)(2,1)S(1)} %collective-permute-done.1.refs_1_, bf16[1,104,256]{2,1,0:T(8,128)(2,1)S(1)} %collective-permute-done.2.refs_2_, ...), custom_call_target="tpu_custom_call" | custom-call | flops 981467136 | bytes 2097152 | tf_op jit(solution)/shard_map/earliest/pallas_call | solution.py:172
  32.2 1.0 %collective-permute-start.15 = (bf16[2,104,256]{2,1,0:T(8,128)(2,1)S(1)}, bf16[2,104,256]{2,1,0:T(8,128)(2,1)S(1)}, u32[]{:S(2)}, u32[]{:S(2)}) collective-permute-start(bf16[2,104,256]{2,1,0:T(8,128)(2,1)S(1)} %pad_maximum_fusion.1), channel_id=1, source_target_pairs={{0,3},{1,0},{2,1},{3,2},{4,7},{5,4},{6,5},{7,6},{8,11},{9,8},{10,9... | collective-permute-start | bytes 319496 | tf_op jit(solution)/shard_map/ppermute | solution.py:194
  33.2 0.0 collective-permute-start.11
  33.2 0.1 collective-permute-start.14
  33.3 0.0 copy-done.5
  33.3 0.0 copy-done.6
  33.3 1.2 %collective-permute-start.8 = (bf16[1,8,104,256]{3,2,1,0:T(8,128)(2,1)S(1)}, bf16[1,8,104,256]{3,2,1,0:T(8,128)(2,1)S(1)}, u32[]{:S(2)}, u32[]{:S(2)}) collective-permute-start(bf16[1,8,104,256]{3,2,1,0:T(8,128)(2,1)S(1)} %get-tuple-element.19.first_ref), channel_id=1, source_target_pairs={{0,4},{4,8},{8,12},{12,16},{16,20},{20,24},{24,28},{28,0},{1,5},{5... | collective-permute-start | bytes 1277960 | tf_op jit(solution)/shard_map/ppermute | solution.py:207
  34.5 1.0 %collective-permute-done.15.down = bf16[2,104,256]{2,1,0:T(8,128)(2,1)S(1)} collective-permute-done((bf16[2,104,256]{2,1,0:T(8,128)(2,1)S(1)}, bf16[2,104,256]{2,1,0:T(8,128)(2,1)S(1)}, u32[]{:S(2)}, u32[]{:S(2)}) %collective-permute-start.15) | collective-permute-done | bytes 106528 | tf_op jit(solution)/shard_map/ppermute | solution.py:194
  35.5 3.0 %collective-permute-done.14.up = bf16[2,104,256]{2,1,0:T(8,128)(2,1)S(1)} collective-permute-done((bf16[2,104,256]{2,1,0:T(8,128)(2,1)S(1)}, bf16[2,104,256]{2,1,0:T(8,128)(2,1)S(1)}, u32[]{:S(2)}, u32[]{:S(2)}) %collective-permute-start.14) | collective-permute-done | bytes 106528 | tf_op jit(solution)/shard_map/ppermute | solution.py:193
  38.5 0.0 copy-done.2
  38.5 0.0 copy-start.4
  38.5 3.6 %own.3 = (f32[832,256]{1,0:T(8,128)S(1)}, f32[832,256]{1,0:T(8,128)S(1)}) custom-call(bf16[1,8,104,256]{3,2,1,0:T(8,128)(2,1)S(1)} %get-tuple-element.20.last_ref, bf16[1,8,104,256]{3,2,1,0:T(8,128)(2,1)S(1)} %get-tuple-element.19.first_ref, bf16[2,104,256]{2,1,0:T(8,128)(2,1)S(1)} %collective-permute-done.14.up, ...), custom_call_target="tpu_custom_call" | custom-call | flops 2944401408 | bytes 6291456 | tf_op jit(solution)/shard_map/own/pallas_call | solution.py:172
  42.1 6.5 %collective-permute-done.11.refs_0_ = bf16[1,8,104,256]{3,2,1,0:T(8,128)(2,1)S(1)} collective-permute-done((bf16[1,8,104,256]{3,2,1,0:T(8,128)(2,1)S(1)}, bf16[1,8,104,256]{3,2,1,0:T(8,128)(2,1)S(1)}, u32[]{:S(2)}, u32[]{:S(2)}) %collective-permute-start.11) | collective-permute-done | bytes 426016 | tf_op jit(solution)/shard_map/ppermute | solution.py:206
  48.6 0.1 collective-permute-start.12
  48.6 1.7 %collective-permute-start.13 = (bf16[1,104,256]{2,1,0:T(8,128)(2,1)S(1)}, bf16[1,104,256]{2,1,0:T(8,128)(2,1)S(1)}, u32[]{:S(2)}, u32[]{:S(2)}) collective-permute-start(bf16[1,104,256]{2,1,0:T(8,128)(2,1)S(1)} %get-tuple-element.31), channel_id=1, source_target_pairs={{0,3},{1,0},{2,1},{3,2},{4,7},{5,4},{6,5},{7,6},{8,11},{9,8},{10,9... | collective-permute-start | bytes 159752 | tf_op jit(solution)/shard_map/ppermute | solution.py:194
  50.4 6.3 %collective-permute-done.8.refs_0_ = bf16[1,8,104,256]{3,2,1,0:T(8,128)(2,1)S(1)} collective-permute-done((bf16[1,8,104,256]{3,2,1,0:T(8,128)(2,1)S(1)}, bf16[1,8,104,256]{3,2,1,0:T(8,128)(2,1)S(1)}, u32[]{:S(2)}, u32[]{:S(2)}) %collective-permute-start.8) | collective-permute-done | bytes 426016 | tf_op jit(solution)/shard_map/ppermute | solution.py:207
  56.7 0.1 collective-permute-start.10
  56.8 0.5 collective-permute-start.9
  57.3 0.0 collective-permute-done.12.refs_1_
  57.3 0.0 collective-permute-done.13.refs_2_
  57.3 0.0 copy-done.4
  57.3 3.0 %before.3 = (bf16[2,8,104,256]{3,2,1,0:T(8,128)(2,1)}, f32[832,256]{1,0:T(8,128)S(1)}) custom-call(bf16[1,8,104,256]{3,2,1,0:T(8,128)(2,1)S(1)} %collective-permute-done.11.refs_0_, bf16[1,104,256]{2,1,0:T(8,128)(2,1)S(1)} %collective-permute-done.12.refs_1_, bf16[1,104,256]{2,1,0:T(8,128)(2,1)S(1)} %collective-permute-done.13.refs_2_, ...), custom_call_target="tpu_custom_call" | custom-call | flops 1962934272 | bytes 4194304 | tf_op jit(solution)/shard_map/before/pallas_call | solution.py:172
  60.3 0.0 collective-permute-done.10.refs_2_
  60.3 0.3 collective-permute-done.9.refs_1_
  60.6 2.3 %earliest.3 = bf16[2,8,104,256]{3,2,1,0:T(8,128)(2,1)} custom-call(bf16[1,8,104,256]{3,2,1,0:T(8,128)(2,1)S(1)} %collective-permute-done.8.refs_0_, bf16[1,104,256]{2,1,0:T(8,128)(2,1)S(1)} %collective-permute-done.9.refs_1_, bf16[1,104,256]{2,1,0:T(8,128)(2,1)S(1)} %collective-permute-done.10.refs_2_, ...), custom_call_target="tpu_custom_call", output_to_operand_aliasing={{}: (8, {})} | custom-call | flops 981467136 | bytes 2097152 | tf_op jit(solution)/shard_map/earliest/pallas_call | solution.py:172
  (10 shorter events, 0.1 us)
Async XLA Ops:
  1.2 16.7 %collective-permute-start.3 = (bf16[1,8,104,256]{3,2,1,0:T(8,128)(2,1)S(1)}, bf16[1,8,104,256]{3,2,1,0:T(8,128)(2,1)S(1)}, u32[]{:S(2)}, u32[]{:S(2)}) collective-permute-start(bf16[1,8,104,256]{3,2,1,0:T(8,128)(2,1)S(1)} %get-tuple-element.29), channel_id=1, source_target_pairs={{0,4},{4,8},{8,12},{12,16},{16,20},{20,24},{24,28},{28,0},{1,5},{5... | collective-permute-start | bytes 1277960 | tf_op jit(solution)/shard_map/ppermute | solution.py:206
  5.2 4.7 %collective-permute-start.6 = (bf16[2,104,256]{2,1,0:T(8,128)(2,1)S(1)}, bf16[2,104,256]{2,1,0:T(8,128)(2,1)S(1)}, u32[]{:S(2)}, u32[]{:S(2)}) collective-permute-start(bf16[2,104,256]{2,1,0:T(8,128)(2,1)S(1)} %get-tuple-element.28), channel_id=1, source_target_pairs={{0,1},{1,2},{2,3},{3,0},{4,5},{5,6},{6,7},{7,4},{8,9},{9,10},{10,1... | collective-permute-start | bytes 319496 | tf_op jit(solution)/shard_map/ppermute | solution.py:193
  5.2 4.6 %collective-permute-start.7 = (bf16[2,104,256]{2,1,0:T(8,128)(2,1)S(1)}, bf16[2,104,256]{2,1,0:T(8,128)(2,1)S(1)}, u32[]{:S(2)}, u32[]{:S(2)}) collective-permute-start(bf16[2,104,256]{2,1,0:T(8,128)(2,1)S(1)} %get-tuple-element.27), channel_id=1, source_target_pairs={{0,3},{1,0},{2,1},{3,2},{4,7},{5,4},{6,5},{7,6},{8,11},{9,8},{10,9... | collective-permute-start | bytes 319496 | tf_op jit(solution)/shard_map/ppermute | solution.py:194
  7.0 19.2 %collective-permute-start = (bf16[1,8,104,256]{3,2,1,0:T(8,128)(2,1)S(1)}, bf16[1,8,104,256]{3,2,1,0:T(8,128)(2,1)S(1)}, u32[]{:S(2)}, u32[]{:S(2)}) collective-permute-start(bf16[1,8,104,256]{3,2,1,0:T(8,128)(2,1)S(1)} %get-tuple-element.30), channel_id=1, source_target_pairs={{0,4},{4,8},{8,12},{12,16},{16,20},{20,24},{24,28},{28,0},{1,5},{5... | collective-permute-start | bytes 1277960 | tf_op jit(solution)/shard_map/ppermute | solution.py:207
  9.8 2.0 %copy-start = (bf16[3,3,3,256,256]{4,3,2,1,0:T(8,128)(2,1)S(1)}, bf16[3,3,3,256,256]{4,3,2,1,0:T(8,128)(2,1)}, u32[]{:S(2)}) copy-start(bf16[3,3,3,256,256]{4,3,2,1,0:T(8,128)(2,1)} %param.9) | copy-start | bytes 10616836
  11.8 1.2 %copy-start.3 = (bf16[2,8,104,256]{3,2,1,0:T(8,128)(2,1)S(1)}, bf16[2,8,104,256]{3,2,1,0:T(8,128)(2,1)}, u32[]{:S(2)}) copy-start(bf16[2,8,104,256]{3,2,1,0:T(8,128)(2,1)} %refs_7_.1) | copy-start | bytes 2555908
  13.0 15.0 %copy-start.1 = (bf16[3,3,3,256,256]{4,3,2,1,0:T(8,128)(2,1)S(1)}, bf16[3,3,3,256,256]{4,3,2,1,0:T(8,128)(2,1)}, u32[]{:S(2)}) copy-start(bf16[3,3,3,256,256]{4,3,2,1,0:T(8,128)(2,1)} %param.9) | copy-start | bytes 10616836
  17.9 10.1 %collective-permute-start.4 = (bf16[1,104,256]{2,1,0:T(8,128)(2,1)S(1)}, bf16[1,104,256]{2,1,0:T(8,128)(2,1)S(1)}, u32[]{:S(2)}, u32[]{:S(2)}) collective-permute-start(bf16[1,104,256]{2,1,0:T(8,128)(2,1)S(1)} %get-tuple-element.36), channel_id=1, source_target_pairs={{0,1},{1,2},{2,3},{3,0},{4,5},{5,6},{6,7},{7,4},{8,9},{9,10},{10,1... | collective-permute-start | bytes 159752 | tf_op jit(solution)/shard_map/ppermute | solution.py:193
  18.0 10.0 %collective-permute-start.5 = (bf16[1,104,256]{2,1,0:T(8,128)(2,1)S(1)}, bf16[1,104,256]{2,1,0:T(8,128)(2,1)S(1)}, u32[]{:S(2)}, u32[]{:S(2)}) collective-permute-start(bf16[1,104,256]{2,1,0:T(8,128)(2,1)S(1)} %get-tuple-element.35), channel_id=1, source_target_pairs={{0,3},{1,0},{2,1},{3,2},{4,7},{5,4},{6,5},{7,6},{8,11},{9,8},{10,9... | collective-permute-start | bytes 159752 | tf_op jit(solution)/shard_map/ppermute | solution.py:194
  26.2 4.4 %collective-permute-start.1 = (bf16[1,104,256]{2,1,0:T(8,128)(2,1)S(1)}, bf16[1,104,256]{2,1,0:T(8,128)(2,1)S(1)}, u32[]{:S(2)}, u32[]{:S(2)}) collective-permute-start(bf16[1,104,256]{2,1,0:T(8,128)(2,1)S(1)} %get-tuple-element.38), channel_id=1, source_target_pairs={{0,1},{1,2},{2,3},{3,0},{4,5},{5,6},{6,7},{7,4},{8,9},{9,10},{10,1... | collective-permute-start | bytes 159752 | tf_op jit(solution)/shard_map/ppermute | solution.py:193
  26.2 4.4 %collective-permute-start.2 = (bf16[1,104,256]{2,1,0:T(8,128)(2,1)S(1)}, bf16[1,104,256]{2,1,0:T(8,128)(2,1)S(1)}, u32[]{:S(2)}, u32[]{:S(2)}) collective-permute-start(bf16[1,104,256]{2,1,0:T(8,128)(2,1)S(1)} %get-tuple-element.37), channel_id=1, source_target_pairs={{0,3},{1,0},{2,1},{3,2},{4,7},{5,4},{6,5},{7,6},{8,11},{9,8},{10,9... | collective-permute-start | bytes 159752 | tf_op jit(solution)/shard_map/ppermute | solution.py:194
  30.6 2.7 %copy-start.5 = (bf16[256]{0:T(256)(128)(2,1)S(1)}, bf16[256]{0:T(256)(128)(2,1)}, u32[]{:S(2)}) copy-start(bf16[256]{0:T(256)(128)(2,1)} %param.11) | copy-start | bytes 1540
  30.6 2.7 %copy-start.6 = (bf16[256]{0:T(256)(128)(2,1)S(1)}, bf16[256]{0:T(256)(128)(2,1)}, u32[]{:S(2)}) copy-start(bf16[256]{0:T(256)(128)(2,1)} %param.13) | copy-start | bytes 1540
  30.6 7.9 %copy-start.2 = (bf16[3,3,3,256,256]{4,3,2,1,0:T(8,128)(2,1)S(1)}, bf16[3,3,3,256,256]{4,3,2,1,0:T(8,128)(2,1)}, u32[]{:S(2)}) copy-start(bf16[3,3,3,256,256]{4,3,2,1,0:T(8,128)(2,1)} %param.12) | copy-start | bytes 10616836
  32.2 3.3 %collective-permute-start.15 = (bf16[2,104,256]{2,1,0:T(8,128)(2,1)S(1)}, bf16[2,104,256]{2,1,0:T(8,128)(2,1)S(1)}, u32[]{:S(2)}, u32[]{:S(2)}) collective-permute-start(bf16[2,104,256]{2,1,0:T(8,128)(2,1)S(1)} %pad_maximum_fusion.1), channel_id=1, source_target_pairs={{0,3},{1,0},{2,1},{3,2},{4,7},{5,4},{6,5},{7,6},{8,11},{9,8},{10,9... | collective-permute-start | bytes 319496 | tf_op jit(solution)/shard_map/ppermute | solution.py:194
  33.2 15.4 %collective-permute-start.11 = (bf16[1,8,104,256]{3,2,1,0:T(8,128)(2,1)S(1)}, bf16[1,8,104,256]{3,2,1,0:T(8,128)(2,1)S(1)}, u32[]{:S(2)}, u32[]{:S(2)}) collective-permute-start(bf16[1,8,104,256]{3,2,1,0:T(8,128)(2,1)S(1)} %get-tuple-element.20.last_ref), channel_id=1, source_target_pairs={{0,4},{4,8},{8,12},{12,16},{16,20},{20,24},{24,28},{28,0},{1,5},{5... | collective-permute-start | bytes 1277960 | tf_op jit(solution)/shard_map/ppermute | solution.py:206
  33.2 5.3 %collective-permute-start.14 = (bf16[2,104,256]{2,1,0:T(8,128)(2,1)S(1)}, bf16[2,104,256]{2,1,0:T(8,128)(2,1)S(1)}, u32[]{:S(2)}, u32[]{:S(2)}) collective-permute-start(bf16[2,104,256]{2,1,0:T(8,128)(2,1)S(1)} %pad_maximum_fusion), channel_id=1, source_target_pairs={{0,1},{1,2},{2,3},{3,0},{4,5},{5,6},{6,7},{7,4},{8,9},{9,10},{10,1... | collective-permute-start | bytes 319496 | tf_op jit(solution)/shard_map/ppermute | solution.py:193
  33.3 23.4 %collective-permute-start.8 = (bf16[1,8,104,256]{3,2,1,0:T(8,128)(2,1)S(1)}, bf16[1,8,104,256]{3,2,1,0:T(8,128)(2,1)S(1)}, u32[]{:S(2)}, u32[]{:S(2)}) collective-permute-start(bf16[1,8,104,256]{3,2,1,0:T(8,128)(2,1)S(1)} %get-tuple-element.19.first_ref), channel_id=1, source_target_pairs={{0,4},{4,8},{8,12},{12,16},{16,20},{20,24},{24,28},{28,0},{1,5},{5... | collective-permute-start | bytes 1277960 | tf_op jit(solution)/shard_map/ppermute | solution.py:207
  38.5 18.7 %copy-start.4 = (bf16[2,8,104,256]{3,2,1,0:T(8,128)(2,1)S(1)}, bf16[2,8,104,256]{3,2,1,0:T(8,128)(2,1)}, u32[]{:S(2)}) copy-start(bf16[2,8,104,256]{3,2,1,0:T(8,128)(2,1)} %refs_7_.1) | copy-start | bytes 2555908
  48.6 8.7 %collective-permute-start.12 = (bf16[1,104,256]{2,1,0:T(8,128)(2,1)S(1)}, bf16[1,104,256]{2,1,0:T(8,128)(2,1)S(1)}, u32[]{:S(2)}, u32[]{:S(2)}) collective-permute-start(bf16[1,104,256]{2,1,0:T(8,128)(2,1)S(1)} %get-tuple-element.32), channel_id=1, source_target_pairs={{0,1},{1,2},{2,3},{3,0},{4,5},{5,6},{6,7},{7,4},{8,9},{9,10},{10,1... | collective-permute-start | bytes 159752 | tf_op jit(solution)/shard_map/ppermute | solution.py:193
  48.6 8.6 %collective-permute-start.13 = (bf16[1,104,256]{2,1,0:T(8,128)(2,1)S(1)}, bf16[1,104,256]{2,1,0:T(8,128)(2,1)S(1)}, u32[]{:S(2)}, u32[]{:S(2)}) collective-permute-start(bf16[1,104,256]{2,1,0:T(8,128)(2,1)S(1)} %get-tuple-element.31), channel_id=1, source_target_pairs={{0,3},{1,0},{2,1},{3,2},{4,7},{5,4},{6,5},{7,6},{8,11},{9,8},{10,9... | collective-permute-start | bytes 159752 | tf_op jit(solution)/shard_map/ppermute | solution.py:194
  56.7 3.6 %collective-permute-start.10 = (bf16[1,104,256]{2,1,0:T(8,128)(2,1)S(1)}, bf16[1,104,256]{2,1,0:T(8,128)(2,1)S(1)}, u32[]{:S(2)}, u32[]{:S(2)}) collective-permute-start(bf16[1,104,256]{2,1,0:T(8,128)(2,1)S(1)} %get-tuple-element.33), channel_id=1, source_target_pairs={{0,3},{1,0},{2,1},{3,2},{4,7},{5,4},{6,5},{7,6},{8,11},{9,8},{10,9... | collective-permute-start | bytes 159752 | tf_op jit(solution)/shard_map/ppermute | solution.py:194
  56.8 3.8 %collective-permute-start.9 = (bf16[1,104,256]{2,1,0:T(8,128)(2,1)S(1)}, bf16[1,104,256]{2,1,0:T(8,128)(2,1)S(1)}, u32[]{:S(2)}, u32[]{:S(2)}) collective-permute-start(bf16[1,104,256]{2,1,0:T(8,128)(2,1)S(1)} %get-tuple-element.34), channel_id=1, source_target_pairs={{0,1},{1,2},{2,3},{3,0},{4,5},{5,6},{6,7},{7,4},{8,9},{9,10},{10,1... | collective-permute-start | bytes 159752 | tf_op jit(solution)/shard_map/ppermute | solution.py:193

commit v2 on v1

--- a/solution.py
+++ b/solution.py
@@ -10,7 +10,6 @@
 EPSILON = 1e-06
 BF16, F32 = jnp.bfloat16, jnp.float32
 VMEM_LIMIT = 26 * 2**20
-CHUNK = 2
 
 
 def ring(axis, step):
@@ -63,9 +62,11 @@
     return above, below, before
 
 
-def load_frame(frame, up, down, gain, bufs, time_halo):
+def load_frame(frame, up, down, gain, bufs, time_halo, edges=None):
     shifts, even, odd = bufs
     rows, cells = frame.shape[0], frame.shape[1]
+    if edges is not None:
+        rows += 2
     above, below, before = masks()
     if time_halo:
         above, below = above * before, below * before
@@ -75,9 +76,14 @@
             return up, above
         if r == rows + 1:
             return down, below
-        return frame[r - 1], before if time_halo else None
-
-    activate_rows(get_row, gain[...].astype(F32), shifts, rows + 2, cells)
+        own = before if time_halo else None
+        if edges is None:
+            return frame[r - 1], own
+        if r in (1, rows):
+            return edges[0 if r == 1 else 1, 0], own
+        return frame[r - 2], own
+
+    activate_rows(get_row, gain[...].astype(F32)[None], shifts, rows + 2, cells)
     pack(shifts, even, odd, rows + 2, cells)
 
 
@@ -100,7 +106,7 @@
 
 
 def finish(total, bias, residual, out, s, n, cells):
-    value = (total + bias[...].astype(F32)).reshape(n // cells, cells, -1)
+    value = (total + bias[...].astype(F32)[None]).reshape(n // cells, cells, -1)
     r = slice(s // cells, (s + n) // cells)
     if residual is not None:
         value = residual[0, r].astype(F32) + value
@@ -134,26 +140,21 @@
 
 
 def earliest_kernel(residual, *refs):
-    frame, up, down, gain, k0, bias, acc_first = refs[:7]
-    refs = refs[7:]
-    res = None
     if residual:
-        res, refs = refs[0], refs[2:]
-    out, refs = refs[0], refs[1:]
-    edges = None
-    if not residual:
-        edges, refs = refs[0], refs[1:]
-    bufs = refs
-    frame = frame.at[0]
-    rows, cells = frame.shape[0], frame.shape[1]
+        frame, edges, up, down, gain, k0, bias, acc_first, res, _, out, *bufs = refs
+    else:
+        frame, up, down, gain, k0, bias, acc_first, out, inner, edges_out, *bufs = refs
+        edges = res = None
+    rows, cells = out.shape[1], out.shape[2]
     even, odd = bufs[1:]
-    load_frame(frame, up[0], down[0], gain, bufs, True)
+    load_frame(frame.at[0], up[0], down[0], gain, bufs, True, edges)
     for s, n in chunks(rows, cells):
         total = acc_first[s : s + n] + taps(even, odd, k0, s, n, cells)
         finish(total, bias, res, out, s, n, cells)
-    if edges is not None:
-        edges[0, 0] = out[0, 0]
-        edges[1, 0] = out[0, rows - 1]
+    if not residual:
+        edges_out[0, 0] = out[0, 0]
+        edges_out[1, 0] = out[0, rows - 1]
+        inner[0] = out[0, 1 : rows - 1]
 
 
 def whole(shape):
@@ -199,39 +200,101 @@
     return array, whole(array.shape)
 
 
-def section(last, first, edges, gain, kernel, bias, residual):
+def shift(array):
+    return lax.ppermute(array, "tm", ring("tm", 1))
+
+
+def shapes():
     rows, cells, channels = call.block
-    frame = (1, rows, cells, channels)
-    last_frame, first_frame = (a if a.shape[0] == 1 else a[i : i + 1] for (a, _), i in ((last, 1), (first, 0)))
-    before = lax.ppermute(last_frame, "tm", ring("tm", 1))
-    earliest = lax.ppermute(first_frame, "tm", ring("tm", 1))
+    acc = jax.ShapeDtypeStruct((rows * cells, channels), F32)
+    frame = jax.ShapeDtypeStruct((1, rows, cells, channels), BF16)
+    inner = jax.ShapeDtypeStruct((1, rows - 2, cells, channels), BF16)
+    edge = jax.ShapeDtypeStruct((2, 1, cells, channels), BF16)
+    return acc, frame, inner, edge
+
+
+def own(last, first, up, down, gain, k):
+    acc = shapes()[0]
+    args = [last, first, w(up), w(down), gain, k[1], k[2]]
+    return call(own_kernel, "own", 3, [whole(acc.shape)] * 2, [acc, acc], args)
+
+
+def after(token, blocks, name):
+    def copy(*refs):
+        count = (len(refs) - 1) // 2
+        for source, target in zip(refs[:count], refs[count + 1 :]):
+            target[...] = source[...]
+
+    outs = [jax.ShapeDtypeStruct(spec.block_shape, array.dtype) for array, spec in blocks]
+    return pl.pallas_call(
+        copy,
+        grid=(1,),
+        in_specs=[spec for _, spec in blocks] + [pl.BlockSpec(memory_space=pl.ANY)],
+        out_specs=[whole(o.shape) for o in outs],
+        out_shape=outs,
+        compiler_params=pltpu.CompilerParams(vmem_limit_bytes=4 * 2**20),
+        name=name,
+    )(*[array for array, _ in blocks], token)
+
+
+def rows_after(token, array, places):
+    block = (1, 1, *array.shape[2:])
+    blocks = [(array, pl.BlockSpec(block, lambda i, p=p: (*p, 0, 0))) for p in places]
+    return [a[0] for a in after(token, blocks, "edges")]
+
+
+def first_section(latents, gain, kernel, bias):
+    rows = latents.shape[1]
+    acc, frame, inner, edge = shapes()
+    k = [(kernel, part(kernel.shape, i)) for i in range(3)]
+    last, first = ((latents, part(latents.shape, i)) for i in (1, 0))
+    before = shift(latents[1:])
+    edges = latents[:, 0], latents[:, rows - 1]
     up, down = exchange_rows(*edges)
-    acc = jax.ShapeDtypeStruct((rows * cells, channels), F32)
-    acc_spec = whole(acc.shape)
-    y = jax.ShapeDtypeStruct(frame, BF16)
-    edge = jax.ShapeDtypeStruct((2, 1, cells, channels), BF16)
+    earliest = shift(after(up, [first], "first")[0])
+    acc_first, acc_last = own(last, first, up, down, gain, k)
+    up, down = exchange_rows(*rows_after(acc_last, before, [(0, 0), (0, rows - 1)]))
+    args = [w(before), w(up), w(down), gain, k[0], k[1], bias, w(acc_first), w(acc_last)]
+    outs = [frame, acc, edge]
+    y_last, acc_first, edge_last = call(
+        functools.partial(before_kernel, False), "before", 2, [whole(o.shape) for o in outs], outs, args
+    )
+    up, down = exchange_rows(earliest[:, 0], earliest[:, rows - 1])
+    args = [w(earliest), w(up), w(down), gain, k[0], bias, w(acc_first)]
+    outs = [frame, inner, edge]
+    y_first, inner_first, edge_first = call(
+        functools.partial(earliest_kernel, False), "earliest", 1, [whole(o.shape) for o in outs], outs, args
+    )
+    return y_last, y_first, edge_last, inner_first, edge_first
+
+
+def second_section(results, latents, gain, kernel, bias):
+    y_last, y_first, edge_last, inner_first, edge_first = results
+    rows = latents.shape[1]
+    acc = shapes()[0]
     k = [(kernel, part(kernel.shape, i)) for i in range(3)]
-    acc_first, acc_last = call(
-        own_kernel, "own", 3, [acc_spec] * 2, [acc] * 2, [last, first, w(up), w(down), w(gain), k[1], k[2]]
-    )
-    up, down = exchange_rows(before[:, 0], before[:, rows - 1])
-    args = [w(before), w(up), w(down), w(gain), k[0], k[1], w(bias), w(acc_first), w(acc_last)]
-    body = functools.partial(before_kernel, residual is not None)
-    if residual is None:
-        y_last, acc_first, edge_last = call(
-            body, "before", 2, [whole(frame), acc_spec, whole(edge.shape)], [y, acc, edge], args
-        )
-    else:
-        out = jax.ShapeDtypeStruct(residual.shape, BF16)
-        args.append((residual, part(residual.shape, 1)))
-        half, acc_first = call(body, "before", 2, [part(out.shape, 1), acc_spec], [out, acc], args)
-    up, down = exchange_rows(earliest[:, 0], earliest[:, rows - 1])
-    args = [w(earliest), w(up), w(down), w(gain), k[0], w(bias), w(acc_first)]
-    body = functools.partial(earliest_kernel, residual is not None)
-    if residual is None:
-        y_first, edge_first = call(body, "earliest", 1, [whole(frame), whole(edge.shape)], [y, edge], args)
-        return y_last, y_first, edge_last, edge_first
-    args += [(residual, part(residual.shape, 0)), (half, pl.BlockSpec(memory_space=pl.ANY))]
+    before = shift(y_last)
+    earliest_edges = shift(edge_first)
+    earliest = shift(inner_first)
+    edges = [jnp.concatenate([edge_first[i], edge_last[i]]) for i in range(2)]
+    up, down = exchange_rows(*edges)
+    acc_first, acc_last = own(w(y_last), w(y_first), up, down, gain, k)
+    up, down = exchange_rows(*rows_after(acc_last, before, [(0, 0), (0, rows - 1)]))
+    args = [w(before), w(up), w(down), gain, k[0], k[1], bias, w(acc_first), w(acc_last)]
+    args.append((latents, part(latents.shape, 1)))
+    out = jax.ShapeDtypeStruct(latents.shape, BF16)
+    half, acc_first = call(
+        functools.partial(before_kernel, True),
+        "before",
+        2,
+        [part(out.shape, 1), whole(acc.shape)],
+        [out, acc],
+        args,
+    )
+    up, down = exchange_rows(*rows_after(acc_last, earliest_edges, [(0, 0), (1, 0)]))
+    args = [w(earliest), w(earliest_edges), w(up), w(down), gain, k[0], bias, w(acc_first)]
+    args += [(latents, part(latents.shape, 0)), (half, pl.BlockSpec(memory_space=pl.ANY))]
+    body = functools.partial(earliest_kernel, True)
     return call(body, "earliest", 1, part(out.shape, 0), out, args, {len(args) - 1: 0})
 
 
@@ -244,15 +307,9 @@
     def columns(kernel):
         return kernel.reshape(3, 3, 3 * channels, channels)
 
-    edges = latents[:, 0], latents[:, rows - 1]
-    lat = [(latents, part(latents.shape, i)) for i in range(2)]
-    y_last, y_first, edge_last, edge_first = section(
-        lat[1], lat[0], edges, first_gain[None], columns(first_kernel), first_bias[None], None
-    )
-    edges = [jnp.concatenate([edge_first[i], edge_last[i]]) for i in range(2)]
-    return section(
-        w(y_last), w(y_first), edges, second_gain[None], columns(second_kernel), second_bias[None], latents
-    )
+    first_gain, first_bias, second_gain, second_bias = map(w, (first_gain, first_bias, second_gain, second_bias))
+    results = first_section(latents, first_gain, columns(first_kernel), first_bias)
+    return second_section(results, latents, second_gain, columns(second_kernel), second_bias)
 
 
 def solution(mesh):

time: 63.4 us -> 54.7 us (0.86)
  waiting for transfers between devices: 24.9 us -> 11 us
  starting transfers between devices: 14.5 us -> 19.8 us
    ppermute x4 -> x5, waiting for transfers between devices: 20.6 us -> 4.2 us  [shift(): return lax.ppermute(array, 'tm', ring('tm', 1))]
    ppermute x6, waiting for transfers between devices: 3.31 us -> 6.74 us  [exchange_rows(): up = lax.ppermute(bottom, 'height', ring('height', 1))]
    ppermute x4 -> x5, starting transfers between devices: 5.74 us -> 8.8 us  [shift(): return lax.ppermute(array, 'tm', ring('tm', 1))]
    unnamed x14 -> x22, local copies, waits for them, and re-layouts: 3.18 us -> 5 us
    ppermute x6, starting transfers between devices: 0.86 us -> 2.22 us  [exchange_rows(): up = lax.ppermute(bottom, 'height', ring('height', 1))]
    broadcast_in_dim x4 -> x0, local copies, waits for them, and re-layouts: 1.33 us -> none  [the longest x1 0.66 us: per_device(): first_gain[None]]
    ppermute x6, waiting for transfers between devices: 1.03 us -> 0.05 us  [exchange_rows(): down = lax.ppermute(top, 'height', ring('height', -1))]
    ppermute x6, starting transfers between devices: 7.93 us -> 8.76 us  [exchange_rows(): down = lax.ppermute(top, 'height', ring('height', -1))]
  transfers between devices with their start and end apart: 16 -> 17, of which waited for: 7 -> 8; matrix products, arithmetic and copies ran while one was open for 4% -> 2% of each run, Pallas kernels for 20% -> 26%
where the time goes in v2:
time: 54.7 us; the launch traced here: 54.3 us
  starting transfers between devices  19.8 us (36%)
  Pallas kernels  16.3 us (30%)
  waiting for transfers between devices  11 us (20%)
  local copies, waits for them, and re-layouts  7.02 us (13%)
    pallas_call x6, Pallas kernels, call(): pl.pallas_call(body, grid=(1,), in_specs=[s for _, s in args], out_specs=...  16.2 us
    ppermute x5, starting transfers between devices, shift(): return lax.ppermute(array, 'tm', ring('tm', 1))  8.8 us
    ppermute x6, starting transfers between devices, exchange_rows(): down = lax.ppermute(top, 'height', ring('height', -1))  8.76 us
    ppermute x6, waiting for transfers between devices, exchange_rows(): up = lax.ppermute(bottom, 'height', ring('height', 1))  6.74 us
    unnamed x22, local copies, waits for them, and re-layouts  5 us
    ppermute x5, waiting for transfers between devices, shift(): return lax.ppermute(array, 'tm', ring('tm', 1))  4.2 us
    ppermute x6, starting transfers between devices, exchange_rows(): up = lax.ppermute(bottom, 'height', ring('height', 1))  2.22 us
  transfers between devices with their start and end apart: 17, of which 8 were waited for; matrix products, arithmetic and copies ran while one was open for 2% of the time, Pallas kernels for 26%

profile of v2, /device:TPU:0, one launch (start us, length us, event | category | flops | bytes accessed | tf_op | source)
XLA Modules:
  0.0 54.3 jit_solution(6344037325587568015)
XLA Ops:
  0.0 1.0 %slice.30 = bf16[1,8,104,256]{3,2,1,0:T(8,128)(2,1)S(1)} slice(bf16[2,8,104,256]{3,2,1,0:T(8,128)(2,1)} %refs_8_.1), slice={[1:2], [0:8], [0:104], [0:256]} | slice | bytes 851968 | tf_op jit(solution)/shard_map/slice | solution.py:251
  1.0 3.0 %collective-permute-start.4 = (bf16[1,8,104,256]{3,2,1,0:T(8,128)(2,1)S(1)}, bf16[1,8,104,256]{3,2,1,0:T(8,128)(2,1)S(1)}, u32[]{:S(2)}, u32[]{:S(2)}) collective-permute-start(bf16[1,8,104,256]{3,2,1,0:T(8,128)(2,1)S(1)} %slice.30), channel_id=1, source_target_pairs={{0,4},{4,8},{8,12},{12,16},{16,20},{20,24},{24,28},{28,0},{1,5},{5... | collective-permute-start | bytes 1277960 | tf_op jit(solution)/shard_map/ppermute | solution.py:204
  4.0 1.0 %slice_bitcast_fusion = (bf16[2,104,256]{2,1,0:T(8,128)(2,1)S(1)}, bf16[2,104,256]{2,1,0:T(8,128)(2,1)S(1)}) fusion(bf16[2,8,104,256]{3,2,1,0:T(8,128)(2,1)} %refs_8_.1), kind=kLoop, calls=%fused_computation.2 | loop fusion | bytes 425984 | tf_op jit(solution)/shard_map/squeeze | solution.py:252
  5.0 0.1 collective-permute-start
  5.1 1.7 %collective-permute-start.5 = (bf16[2,104,256]{2,1,0:T(8,128)(2,1)S(1)}, bf16[2,104,256]{2,1,0:T(8,128)(2,1)S(1)}, u32[]{:S(2)}, u32[]{:S(2)}) collective-permute-start(bf16[2,104,256]{2,1,0:T(8,128)(2,1)S(1)} %get-tuple-element.41), channel_id=1, source_target_pairs={{0,3},{1,0},{2,1},{3,2},{4,7},{5,4},{6,5},{7,6},{8,11},{9,8},{10,9... | collective-permute-start | bytes 319496 | tf_op jit(solution)/shard_map/ppermute | solution.py:195
  6.8 2.4 %collective-permute-done.refs_1_.up = bf16[2,104,256]{2,1,0:T(8,128)(2,1)S(1)} collective-permute-done((bf16[2,104,256]{2,1,0:T(8,128)(2,1)S(1)}, bf16[2,104,256]{2,1,0:T(8,128)(2,1)S(1)}, u32[]{:S(2)}, u32[]{:S(2)}) %collective-permute-start) | collective-permute-done | bytes 106528 | tf_op jit(solution)/shard_map/ppermute | solution.py:194
  9.2 0.0 copy-start.3
  9.2 1.2 %copy-done.3 = bf16[2,8,104,256]{3,2,1,0:T(8,128)(2,1)S(1)} copy-done((bf16[2,8,104,256]{3,2,1,0:T(8,128)(2,1)S(1)}, bf16[2,8,104,256]{3,2,1,0:T(8,128)(2,1)}, u32[]{:S(2)}) %copy-start.3) | copy-done | bytes 851992
  10.4 1.6 %collective-permute-start.1 = (bf16[1,8,104,256]{3,2,1,0:T(8,128)(2,1)S(1)}, bf16[1,8,104,256]{3,2,1,0:T(8,128)(2,1)S(1)}, u32[]{:S(2)}, u32[]{:S(2)}) collective-permute-start(bf16[1,8,104,256]{3,2,1,0:T(8,128)(2,1)S(1)} %first.1), channel_id=1, source_target_pairs={{0,4},{4,8},{8,12},{12,16},{16,20},{20,24},{24,28},{28,0},{1,5},{5... | collective-permute-start | bytes 1277960 | tf_op jit(solution)/shard_map/ppermute | solution.py:204
  12.0 0.0 collective-permute-done.5.down
  12.0 0.0 copy-start.1
  12.0 2.0 %copy-done.1 = bf16[3,3,3,256,256]{4,3,2,1,0:T(8,128)(2,1)S(1)} copy-done((bf16[3,3,3,256,256]{4,3,2,1,0:T(8,128)(2,1)S(1)}, bf16[3,3,3,256,256]{4,3,2,1,0:T(8,128)(2,1)}, u32[]{:S(2)}) %copy-start.1) | copy-done | bytes 3538968
  14.0 0.0 copy-start.4
  14.0 1.2 %copy-done.4 = bf16[2,8,104,256]{3,2,1,0:T(8,128)(2,1)S(1)} copy-done((bf16[2,8,104,256]{3,2,1,0:T(8,128)(2,1)S(1)}, bf16[2,8,104,256]{3,2,1,0:T(8,128)(2,1)}, u32[]{:S(2)}) %copy-start.4) | copy-done | bytes 851992
  15.1 0.0 copy-start.8
  15.1 0.7 %copy-done.8 = bf16[256]{0:T(256)(128)(2,1)S(1)} copy-done((bf16[256]{0:T(256)(128)(2,1)S(1)}, bf16[256]{0:T(256)(128)(2,1)}, u32[]{:S(2)}) %copy-start.8) | copy-done | bytes 536
  15.8 0.0 copy-start.2
  15.8 0.0 copy-start.10
  15.8 3.5 %own.2 = (f32[832,256]{1,0:T(8,128)S(1)}, f32[832,256]{1,0:T(8,128)S(1)}) custom-call(bf16[2,8,104,256]{3,2,1,0:T(8,128)(2,1)S(1)} %copy-done.4, bf16[2,8,104,256]{3,2,1,0:T(8,128)(2,1)S(1)} %copy-done.4, bf16[2,104,256]{2,1,0:T(8,128)(2,1)S(1)} %collective-permute-done.refs_1_.up, bf16[2,104,256]{2,1,0:T(8,128)(2,1)S(1)} %collective-permute-done.5.down, ...), custom_call_target="tpu_custom_call" | custom-call | flops 2944401408 | bytes 6291456 | tf_op jit(solution)/shard_map/own/pallas_call | solution.py:173
  19.3 0.0 collective-permute-done.4.refs_0_.refs_1_
  19.3 0.1 collective-permute-start.6
  19.4 1.7 %collective-permute-start.7 = (bf16[1,104,256]{2,1,0:T(8,128)(2,1)S(1)}, bf16[1,104,256]{2,1,0:T(8,128)(2,1)S(1)}, u32[]{:S(2)}, u32[]{:S(2)}) collective-permute-start(bf16[1,104,256]{2,1,0:T(8,128)(2,1)S(1)} %bitcast.42), channel_id=1, source_target_pairs={{0,3},{1,0},{2,1},{3,2},{4,7},{5,4},{6,5},{7,6},{8,11},{9,8},{10,9... | collective-permute-start | bytes 159752 | tf_op jit(solution)/shard_map/ppermute | solution.py:195
  21.1 1.8 %collective-permute-done.6.refs_1_ = bf16[1,104,256]{2,1,0:T(8,128)(2,1)S(1)} collective-permute-done((bf16[1,104,256]{2,1,0:T(8,128)(2,1)S(1)}, bf16[1,104,256]{2,1,0:T(8,128)(2,1)S(1)}, u32[]{:S(2)}, u32[]{:S(2)}) %collective-permute-start.6) | collective-permute-done | bytes 53280 | tf_op jit(solution)/shard_map/ppermute | solution.py:194
  23.0 0.0 collective-permute-done.7.refs_2_
  23.0 0.0 copy-done.2
  23.0 0.0 copy-done.10
  23.0 0.0 copy-start.9
  23.0 2.5 %before.2 = (bf16[1,8,104,256]{3,2,1,0:T(8,128)(2,1)S(1)}, f32[832,256]{1,0:T(8,128)S(1)}, bf16[2,1,104,256]{3,2,1,0:T(8,128)(2,1)S(1)}) custom-call(bf16[1,8,104,256]{3,2,1,0:T(8,128)(2,1)S(1)} %collective-permute-done.4.refs_0_.refs_1_, bf16[1,104,256]{2,1,0:T(8,128)(2,1)S(1)} %collective-permute-done.6.refs_1_, ...), custom_call_target="tpu_custom_call" | custom-call | flops 1962934272 | bytes 4194304 | tf_op jit(solution)/shard_map/before/pallas_call | solution.py:173
  25.5 0.0 copy-start
  25.5 0.0 copy-start.6
  25.5 0.5 collective-permute-done.1.refs_0_
  26.0 1.9 %collective-permute-start.2 = (bf16[1,104,256]{2,1,0:T(8,128)(2,1)S(1)}, bf16[1,104,256]{2,1,0:T(8,128)(2,1)S(1)}, u32[]{:S(2)}, u32[]{:S(2)}) collective-permute-start(bf16[1,104,256]{2,1,0:T(8,128)(2,1)S(1)} %get-tuple-element.44), channel_id=1, source_target_pairs={{0,1},{1,2},{2,3},{3,0},{4,5},{5,6},{6,7},{7,4},{8,9},{9,10},{10,1... | collective-permute-start | bytes 159752 | tf_op jit(solution)/shard_map/ppermute | solution.py:194
  27.9 0.0 collective-permute-start.3
  27.9 1.2 %collective-permute-start.14 = (bf16[1,8,104,256]{3,2,1,0:T(8,128)(2,1)S(1)}, bf16[1,8,104,256]{3,2,1,0:T(8,128)(2,1)S(1)}, u32[]{:S(2)}, u32[]{:S(2)}) collective-permute-start(bf16[1,8,104,256]{3,2,1,0:T(8,128)(2,1)S(1)} %get-tuple-element.30.last_ref), channel_id=1, source_target_pairs={{0,4},{4,8},{8,12},{12,16},{16,20},{20,24},{24,28},{28,0},{1,5},{5... | collective-permute-start | bytes 1277960 | tf_op jit(solution)/shard_map/ppermute | solution.py:204
  29.1 0.5 collective-permute-done.2.refs_1_
  29.6 0.0 collective-permute-done.3.refs_2_
  29.7 0.0 copy-done.9
  29.7 1.5 %earliest.2 = (bf16[1,8,104,256]{3,2,1,0:T(8,128)(2,1)S(1)}, bf16[1,6,104,256]{3,2,1,0:T(8,128)(2,1)S(1)}, bf16[2,1,104,256]{3,2,1,0:T(8,128)(2,1)S(1)}) custom-call(bf16[1,8,104,256]{3,2,1,0:T(8,128)(2,1)S(1)} %collective-permute-done.1.refs_0_, bf16[1,104,256]{2,1,0:T(8,128)(2,1)S(1)} %collective-permute-done.2.refs_1_, ...), custom_call_target="tpu_custom_call" | custom-call | flops 981467136 | bytes 2097152 | tf_op jit(solution)/shard_map/earliest/pallas_call | solution.py:173
  31.2 1.8 %collective-permute-start.11 = (bf16[2,104,256]{2,1,0:T(8,128)(2,1)S(1)}, bf16[2,104,256]{2,1,0:T(8,128)(2,1)S(1)}, u32[]{:S(2)}, u32[]{:S(2)}) collective-permute-start(bf16[2,104,256]{2,1,0:T(8,128)(2,1)S(1)} %pad_maximum_fusion.1), channel_id=1, source_target_pairs={{0,3},{1,0},{2,1},{3,2},{4,7},{5,4},{6,5},{7,6},{8,11},{9,8},{10,9... | collective-permute-start | bytes 319496 | tf_op jit(solution)/shard_map/ppermute | solution.py:195
  33.1 0.1 collective-permute-start.10
  33.2 1.7 %collective-permute-start.9 = (bf16[2,1,104,256]{3,2,1,0:T(8,128)(2,1)S(1)}, bf16[2,1,104,256]{3,2,1,0:T(8,128)(2,1)S(1)}, u32[]{:S(2)}, u32[]{:S(2)}) collective-permute-start(bf16[2,1,104,256]{3,2,1,0:T(8,128)(2,1)S(1)} %get-tuple-element.29), channel_id=1, source_target_pairs={{0,4},{4,8},{8,12},{12,16},{16,20},{20,24},{24,28},{28,0},{1,5},{5... | collective-permute-start | bytes 319496 | tf_op jit(solution)/shard_map/ppermute | solution.py:204
  34.8 1.3 %collective-permute-start.8 = (bf16[1,6,104,256]{3,2,1,0:T(8,128)(2,1)S(1)}, bf16[1,6,104,256]{3,2,1,0:T(8,128)(2,1)S(1)}, u32[]{:S(2)}, u32[]{:S(2)}) collective-permute-start(bf16[1,6,104,256]{3,2,1,0:T(8,128)(2,1)S(1)} %get-tuple-element.28), channel_id=1, source_target_pairs={{0,4},{4,8},{8,12},{12,16},{16,20},{20,24},{24,28},{28,0},{1,5},{5... | collective-permute-start | bytes 958472 | tf_op jit(solution)/shard_map/ppermute | solution.py:204
  36.2 0.0 collective-permute-done.11.down
  36.2 2.0 %collective-permute-done.10.up = bf16[2,104,256]{2,1,0:T(8,128)(2,1)S(1)} collective-permute-done((bf16[2,104,256]{2,1,0:T(8,128)(2,1)S(1)}, bf16[2,104,256]{2,1,0:T(8,128)(2,1)S(1)}, u32[]{:S(2)}, u32[]{:S(2)}) %collective-permute-start.10) | collective-permute-done | bytes 106528 | tf_op jit(solution)/shard_map/ppermute | solution.py:194
  38.2 0.0 copy-done
  38.2 0.0 copy-done.6
  38.2 0.0 copy-start.5
  38.2 0.0 copy-start.7
  38.2 3.5 %own.3 = (f32[832,256]{1,0:T(8,128)S(1)}, f32[832,256]{1,0:T(8,128)S(1)}) custom-call(bf16[1,8,104,256]{3,2,1,0:T(8,128)(2,1)S(1)} %get-tuple-element.30.last_ref, bf16[1,8,104,256]{3,2,1,0:T(8,128)(2,1)S(1)} %get-tuple-element.31.first_ref, bf16[2,104,256]{2,1,0:T(8,128)(2,1)S(1)} %collective-permute-done.10.up, ...), custom_call_target="tpu_custom_call" | custom-call | flops 2944401408 | bytes 6291456 | tf_op jit(solution)/shard_map/own/pallas_call | solution.py:173
  41.7 1.6 %collective-permute-done.14.refs_0_.refs_1_ = bf16[1,8,104,256]{3,2,1,0:T(8,128)(2,1)S(1)} collective-permute-done((bf16[1,8,104,256]{3,2,1,0:T(8,128)(2,1)S(1)}, bf16[1,8,104,256]{3,2,1,0:T(8,128)(2,1)S(1)}, u32[]{:S(2)}, u32[]{:S(2)}) %collective-permute-start.14) | collective-permute-done | bytes 426016 | tf_op jit(solution)/shard_map/ppermute | solution.py:204
  43.3 0.1 collective-permute-start.15
  43.3 1.7 %collective-permute-start.16 = (bf16[1,104,256]{2,1,0:T(8,128)(2,1)S(1)}, bf16[1,104,256]{2,1,0:T(8,128)(2,1)S(1)}, u32[]{:S(2)}, u32[]{:S(2)}) collective-permute-start(bf16[1,104,256]{2,1,0:T(8,128)(2,1)S(1)} %bitcast.39), channel_id=1, source_target_pairs={{0,3},{1,0},{2,1},{3,2},{4,7},{5,4},{6,5},{7,6},{8,11},{9,8},{10,9... | collective-permute-start | bytes 159752 | tf_op jit(solution)/shard_map/ppermute | solution.py:195
  45.1 0.5 collective-permute-done.9.refs_0_.refs_1_
  45.6 0.1 collective-permute-start.12
  45.6 1.7 %collective-permute-start.13 = (bf16[1,104,256]{2,1,0:T(8,128)(2,1)S(1)}, bf16[1,104,256]{2,1,0:T(8,128)(2,1)S(1)}, u32[]{:S(2)}, u32[]{:S(2)}) collective-permute-start(bf16[1,104,256]{2,1,0:T(8,128)(2,1)S(1)} %bitcast.38), channel_id=1, source_target_pairs={{0,3},{1,0},{2,1},{3,2},{4,7},{5,4},{6,5},{7,6},{8,11},{9,8},{10,9... | collective-permute-start | bytes 159752 | tf_op jit(solution)/shard_map/ppermute | solution.py:195
  47.4 0.0 collective-permute-done.15.refs_1_
  47.4 0.0 collective-permute-done.16.refs_2_
  47.4 0.0 copy-done.5
  47.4 0.0 copy-done.7
  47.4 3.0 %before.3 = (bf16[2,8,104,256]{3,2,1,0:T(8,128)(2,1)}, f32[832,256]{1,0:T(8,128)S(1)}) custom-call(bf16[1,8,104,256]{3,2,1,0:T(8,128)(2,1)S(1)} %collective-permute-done.14.refs_0_.refs_1_, bf16[1,104,256]{2,1,0:T(8,128)(2,1)S(1)} %collective-permute-done.15.refs_1_, bf16[1,104,256]{2,1,0:T(8,128)(2,1)S(1)} %collective-permute-done.16.refs_2_, ...), custom_call_target="tpu_custom_call" | custom-call | flops 1962934272 | bytes 4194304 | tf_op jit(solution)/shard_map/before/pallas_call | solution.py:173
  50.3 0.0 collective-permute-done.12.refs_2_
  50.3 0.0 collective-permute-done.13.refs_3_
  50.3 1.7 %collective-permute-done.8.refs_0_ = bf16[1,6,104,256]{3,2,1,0:T(8,128)(2,1)S(1)} collective-permute-done((bf16[1,6,104,256]{3,2,1,0:T(8,128)(2,1)S(1)}, bf16[1,6,104,256]{3,2,1,0:T(8,128)(2,1)S(1)}, u32[]{:S(2)}, u32[]{:S(2)}) %collective-permute-start.8) | collective-permute-done | bytes 319520 | tf_op jit(solution)/shard_map/ppermute | solution.py:204
  52.0 2.3 %earliest.3 = bf16[2,8,104,256]{3,2,1,0:T(8,128)(2,1)} custom-call(bf16[1,6,104,256]{3,2,1,0:T(8,128)(2,1)S(1)} %collective-permute-done.8.refs_0_, bf16[2,1,104,256]{3,2,1,0:T(8,128)(2,1)S(1)} %collective-permute-done.9.refs_0_.refs_1_, bf16[1,104,256]{2,1,0:T(8,128)(2,1)S(1)} %collective-permute-done.12.refs_2_, ...), custom_call_target="tpu_custom_call", output_to_operand_aliasing={{}: (9, {})} | custom-call | flops 981467136 | bytes 2097152 | tf_op jit(solution)/shard_map/earliest/pallas_call | solution.py:173
  (9 shorter events, 0.1 us)
Async XLA Ops:
  1.0 18.3 %collective-permute-start.4 = (bf16[1,8,104,256]{3,2,1,0:T(8,128)(2,1)S(1)}, bf16[1,8,104,256]{3,2,1,0:T(8,128)(2,1)S(1)}, u32[]{:S(2)}, u32[]{:S(2)}) collective-permute-start(bf16[1,8,104,256]{3,2,1,0:T(8,128)(2,1)S(1)} %slice.30), channel_id=1, source_target_pairs={{0,4},{4,8},{8,12},{12,16},{16,20},{20,24},{24,28},{28,0},{1,5},{5... | collective-permute-start | bytes 1277960 | tf_op jit(solution)/shard_map/ppermute | solution.py:204
  5.0 4.2 %collective-permute-start = (bf16[2,104,256]{2,1,0:T(8,128)(2,1)S(1)}, bf16[2,104,256]{2,1,0:T(8,128)(2,1)S(1)}, u32[]{:S(2)}, u32[]{:S(2)}) collective-permute-start(bf16[2,104,256]{2,1,0:T(8,128)(2,1)S(1)} %get-tuple-element.42), channel_id=1, source_target_pairs={{0,1},{1,2},{2,3},{3,0},{4,5},{5,6},{6,7},{7,4},{8,9},{9,10},{10,1... | collective-permute-start | bytes 319496 | tf_op jit(solution)/shard_map/ppermute | solution.py:194
  5.1 6.9 %collective-permute-start.5 = (bf16[2,104,256]{2,1,0:T(8,128)(2,1)S(1)}, bf16[2,104,256]{2,1,0:T(8,128)(2,1)S(1)}, u32[]{:S(2)}, u32[]{:S(2)}) collective-permute-start(bf16[2,104,256]{2,1,0:T(8,128)(2,1)S(1)} %get-tuple-element.41), channel_id=1, source_target_pairs={{0,3},{1,0},{2,1},{3,2},{4,7},{5,4},{6,5},{7,6},{8,11},{9,8},{10,9... | collective-permute-start | bytes 319496 | tf_op jit(solution)/shard_map/ppermute | solution.py:195
  9.2 1.2 %copy-start.3 = (bf16[2,8,104,256]{3,2,1,0:T(8,128)(2,1)S(1)}, bf16[2,8,104,256]{3,2,1,0:T(8,128)(2,1)}, u32[]{:S(2)}) copy-start(bf16[2,8,104,256]{3,2,1,0:T(8,128)(2,1)} %refs_8_.1) | copy-start | bytes 2555908
  10.4 15.6 %collective-permute-start.1 = (bf16[1,8,104,256]{3,2,1,0:T(8,128)(2,1)S(1)}, bf16[1,8,104,256]{3,2,1,0:T(8,128)(2,1)S(1)}, u32[]{:S(2)}, u32[]{:S(2)}) collective-permute-start(bf16[1,8,104,256]{3,2,1,0:T(8,128)(2,1)S(1)} %first.1), channel_id=1, source_target_pairs={{0,4},{4,8},{8,12},{12,16},{16,20},{20,24},{24,28},{28,0},{1,5},{5... | collective-permute-start | bytes 1277960 | tf_op jit(solution)/shard_map/ppermute | solution.py:204
  12.0 2.0 %copy-start.1 = (bf16[3,3,3,256,256]{4,3,2,1,0:T(8,128)(2,1)S(1)}, bf16[3,3,3,256,256]{4,3,2,1,0:T(8,128)(2,1)}, u32[]{:S(2)}) copy-start(bf16[3,3,3,256,256]{4,3,2,1,0:T(8,128)(2,1)} %param.9) | copy-start | bytes 10616836
  14.0 1.2 %copy-start.4 = (bf16[2,8,104,256]{3,2,1,0:T(8,128)(2,1)S(1)}, bf16[2,8,104,256]{3,2,1,0:T(8,128)(2,1)}, u32[]{:S(2)}) copy-start(bf16[2,8,104,256]{3,2,1,0:T(8,128)(2,1)} %refs_8_.1) | copy-start | bytes 2555908
  15.1 0.7 %copy-start.8 = (bf16[256]{0:T(256)(128)(2,1)S(1)}, bf16[256]{0:T(256)(128)(2,1)}, u32[]{:S(2)}) copy-start(bf16[256]{0:T(256)(128)(2,1)} %refs_3_.4) | copy-start | bytes 1540
  15.8 7.2 %copy-start.2 = (bf16[3,3,3,256,256]{4,3,2,1,0:T(8,128)(2,1)S(1)}, bf16[3,3,3,256,256]{4,3,2,1,0:T(8,128)(2,1)}, u32[]{:S(2)}) copy-start(bf16[3,3,3,256,256]{4,3,2,1,0:T(8,128)(2,1)} %param.9) | copy-start | bytes 10616836
  15.8 7.2 %copy-start.10 = (bf16[256]{0:T(256)(128)(2,1)S(1)}, bf16[256]{0:T(256)(128)(2,1)}, u32[]{:S(2)}) copy-start(bf16[256]{0:T(256)(128)(2,1)} %refs_5_.1) | copy-start | bytes 1540
  19.3 3.6 %collective-permute-start.6 = (bf16[1,104,256]{2,1,0:T(8,128)(2,1)S(1)}, bf16[1,104,256]{2,1,0:T(8,128)(2,1)S(1)}, u32[]{:S(2)}, u32[]{:S(2)}) collective-permute-start(bf16[1,104,256]{2,1,0:T(8,128)(2,1)S(1)} %bitcast.43), channel_id=1, source_target_pairs={{0,1},{1,2},{2,3},{3,0},{4,5},{5,6},{6,7},{7,4},{8,9},{9,10},{10,1... | collective-permute-start | bytes 159752 | tf_op jit(solution)/shard_map/ppermute | solution.py:194
  19.4 3.5 %collective-permute-start.7 = (bf16[1,104,256]{2,1,0:T(8,128)(2,1)S(1)}, bf16[1,104,256]{2,1,0:T(8,128)(2,1)S(1)}, u32[]{:S(2)}, u32[]{:S(2)}) collective-permute-start(bf16[1,104,256]{2,1,0:T(8,128)(2,1)S(1)} %bitcast.42), channel_id=1, source_target_pairs={{0,3},{1,0},{2,1},{3,2},{4,7},{5,4},{6,5},{7,6},{8,11},{9,8},{10,9... | collective-permute-start | bytes 159752 | tf_op jit(solution)/shard_map/ppermute | solution.py:195
  23.0 6.7 %copy-start.9 = (bf16[256]{0:T(256)(128)(2,1)S(1)}, bf16[256]{0:T(256)(128)(2,1)}, u32[]{:S(2)}) copy-start(bf16[256]{0:T(256)(128)(2,1)} %refs_3_.4) | copy-start | bytes 1540
  25.5 12.7 %copy-start = (bf16[3,3,3,256,256]{4,3,2,1,0:T(8,128)(2,1)S(1)}, bf16[3,3,3,256,256]{4,3,2,1,0:T(8,128)(2,1)}, u32[]{:S(2)}) copy-start(bf16[3,3,3,256,256]{4,3,2,1,0:T(8,128)(2,1)} %param.12) | copy-start | bytes 10616836
  25.5 12.7 %copy-start.6 = (bf16[256]{0:T(256)(128)(2,1)S(1)}, bf16[256]{0:T(256)(128)(2,1)}, u32[]{:S(2)}) copy-start(bf16[256]{0:T(256)(128)(2,1)} %refs_4_.1) | copy-start | bytes 1540
  26.0 3.6 %collective-permute-start.2 = (bf16[1,104,256]{2,1,0:T(8,128)(2,1)S(1)}, bf16[1,104,256]{2,1,0:T(8,128)(2,1)S(1)}, u32[]{:S(2)}, u32[]{:S(2)}) collective-permute-start(bf16[1,104,256]{2,1,0:T(8,128)(2,1)S(1)} %get-tuple-element.44), channel_id=1, source_target_pairs={{0,1},{1,2},{2,3},{3,0},{4,5},{5,6},{6,7},{7,4},{8,9},{9,10},{10,1... | collective-permute-start | bytes 159752 | tf_op jit(solution)/shard_map/ppermute | solution.py:194
  27.9 1.8 %collective-permute-start.3 = (bf16[1,104,256]{2,1,0:T(8,128)(2,1)S(1)}, bf16[1,104,256]{2,1,0:T(8,128)(2,1)S(1)}, u32[]{:S(2)}, u32[]{:S(2)}) collective-permute-start(bf16[1,104,256]{2,1,0:T(8,128)(2,1)S(1)} %get-tuple-element.43), channel_id=1, source_target_pairs={{0,3},{1,0},{2,1},{3,2},{4,7},{5,4},{6,5},{7,6},{8,11},{9,8},{10,9... | collective-permute-start | bytes 159752 | tf_op jit(solution)/shard_map/ppermute | solution.py:195
  27.9 15.4 %collective-permute-start.14 = (bf16[1,8,104,256]{3,2,1,0:T(8,128)(2,1)S(1)}, bf16[1,8,104,256]{3,2,1,0:T(8,128)(2,1)S(1)}, u32[]{:S(2)}, u32[]{:S(2)}) collective-permute-start(bf16[1,8,104,256]{3,2,1,0:T(8,128)(2,1)S(1)} %get-tuple-element.30.last_ref), channel_id=1, source_target_pairs={{0,4},{4,8},{8,12},{12,16},{16,20},{20,24},{24,28},{28,0},{1,5},{5... | collective-permute-start | bytes 1277960 | tf_op jit(solution)/shard_map/ppermute | solution.py:204
  31.2 4.9 %collective-permute-start.11 = (bf16[2,104,256]{2,1,0:T(8,128)(2,1)S(1)}, bf16[2,104,256]{2,1,0:T(8,128)(2,1)S(1)}, u32[]{:S(2)}, u32[]{:S(2)}) collective-permute-start(bf16[2,104,256]{2,1,0:T(8,128)(2,1)S(1)} %pad_maximum_fusion.1), channel_id=1, source_target_pairs={{0,3},{1,0},{2,1},{3,2},{4,7},{5,4},{6,5},{7,6},{8,11},{9,8},{10,9... | collective-permute-start | bytes 319496 | tf_op jit(solution)/shard_map/ppermute | solution.py:195
  33.1 5.1 %collective-permute-start.10 = (bf16[2,104,256]{2,1,0:T(8,128)(2,1)S(1)}, bf16[2,104,256]{2,1,0:T(8,128)(2,1)S(1)}, u32[]{:S(2)}, u32[]{:S(2)}) collective-permute-start(bf16[2,104,256]{2,1,0:T(8,128)(2,1)S(1)} %pad_maximum_fusion), channel_id=1, source_target_pairs={{0,1},{1,2},{2,3},{3,0},{4,5},{5,6},{6,7},{7,4},{8,9},{9,10},{10,1... | collective-permute-start | bytes 319496 | tf_op jit(solution)/shard_map/ppermute | solution.py:194
  33.2 12.3 %collective-permute-start.9 = (bf16[2,1,104,256]{3,2,1,0:T(8,128)(2,1)S(1)}, bf16[2,1,104,256]{3,2,1,0:T(8,128)(2,1)S(1)}, u32[]{:S(2)}, u32[]{:S(2)}) collective-permute-start(bf16[2,1,104,256]{3,2,1,0:T(8,128)(2,1)S(1)} %get-tuple-element.29), channel_id=1, source_target_pairs={{0,4},{4,8},{8,12},{12,16},{16,20},{20,24},{24,28},{28,0},{1,5},{5... | collective-permute-start | bytes 319496 | tf_op jit(solution)/shard_map/ppermute | solution.py:204
  34.8 17.2 %collective-permute-start.8 = (bf16[1,6,104,256]{3,2,1,0:T(8,128)(2,1)S(1)}, bf16[1,6,104,256]{3,2,1,0:T(8,128)(2,1)S(1)}, u32[]{:S(2)}, u32[]{:S(2)}) collective-permute-start(bf16[1,6,104,256]{3,2,1,0:T(8,128)(2,1)S(1)} %get-tuple-element.28), channel_id=1, source_target_pairs={{0,4},{4,8},{8,12},{12,16},{16,20},{20,24},{24,28},{28,0},{1,5},{5... | collective-permute-start | bytes 958472 | tf_op jit(solution)/shard_map/ppermute | solution.py:204
  38.2 9.2 %copy-start.5 = (bf16[2,8,104,256]{3,2,1,0:T(8,128)(2,1)S(1)}, bf16[2,8,104,256]{3,2,1,0:T(8,128)(2,1)}, u32[]{:S(2)}) copy-start(bf16[2,8,104,256]{3,2,1,0:T(8,128)(2,1)} %refs_8_.1) | copy-start | bytes 2555908
  38.2 9.2 %copy-start.7 = (bf16[256]{0:T(256)(128)(2,1)S(1)}, bf16[256]{0:T(256)(128)(2,1)}, u32[]{:S(2)}) copy-start(bf16[256]{0:T(256)(128)(2,1)} %refs_6_.5) | copy-start | bytes 1540
  43.3 4.1 %collective-permute-start.15 = (bf16[1,104,256]{2,1,0:T(8,128)(2,1)S(1)}, bf16[1,104,256]{2,1,0:T(8,128)(2,1)S(1)}, u32[]{:S(2)}, u32[]{:S(2)}) collective-permute-start(bf16[1,104,256]{2,1,0:T(8,128)(2,1)S(1)} %bitcast.41), channel_id=1, source_target_pairs={{0,1},{1,2},{2,3},{3,0},{4,5},{5,6},{6,7},{7,4},{8,9},{9,10},{10,1... | collective-permute-start | bytes 159752 | tf_op jit(solution)/shard_map/ppermute | solution.py:194
  43.3 4.0 %collective-permute-start.16 = (bf16[1,104,256]{2,1,0:T(8,128)(2,1)S(1)}, bf16[1,104,256]{2,1,0:T(8,128)(2,1)S(1)}, u32[]{:S(2)}, u32[]{:S(2)}) collective-permute-start(bf16[1,104,256]{2,1,0:T(8,128)(2,1)S(1)} %bitcast.39), channel_id=1, source_target_pairs={{0,3},{1,0},{2,1},{3,2},{4,7},{5,4},{6,5},{7,6},{8,11},{9,8},{10,9... | collective-permute-start | bytes 159752 | tf_op jit(solution)/shard_map/ppermute | solution.py:195
  45.6 4.8 %collective-permute-start.12 = (bf16[1,104,256]{2,1,0:T(8,128)(2,1)S(1)}, bf16[1,104,256]{2,1,0:T(8,128)(2,1)S(1)}, u32[]{:S(2)}, u32[]{:S(2)}) collective-permute-start(bf16[1,104,256]{2,1,0:T(8,128)(2,1)S(1)} %bitcast.40), channel_id=1, source_target_pairs={{0,1},{1,2},{2,3},{3,0},{4,5},{5,6},{6,7},{7,4},{8,9},{9,10},{10,1... | collective-permute-start | bytes 159752 | tf_op jit(solution)/shard_map/ppermute | solution.py:194
  45.6 4.7 %collective-permute-start.13 = (bf16[1,104,256]{2,1,0:T(8,128)(2,1)S(1)}, bf16[1,104,256]{2,1,0:T(8,128)(2,1)S(1)}, u32[]{:S(2)}, u32[]{:S(2)}) collective-permute-start(bf16[1,104,256]{2,1,0:T(8,128)(2,1)S(1)} %bitcast.38), channel_id=1, source_target_pairs={{0,3},{1,0},{2,1},{3,2},{4,7},{5,4},{6,5},{7,6},{8,11},{9,8},{10,9... | collective-permute-start | bytes 159752 | tf_op jit(solution)/shard_map/ppermute | solution.py:195

commit v3 on v2

--- a/solution.py
+++ b/solution.py
@@ -58,30 +58,28 @@
     row_id, rows = lax.axis_index("height"), lax.axis_size("height")
     above = (row_id > 0).astype(F32)
     below = (row_id < rows - 1).astype(F32)
-    before = (lax.axis_index("tm") > 0).astype(F32)
-    return above, below, before
-
-
-def load_frame(frame, up, down, gain, bufs, time_halo, edges=None):
+    return above, below
+
+
+def load_frame(frame, inward, outward, gain, bufs, edges=None):
     shifts, even, odd = bufs
     rows, cells = frame.shape[0], frame.shape[1]
     if edges is not None:
         rows += 2
-    above, below, before = masks()
-    if time_halo:
-        above, below = above * before, below * before
+    above, below = masks()
+
+    lower = lax.axis_index("height") % 2 == 0
 
     def get_row(r):
         if r == 0:
-            return up, above
+            return jnp.where(lower, outward, inward), above
         if r == rows + 1:
-            return down, below
-        own = before if time_halo else None
+            return jnp.where(lower, inward, outward), below
         if edges is None:
-            return frame[r - 1], own
+            return frame[r - 1], None
         if r in (1, rows):
-            return edges[0 if r == 1 else 1, 0], own
-        return frame[r - 2], own
+            return edges[0 if r == 1 else 1, 0], None
+        return frame[r - 2], None
 
     activate_rows(get_row, gain[...].astype(F32)[None], shifts, rows + 2, cells)
     pack(shifts, even, odd, rows + 2, cells)
@@ -92,14 +90,14 @@
     return [(s, step) for s in range(0, rows * cells, step)]
 
 
-def own_kernel(last_ref, first_ref, up, down, gain, k1, k2, acc_first, acc_last, *bufs):
+def own_kernel(last_ref, first_ref, up, down, gain, k1, k2, _, acc_first, acc_last, *bufs):
     last, first = last_ref.at[0], first_ref.at[0]
     rows, cells = last.shape[0], last.shape[1]
     even, odd = bufs[1:]
-    load_frame(last, up[1], down[1], gain, bufs, False)
+    load_frame(last, up[1], down[1], gain, bufs)
     for s, n in chunks(rows, cells):
         acc_last[s : s + n] = taps(even, odd, k2, s, n, cells)
-    load_frame(first, up[0], down[0], gain, bufs, False)
+    load_frame(first, up[0], down[0], gain, bufs)
     for s, n in chunks(rows, cells):
         acc_last[s : s + n] += taps(even, odd, k1, s, n, cells)
         acc_first[s : s + n] = taps(even, odd, k2, s, n, cells)
@@ -111,6 +109,12 @@
     if residual is not None:
         value = residual[0, r].astype(F32) + value
     out[0, r] = value.astype(BF16)
+
+
+def frames_before(body):
+    first = lax.axis_index("tm") == 0
+    pl.when(first)(lambda: body(False))
+    pl.when(jnp.logical_not(first))(lambda: body(True))
 
 
 def before_kernel(residual, *refs):
@@ -128,15 +132,25 @@
     frame = frame.at[0]
     rows, cells = frame.shape[0], frame.shape[1]
     even, odd = bufs[1:]
-    load_frame(frame, up[0], down[0], gain, bufs, True)
-    for s, n in chunks(rows, cells):
-        total = acc_last[s : s + n] + taps(even, odd, k0, s, n, cells)
-        finish(total, bias, res, out, s, n, cells)
+
+    @frames_before
+    def _(there):
+        if there:
+            load_frame(frame, up[0], down[0], gain, bufs)
+        for s, n in chunks(rows, cells):
+            total = acc_last[s : s + n]
+            if there:
+                total = total + taps(even, odd, k0, s, n, cells)
+            finish(total, bias, res, out, s, n, cells)
+        for s, n in chunks(rows, cells):
+            total = acc_first[s : s + n]
+            if there:
+                total = total + taps(even, odd, k1, s, n, cells)
+            acc_out[s : s + n] = total
+
     if edges is not None:
         edges[0, 0] = out[0, 0]
         edges[1, 0] = out[0, rows - 1]
-    for s, n in chunks(rows, cells):
-        acc_out[s : s + n] = acc_first[s : s + n] + taps(even, odd, k1, s, n, cells)
 
 
 def earliest_kernel(residual, *refs):
@@ -147,10 +161,17 @@
         edges = res = None
     rows, cells = out.shape[1], out.shape[2]
     even, odd = bufs[1:]
-    load_frame(frame.at[0], up[0], down[0], gain, bufs, True, edges)
-    for s, n in chunks(rows, cells):
-        total = acc_first[s : s + n] + taps(even, odd, k0, s, n, cells)
-        finish(total, bias, res, out, s, n, cells)
+
+    @frames_before
+    def _(there):
+        if there:
+            load_frame(frame.at[0], up[0], down[0], gain, bufs, edges)
+        for s, n in chunks(rows, cells):
+            total = acc_first[s : s + n]
+            if there:
+                total = total + taps(even, odd, k0, s, n, cells)
+            finish(total, bias, res, out, s, n, cells)
+
     if not residual:
         edges_out[0, 0] = out[0, 0]
         edges_out[1, 0] = out[0, rows - 1]
@@ -190,10 +211,12 @@
     )(*arrays)
 
 
-def exchange_rows(top, bottom):
-    up = lax.ppermute(bottom, "height", ring("height", 1))
-    down = lax.ppermute(top, "height", ring("height", -1))
-    return up, down
+def exchange_rows(inward, outward):
+    bands = lax.axis_size("height")
+    pairs = [(i, i ^ 1) for i in range(bands)]
+    others = [(i, (i + (1 if i % 2 else -1)) % bands) for i in range(bands)]
+    outward = lax.ppermute(outward, "height", others)
+    return lax.ppermute(inward, "height", pairs), outward
 
 
 def w(array):
@@ -213,9 +236,9 @@
     return acc, frame, inner, edge
 
 
-def own(last, first, up, down, gain, k):
+def own(last, first, up, down, gain, k, token):
     acc = shapes()[0]
-    args = [last, first, w(up), w(down), gain, k[1], k[2]]
+    args = [last, first, w(up), w(down), gain, k[1], k[2], (token, pl.BlockSpec(memory_space=pl.ANY))]
     return call(own_kernel, "own", 3, [whole(acc.shape)] * 2, [acc, acc], args)
 
 
@@ -237,10 +260,32 @@
     )(*[array for array, _ in blocks], token)
 
 
-def rows_after(token, array, places):
-    block = (1, 1, *array.shape[2:])
-    blocks = [(array, pl.BlockSpec(block, lambda i, p=p: (*p, 0, 0))) for p in places]
-    return [a[0] for a in after(token, blocks, "edges")]
+def rows_after(token, *sources):
+    def copy(*refs):
+        count = len(sources)
+        inward, outward = refs[-2:]
+        lower = lax.axis_index("height") % 2 == 0
+        for n in range(count):
+            top, bottom = (ref.reshape(inward.shape[1:])[...] for ref in refs[2 * n : 2 * n + 2])
+            inward[n] = jnp.where(lower, bottom, top)
+            outward[n] = jnp.where(lower, top, bottom)
+
+    args = []
+    for array, *places in sources:
+        for place in places:
+            block = (1,) * len(place) + array.shape[len(place) :]
+            tail = (0,) * (array.ndim - len(place))
+            args.append((array, pl.BlockSpec(block, lambda i, p=place, t=tail: (*p, *t))))
+    out = jax.ShapeDtypeStruct((len(sources), *sources[0][0].shape[-2:]), BF16)
+    return pl.pallas_call(
+        copy,
+        grid=(1,),
+        in_specs=[spec for _, spec in args] + [pl.BlockSpec(memory_space=pl.ANY)],
+        out_specs=[whole(out.shape)] * 2,
+        out_shape=[out] * 2,
+        compiler_params=pltpu.CompilerParams(vmem_limit_bytes=4 * 2**20),
+        name="edges",
+    )(*[array for array, _ in args], token)
 
 
 def first_section(latents, gain, kernel, bias):
@@ -249,17 +294,18 @@
     k = [(kernel, part(kernel.shape, i)) for i in range(3)]
     last, first = ((latents, part(latents.shape, i)) for i in (1, 0))
     before = shift(latents[1:])
-    edges = latents[:, 0], latents[:, rows - 1]
-    up, down = exchange_rows(*edges)
+    bottom = rows - 1
+    up, down = exchange_rows(*rows_after(gain[0], (latents, (0, 0), (0, bottom)), (latents, (1, 0), (1, bottom))))
     earliest = shift(after(up, [first], "first")[0])
-    acc_first, acc_last = own(last, first, up, down, gain, k)
-    up, down = exchange_rows(*rows_after(acc_last, before, [(0, 0), (0, rows - 1)]))
+    before_edges = rows_after(up, (before, (0, 0), (0, bottom)))
+    acc_first, acc_last = own(last, first, up, down, gain, k, before_edges[0])
+    up, down = exchange_rows(*before_edges)
     args = [w(before), w(up), w(down), gain, k[0], k[1], bias, w(acc_first), w(acc_last)]
     outs = [frame, acc, edge]
     y_last, acc_first, edge_last = call(
         functools.partial(before_kernel, False), "before", 2, [whole(o.shape) for o in outs], outs, args
     )
-    up, down = exchange_rows(earliest[:, 0], earliest[:, rows - 1])
+    up, down = exchange_rows(*rows_after(y_last, (earliest, (0, 0), (0, bottom))))
     args = [w(earliest), w(up), w(down), gain, k[0], bias, w(acc_first)]
     outs = [frame, inner, edge]
     y_first, inner_first, edge_first = call(
@@ -276,10 +322,10 @@
     before = shift(y_last)
     earliest_edges = shift(edge_first)
     earliest = shift(inner_first)
-    edges = [jnp.concatenate([edge_first[i], edge_last[i]]) for i in range(2)]
-    up, down = exchange_rows(*edges)
-    acc_first, acc_last = own(w(y_last), w(y_first), up, down, gain, k)
-    up, down = exchange_rows(*rows_after(acc_last, before, [(0, 0), (0, rows - 1)]))
+    up, down = exchange_rows(*rows_after(edge_first, (edge_first, (0,), (1,)), (edge_last, (0,), (1,))))
+    before_edges = rows_after(up, (before, (0, 0), (0, rows - 1)))
+    acc_first, acc_last = own(w(y_last), w(y_first), up, down, gain, k, before_edges[0])
+    up, down = exchange_rows(*before_edges)
     args = [w(before), w(up), w(down), gain, k[0], k[1], bias, w(acc_first), w(acc_last)]
     args.append((latents, part(latents.shape, 1)))
     out = jax.ShapeDtypeStruct(latents.shape, BF16)
@@ -291,7 +337,7 @@
         [out, acc],
         args,
     )
-    up, down = exchange_rows(*rows_after(acc_last, earliest_edges, [(0, 0), (1, 0)]))
+    up, down = exchange_rows(*rows_after(acc_last, (earliest_edges, (0,), (1,))))
     args = [w(earliest), w(earliest_edges), w(up), w(down), gain, k[0], bias, w(acc_first)]
     args += [(latents, part(latents.shape, 0)), (half, pl.BlockSpec(memory_space=pl.ANY))]
     body = functools.partial(earliest_kernel, True)

time: 54.7 us -> 48.4 us (0.88)
  Pallas kernels: 16.3 us -> 9.24 us
  waiting for transfers between devices: 11 us -> 17.4 us
  local copies, waits for them, and re-layouts: 7.02 us -> 2.96 us
  starting transfers between devices: 19.8 us -> 18.2 us
    ppermute x5, waiting for transfers between devices: 4.2 us -> 15.4 us  [shift(): return lax.ppermute(array, 'tm', ring('tm', 1))]
    pallas_call x6, Pallas kernels: 16.2 us -> 9.09 us  [call(): pl.pallas_call(body, grid=(1,), in_specs=[s for _, s in args], out_specs=...]
    ppermute x12, waiting for transfers between devices: 6.79 us -> 2.01 us  [the longest x6 2 us: exchange_rows(): outward = lax.ppermute(outward, 'height', others)]
    unnamed x22 -> x18, local copies, waits for them, and re-layouts: 5 us -> 1.85 us
    ppermute x12, starting transfers between devices: 11 us -> 9.75 us  [the longest x6 8.54 us: exchange_rows(): outward = lax.ppermute(outward, 'height', others)]
    squeeze x4 -> x0, local copies, waits for them, and re-layouts: 0.99 us -> none  [the longest x1 0.96 us: first_section(): edges = (latents[:, 0], latents[:, rows - 1])]
  transfers between devices with their start and end apart: 17 -> 17, of which waited for: 8 -> 5; matrix products, arithmetic and copies ran while one was open for 2% -> 0% of each run, Pallas kernels for 26% -> 17%
where the time goes in v3:
time: 48.4 us; the launch traced here: 48 us
  starting transfers between devices  18.2 us (38%)
  waiting for transfers between devices  17.4 us (36%)
  Pallas kernels  9.24 us (19%)
  local copies, waits for them, and re-layouts  2.96 us (6%)
    ppermute x5, waiting for transfers between devices, shift(): return lax.ppermute(array, 'tm', ring('tm', 1))  15.4 us
    pallas_call x6, Pallas kernels, call(): pl.pallas_call(body, grid=(1,), in_specs=[s for _, s in args], out_specs=...  9.09 us
    ppermute x6, starting transfers between devices, exchange_rows(): outward = lax.ppermute(outward, 'height', others)  8.54 us
    ppermute x5, starting transfers between devices, shift(): return lax.ppermute(array, 'tm', ring('tm', 1))  8.41 us
    ppermute x6, waiting for transfers between devices, exchange_rows(): outward = lax.ppermute(outward, 'height', others)  2 us
    unnamed x18, local copies, waits for them, and re-layouts  1.85 us
    ppermute x6, starting transfers between devices, exchange_rows(): return (lax.ppermute(inward, 'height', pairs), outward)  1.22 us
    slice x1, local copies, waits for them, and re-layouts, first_section(): before = shift(latents[1:])  1.11 us
  transfers between devices with their start and end apart: 17, of which 5 were waited for; matrix products, arithmetic and copies ran while one was open for 0% of the time, Pallas kernels for 17%

profile of v3, /device:TPU:0, one launch (start us, length us, event | category | flops | bytes accessed | tf_op | source)
XLA Modules:
  0.0 48.0 jit_solution(14727783858487975613)
XLA Ops:
  0.0 0.0 copy-start.1
  0.0 1.1 %slice.3 = bf16[1,8,104,256]{3,2,1,0:T(8,128)(2,1)S(1)} slice(bf16[2,8,104,256]{3,2,1,0:T(8,128)(2,1)} %refs_8_.1), slice={[1:2], [0:8], [0:104], [0:256]} | slice | bytes 851968 | tf_op jit(solution)/shard_map/slice | solution.py:296
  1.1 3.0 %collective-permute-start.2 = (bf16[1,8,104,256]{3,2,1,0:T(8,128)(2,1)S(1)}, bf16[1,8,104,256]{3,2,1,0:T(8,128)(2,1)S(1)}, u32[]{:S(2)}, u32[]{:S(2)}) collective-permute-start(bf16[1,8,104,256]{3,2,1,0:T(8,128)(2,1)S(1)} %slice.3), channel_id=1, source_target_pairs={{0,4},{4,8},{8,12},{12,16},{16,20},{20,24},{24,28},{28,0},{1,5},{5... | collective-permute-start | bytes 1277960 | tf_op jit(solution)/shard_map/ppermute | solution.py:227
  4.1 0.0 copy-start
  4.1 1.2 %copy-done = bf16[2,8,104,256]{3,2,1,0:T(8,128)(2,1)S(1)} copy-done((bf16[2,8,104,256]{3,2,1,0:T(8,128)(2,1)S(1)}, bf16[2,8,104,256]{3,2,1,0:T(8,128)(2,1)}, u32[]{:S(2)}) %copy-start) | copy-done | bytes 851992
  5.3 0.0 copy-start.4
  5.3 0.7 %copy-done.4 = bf16[256]{0:T(256)(128)(2,1)S(1)} copy-done((bf16[256]{0:T(256)(128)(2,1)S(1)}, bf16[256]{0:T(256)(128)(2,1)}, u32[]{:S(2)}) %copy-start.4) | copy-done | bytes 536
  5.9 0.0 copy-start.3
  5.9 0.0 copy-start.5
  6.0 0.1 collective-permute-start
  6.0 1.6 %collective-permute-start.5 = (bf16[2,104,256]{2,1,0:T(8,128)(2,1)S(1)}, bf16[2,104,256]{2,1,0:T(8,128)(2,1)S(1)}, u32[]{:S(2)}, u32[]{:S(2)}) collective-permute-start(bf16[2,104,256]{2,1,0:T(8,128)(2,1)S(1)} %get-tuple-element.32), channel_id=1, source_target_pairs={{0,3},{1,2},{2,1},{3,0},{4,7},{5,6},{6,5},{7,4},{8,11},{9,10},{10,... | collective-permute-start | bytes 319496 | tf_op jit(solution)/shard_map/ppermute | solution.py:218
  7.7 0.0 collective-permute-done.refs_1_.refs_2_.up
  7.7 1.6 %collective-permute-start.1 = (bf16[1,8,104,256]{3,2,1,0:T(8,128)(2,1)S(1)}, bf16[1,8,104,256]{3,2,1,0:T(8,128)(2,1)S(1)}, u32[]{:S(2)}, u32[]{:S(2)}) collective-permute-start(bf16[1,8,104,256]{3,2,1,0:T(8,128)(2,1)S(1)} %first.1), channel_id=1, source_target_pairs={{0,4},{4,8},{8,12},{12,16},{16,20},{20,24},{24,28},{28,0},{1,5},{5... | collective-permute-start | bytes 1277960 | tf_op jit(solution)/shard_map/ppermute | solution.py:227
  9.3 8.5 %collective-permute-done.2.refs_0_.refs_1_ = bf16[1,8,104,256]{3,2,1,0:T(8,128)(2,1)S(1)} collective-permute-done((bf16[1,8,104,256]{3,2,1,0:T(8,128)(2,1)S(1)}, bf16[1,8,104,256]{3,2,1,0:T(8,128)(2,1)S(1)}, u32[]{:S(2)}, u32[]{:S(2)}) %collective-permute-start.2) | collective-permute-done | bytes 426016 | tf_op jit(solution)/shard_map/ppermute | solution.py:227
  17.8 0.1 collective-permute-start.3
  17.9 1.9 %collective-permute-start.4 = (bf16[1,104,256]{2,1,0:T(8,128)(2,1)S(1)}, bf16[1,104,256]{2,1,0:T(8,128)(2,1)S(1)}, u32[]{:S(2)}, u32[]{:S(2)}) collective-permute-start(bf16[1,104,256]{2,1,0:T(8,128)(2,1)S(1)} %get-tuple-element.31), channel_id=1, source_target_pairs={{0,3},{1,2},{2,1},{3,0},{4,7},{5,6},{6,5},{7,4},{8,11},{9,10},{10,... | collective-permute-start | bytes 159752 | tf_op jit(solution)/shard_map/ppermute | solution.py:218
  19.7 0.0 collective-permute-done.5.down
  19.7 0.0 copy-done.1
  19.8 0.0 copy-done.3
  19.8 0.0 copy-done.5
  19.8 0.0 copy-start.8
  19.8 3.5 %own.2 = (f32[832,256]{1,0:T(8,128)S(1)}, f32[832,256]{1,0:T(8,128)S(1)}) custom-call(bf16[2,8,104,256]{3,2,1,0:T(8,128)(2,1)S(1)} %copy-done.1, bf16[2,8,104,256]{3,2,1,0:T(8,128)(2,1)S(1)} %copy-done.1, bf16[2,104,256]{2,1,0:T(8,128)(2,1)S(1)} %collective-permute-done.refs_1_.refs_2_.up, bf16[2,104,256]{2,1,0:T(8,128)(2,1)S(1)} %collective-permute-done.5.down, ...), custom_call_target="tpu_custom_call" | custom-call | flops 2944401408 | bytes 6291456 | tf_op jit(solution)/shard_map/own/pallas_call | solution.py:194
  23.2 0.0 collective-permute-done.3.refs_1_
  23.3 0.0 collective-permute-done.4.refs_2_
  23.3 0.0 copy-done.8
  23.3 0.1 before.2
  23.4 0.0 copy-start.2
  23.4 0.0 copy-start.6
  23.4 1.2 %collective-permute-start.12 = (bf16[1,8,104,256]{3,2,1,0:T(8,128)(2,1)S(1)}, bf16[1,8,104,256]{3,2,1,0:T(8,128)(2,1)S(1)}, u32[]{:S(2)}, u32[]{:S(2)}) collective-permute-start(bf16[1,8,104,256]{3,2,1,0:T(8,128)(2,1)S(1)} %get-tuple-element.35.refs_2_.last_ref), channel_id=1, source_target_pairs={{0,4},{4,8},{8,12},{12,16},{16,20},{20,24},{24,28},{28,0},{1,5},{5... | collective-permute-start | bytes 1277960 | tf_op jit(solution)/shard_map/ppermute | solution.py:227
  24.7 1.4 %collective-permute-done.1.refs_0_.refs_1_ = bf16[1,8,104,256]{3,2,1,0:T(8,128)(2,1)S(1)} collective-permute-done((bf16[1,8,104,256]{3,2,1,0:T(8,128)(2,1)S(1)}, bf16[1,8,104,256]{3,2,1,0:T(8,128)(2,1)S(1)}, u32[]{:S(2)}, u32[]{:S(2)}) %collective-permute-start.1) | collective-permute-done | bytes 426016 | tf_op jit(solution)/shard_map/ppermute | solution.py:227
  26.1 0.1 collective-permute-start.6
  26.2 1.6 %collective-permute-start.7 = (bf16[1,104,256]{2,1,0:T(8,128)(2,1)S(1)}, bf16[1,104,256]{2,1,0:T(8,128)(2,1)S(1)}, u32[]{:S(2)}, u32[]{:S(2)}) collective-permute-start(bf16[1,104,256]{2,1,0:T(8,128)(2,1)S(1)} %get-tuple-element.37), channel_id=1, source_target_pairs={{0,3},{1,2},{2,1},{3,0},{4,7},{5,6},{6,5},{7,4},{8,11},{9,10},{10,... | collective-permute-start | bytes 159752 | tf_op jit(solution)/shard_map/ppermute | solution.py:218
  27.8 0.0 collective-permute-done.6.refs_1_
  27.8 2.0 %collective-permute-done.7.refs_2_ = bf16[1,104,256]{2,1,0:T(8,128)(2,1)S(1)} collective-permute-done((bf16[1,104,256]{2,1,0:T(8,128)(2,1)S(1)}, bf16[1,104,256]{2,1,0:T(8,128)(2,1)S(1)}, u32[]{:S(2)}, u32[]{:S(2)}) %collective-permute-start.7) | collective-permute-done | bytes 53280 | tf_op jit(solution)/shard_map/ppermute | solution.py:218
  29.8 0.1 earliest.2
  29.9 0.8 %collective-permute-start.10 = (bf16[2,104,256]{2,1,0:T(8,128)(2,1)S(1)}, bf16[2,104,256]{2,1,0:T(8,128)(2,1)S(1)}, u32[]{:S(2)}, u32[]{:S(2)}) collective-permute-start(bf16[2,104,256]{2,1,0:T(8,128)(2,1)S(1)} %get-tuple-element.43), channel_id=1, source_target_pairs={{0,1},{1,0},{2,3},{3,2},{4,5},{5,4},{6,7},{7,6},{8,9},{9,8},{10,11... | collective-permute-start | bytes 319496 | tf_op jit(solution)/shard_map/ppermute | solution.py:219
  30.7 1.2 %collective-permute-start.11 = (bf16[2,104,256]{2,1,0:T(8,128)(2,1)S(1)}, bf16[2,104,256]{2,1,0:T(8,128)(2,1)S(1)}, u32[]{:S(2)}, u32[]{:S(2)}) collective-permute-start(bf16[2,104,256]{2,1,0:T(8,128)(2,1)S(1)} %get-tuple-element.44), channel_id=1, source_target_pairs={{0,3},{1,2},{2,1},{3,0},{4,7},{5,6},{6,5},{7,4},{8,11},{9,10},{10,... | collective-permute-start | bytes 319496 | tf_op jit(solution)/shard_map/ppermute | solution.py:218
  32.0 1.4 %collective-permute-start.9 = (bf16[2,1,104,256]{3,2,1,0:T(8,128)(2,1)S(1)}, bf16[2,1,104,256]{3,2,1,0:T(8,128)(2,1)S(1)}, u32[]{:S(2)}, u32[]{:S(2)}) collective-permute-start(bf16[2,1,104,256]{3,2,1,0:T(8,128)(2,1)S(1)} %get-tuple-element.40.refs_0_.refs_1_.refs_4_), channel_id=1, source_target_pairs={{0,4},{4,8},{8,12},{12,16},{16,20},{20,24},{24,28},{28,0},{1,5},{5... | collective-permute-start | bytes 319496 | tf_op jit(solution)/shard_map/ppermute | solution.py:227
  33.4 1.1 %collective-permute-start.8 = (bf16[1,6,104,256]{3,2,1,0:T(8,128)(2,1)S(1)}, bf16[1,6,104,256]{3,2,1,0:T(8,128)(2,1)S(1)}, u32[]{:S(2)}, u32[]{:S(2)}) collective-permute-start(bf16[1,6,104,256]{3,2,1,0:T(8,128)(2,1)S(1)} %get-tuple-element.39), channel_id=1, source_target_pairs={{0,4},{4,8},{8,12},{12,16},{16,20},{20,24},{24,28},{28,0},{1,5},{5... | collective-permute-start | bytes 958472 | tf_op jit(solution)/shard_map/ppermute | solution.py:227
  34.5 0.0 collective-permute-done.10.refs_2_.up
  34.5 3.7 %collective-permute-done.12.refs_0_.refs_1_ = bf16[1,8,104,256]{3,2,1,0:T(8,128)(2,1)S(1)} collective-permute-done((bf16[1,8,104,256]{3,2,1,0:T(8,128)(2,1)S(1)}, bf16[1,8,104,256]{3,2,1,0:T(8,128)(2,1)S(1)}, u32[]{:S(2)}, u32[]{:S(2)}) %collective-permute-start.12) | collective-permute-done | bytes 426016 | tf_op jit(solution)/shard_map/ppermute | solution.py:227
  38.2 0.1 collective-permute-start.15
  38.3 0.9 %collective-permute-start.16 = (bf16[1,104,256]{2,1,0:T(8,128)(2,1)S(1)}, bf16[1,104,256]{2,1,0:T(8,128)(2,1)S(1)}, u32[]{:S(2)}, u32[]{:S(2)}) collective-permute-start(bf16[1,104,256]{2,1,0:T(8,128)(2,1)S(1)} %get-tuple-element.49), channel_id=1, source_target_pairs={{0,3},{1,2},{2,1},{3,0},{4,7},{5,6},{6,5},{7,4},{8,11},{9,10},{10,... | collective-permute-start | bytes 159752 | tf_op jit(solution)/shard_map/ppermute | solution.py:218
  39.2 0.0 collective-permute-done.11.down
  39.2 0.0 copy-done.2
  39.2 0.0 copy-done.6
  39.2 0.0 copy-start.7
  39.2 3.5 %own.3 = (f32[832,256]{1,0:T(8,128)S(1)}, f32[832,256]{1,0:T(8,128)S(1)}) custom-call(bf16[1,8,104,256]{3,2,1,0:T(8,128)(2,1)S(1)} %get-tuple-element.35.refs_2_.last_ref, bf16[1,8,104,256]{3,2,1,0:T(8,128)(2,1)S(1)} %get-tuple-element.41.first_ref, bf16[2,104,256]{2,1,0:T(8,128)(2,1)S(1)} %collective-permute-done.10.refs_2_.up, ...), custom_call_target="tpu_custom_call" | custom-call | flops 2944401408 | bytes 6291456 | tf_op jit(solution)/shard_map/own/pallas_call | solution.py:194
  42.7 0.0 collective-permute-done.9.refs_0_.refs_1_
  42.7 0.1 collective-permute-start.13
  42.9 1.3 %collective-permute-start.14 = (bf16[1,104,256]{2,1,0:T(8,128)(2,1)S(1)}, bf16[1,104,256]{2,1,0:T(8,128)(2,1)S(1)}, u32[]{:S(2)}, u32[]{:S(2)}) collective-permute-start(bf16[1,104,256]{2,1,0:T(8,128)(2,1)S(1)} %get-tuple-element.48), channel_id=1, source_target_pairs={{0,3},{1,2},{2,1},{3,0},{4,7},{5,6},{6,5},{7,4},{8,11},{9,10},{10,... | collective-permute-start | bytes 159752 | tf_op jit(solution)/shard_map/ppermute | solution.py:218
  44.1 0.0 collective-permute-done.15.refs_1_
  44.1 0.0 collective-permute-done.16.refs_2_
  44.2 0.0 copy-done.7
  44.2 1.1 %before.3 = (bf16[2,8,104,256]{3,2,1,0:T(8,128)(2,1)}, f32[832,256]{1,0:T(8,128)S(1)}) custom-call(bf16[1,8,104,256]{3,2,1,0:T(8,128)(2,1)S(1)} %collective-permute-done.12.refs_0_.refs_1_, bf16[1,104,256]{2,1,0:T(8,128)(2,1)S(1)} %collective-permute-done.15.refs_1_, bf16[1,104,256]{2,1,0:T(8,128)(2,1)S(1)} %collective-permute-done.16.refs_2_, ...), custom_call_target="tpu_custom_call" | custom-call | flops 1962934272 | bytes 4194304 | tf_op jit(solution)/shard_map/before/pallas_call | solution.py:194
  45.3 1.8 %collective-permute-done.8.refs_0_ = bf16[1,6,104,256]{3,2,1,0:T(8,128)(2,1)S(1)} collective-permute-done((bf16[1,6,104,256]{3,2,1,0:T(8,128)(2,1)S(1)}, bf16[1,6,104,256]{3,2,1,0:T(8,128)(2,1)S(1)}, u32[]{:S(2)}, u32[]{:S(2)}) %collective-permute-start.8) | collective-permute-done | bytes 319520 | tf_op jit(solution)/shard_map/ppermute | solution.py:227
  47.1 0.0 collective-permute-done.13.refs_2_
  47.1 0.0 collective-permute-done.14.refs_3_
  47.1 0.9 %earliest.3 = bf16[2,8,104,256]{3,2,1,0:T(8,128)(2,1)} custom-call(bf16[1,6,104,256]{3,2,1,0:T(8,128)(2,1)S(1)} %collective-permute-done.8.refs_0_, bf16[2,1,104,256]{3,2,1,0:T(8,128)(2,1)S(1)} %collective-permute-done.9.refs_0_.refs_1_, bf16[1,104,256]{2,1,0:T(8,128)(2,1)S(1)} %collective-permute-done.13.refs_2_, ...), custom_call_target="tpu_custom_call", output_to_operand_aliasing={{}: (9, {})} | custom-call | flops 981467136 | bytes 2097152 | tf_op jit(solution)/shard_map/earliest/pallas_call | solution.py:194
  (7 shorter events, 0.1 us)
Async XLA Ops:
  0.0 19.7 %copy-start.1 = (bf16[2,8,104,256]{3,2,1,0:T(8,128)(2,1)S(1)}, bf16[2,8,104,256]{3,2,1,0:T(8,128)(2,1)}, u32[]{:S(2)}) copy-start(bf16[2,8,104,256]{3,2,1,0:T(8,128)(2,1)} %refs_8_.1) | copy-start | bytes 2555908
  1.1 16.7 %collective-permute-start.2 = (bf16[1,8,104,256]{3,2,1,0:T(8,128)(2,1)S(1)}, bf16[1,8,104,256]{3,2,1,0:T(8,128)(2,1)S(1)}, u32[]{:S(2)}, u32[]{:S(2)}) collective-permute-start(bf16[1,8,104,256]{3,2,1,0:T(8,128)(2,1)S(1)} %slice.3), channel_id=1, source_target_pairs={{0,4},{4,8},{8,12},{12,16},{16,20},{20,24},{24,28},{28,0},{1,5},{5... | collective-permute-start | bytes 1277960 | tf_op jit(solution)/shard_map/ppermute | solution.py:227
  4.1 1.2 %copy-start = (bf16[2,8,104,256]{3,2,1,0:T(8,128)(2,1)S(1)}, bf16[2,8,104,256]{3,2,1,0:T(8,128)(2,1)}, u32[]{:S(2)}) copy-start(bf16[2,8,104,256]{3,2,1,0:T(8,128)(2,1)} %refs_8_.1) | copy-start | bytes 2555908
  5.3 0.7 %copy-start.4 = (bf16[256]{0:T(256)(128)(2,1)S(1)}, bf16[256]{0:T(256)(128)(2,1)}, u32[]{:S(2)}) copy-start(bf16[256]{0:T(256)(128)(2,1)} %refs_3_.6) | copy-start | bytes 1540
  5.9 13.8 %copy-start.3 = (bf16[3,3,3,256,256]{4,3,2,1,0:T(8,128)(2,1)S(1)}, bf16[3,3,3,256,256]{4,3,2,1,0:T(8,128)(2,1)}, u32[]{:S(2)}) copy-start(bf16[3,3,3,256,256]{4,3,2,1,0:T(8,128)(2,1)} %param.9) | copy-start | bytes 10616836
  5.9 13.8 %copy-start.5 = (bf16[256]{0:T(256)(128)(2,1)S(1)}, bf16[256]{0:T(256)(128)(2,1)}, u32[]{:S(2)}) copy-start(bf16[256]{0:T(256)(128)(2,1)} %refs_3_.6) | copy-start | bytes 1540
  6.0 1.7 %collective-permute-start = (bf16[2,104,256]{2,1,0:T(8,128)(2,1)S(1)}, bf16[2,104,256]{2,1,0:T(8,128)(2,1)S(1)}, u32[]{:S(2)}, u32[]{:S(2)}) collective-permute-start(bf16[2,104,256]{2,1,0:T(8,128)(2,1)S(1)} %get-tuple-element.29), channel_id=1, source_target_pairs={{0,1},{1,0},{2,3},{3,2},{4,5},{5,4},{6,7},{7,6},{8,9},{9,8},{10,11... | collective-permute-start | bytes 319496 | tf_op jit(solution)/shard_map/ppermute | solution.py:219
  6.0 13.7 %collective-permute-start.5 = (bf16[2,104,256]{2,1,0:T(8,128)(2,1)S(1)}, bf16[2,104,256]{2,1,0:T(8,128)(2,1)S(1)}, u32[]{:S(2)}, u32[]{:S(2)}) collective-permute-start(bf16[2,104,256]{2,1,0:T(8,128)(2,1)S(1)} %get-tuple-element.32), channel_id=1, source_target_pairs={{0,3},{1,2},{2,1},{3,0},{4,7},{5,6},{6,5},{7,4},{8,11},{9,10},{10,... | collective-permute-start | bytes 319496 | tf_op jit(solution)/shard_map/ppermute | solution.py:218
  7.7 18.4 %collective-permute-start.1 = (bf16[1,8,104,256]{3,2,1,0:T(8,128)(2,1)S(1)}, bf16[1,8,104,256]{3,2,1,0:T(8,128)(2,1)S(1)}, u32[]{:S(2)}, u32[]{:S(2)}) collective-permute-start(bf16[1,8,104,256]{3,2,1,0:T(8,128)(2,1)S(1)} %first.1), channel_id=1, source_target_pairs={{0,4},{4,8},{8,12},{12,16},{16,20},{20,24},{24,28},{28,0},{1,5},{5... | collective-permute-start | bytes 1277960 | tf_op jit(solution)/shard_map/ppermute | solution.py:227
  17.8 5.4 %collective-permute-start.3 = (bf16[1,104,256]{2,1,0:T(8,128)(2,1)S(1)}, bf16[1,104,256]{2,1,0:T(8,128)(2,1)S(1)}, u32[]{:S(2)}, u32[]{:S(2)}) collective-permute-start(bf16[1,104,256]{2,1,0:T(8,128)(2,1)S(1)} %get-tuple-element.30._), channel_id=1, source_target_pairs={{0,1},{1,0},{2,3},{3,2},{4,5},{5,4},{6,7},{7,6},{8,9},{9,8},{10,11... | collective-permute-start | bytes 159752 | tf_op jit(solution)/shard_map/ppermute | solution.py:219
  17.9 5.4 %collective-permute-start.4 = (bf16[1,104,256]{2,1,0:T(8,128)(2,1)S(1)}, bf16[1,104,256]{2,1,0:T(8,128)(2,1)S(1)}, u32[]{:S(2)}, u32[]{:S(2)}) collective-permute-start(bf16[1,104,256]{2,1,0:T(8,128)(2,1)S(1)} %get-tuple-element.31), channel_id=1, source_target_pairs={{0,3},{1,2},{2,1},{3,0},{4,7},{5,6},{6,5},{7,4},{8,11},{9,10},{10,... | collective-permute-start | bytes 159752 | tf_op jit(solution)/shard_map/ppermute | solution.py:218
  19.8 3.5 %copy-start.8 = (bf16[256]{0:T(256)(128)(2,1)S(1)}, bf16[256]{0:T(256)(128)(2,1)}, u32[]{:S(2)}) copy-start(bf16[256]{0:T(256)(128)(2,1)} %refs_5_.1) | copy-start | bytes 1540
  23.4 15.8 %copy-start.2 = (bf16[3,3,3,256,256]{4,3,2,1,0:T(8,128)(2,1)S(1)}, bf16[3,3,3,256,256]{4,3,2,1,0:T(8,128)(2,1)}, u32[]{:S(2)}) copy-start(bf16[3,3,3,256,256]{4,3,2,1,0:T(8,128)(2,1)} %param.12) | copy-start | bytes 10616836
  23.4 15.8 %copy-start.6 = (bf16[256]{0:T(256)(128)(2,1)S(1)}, bf16[256]{0:T(256)(128)(2,1)}, u32[]{:S(2)}) copy-start(bf16[256]{0:T(256)(128)(2,1)} %refs_4_.3) | copy-start | bytes 1540
  23.4 14.8 %collective-permute-start.12 = (bf16[1,8,104,256]{3,2,1,0:T(8,128)(2,1)S(1)}, bf16[1,8,104,256]{3,2,1,0:T(8,128)(2,1)S(1)}, u32[]{:S(2)}, u32[]{:S(2)}) collective-permute-start(bf16[1,8,104,256]{3,2,1,0:T(8,128)(2,1)S(1)} %get-tuple-element.35.refs_2_.last_ref), channel_id=1, source_target_pairs={{0,4},{4,8},{8,12},{12,16},{16,20},{20,24},{24,28},{28,0},{1,5},{5... | collective-permute-start | bytes 1277960 | tf_op jit(solution)/shard_map/ppermute | solution.py:227
  26.1 1.7 %collective-permute-start.6 = (bf16[1,104,256]{2,1,0:T(8,128)(2,1)S(1)}, bf16[1,104,256]{2,1,0:T(8,128)(2,1)S(1)}, u32[]{:S(2)}, u32[]{:S(2)}) collective-permute-start(bf16[1,104,256]{2,1,0:T(8,128)(2,1)S(1)} %get-tuple-element.36), channel_id=1, source_target_pairs={{0,1},{1,0},{2,3},{3,2},{4,5},{5,4},{6,7},{7,6},{8,9},{9,8},{10,11... | collective-permute-start | bytes 159752 | tf_op jit(solution)/shard_map/ppermute | solution.py:219
  26.2 3.6 %collective-permute-start.7 = (bf16[1,104,256]{2,1,0:T(8,128)(2,1)S(1)}, bf16[1,104,256]{2,1,0:T(8,128)(2,1)S(1)}, u32[]{:S(2)}, u32[]{:S(2)}) collective-permute-start(bf16[1,104,256]{2,1,0:T(8,128)(2,1)S(1)} %get-tuple-element.37), channel_id=1, source_target_pairs={{0,3},{1,2},{2,1},{3,0},{4,7},{5,6},{6,5},{7,4},{8,11},{9,10},{10,... | collective-permute-start | bytes 159752 | tf_op jit(solution)/shard_map/ppermute | solution.py:218
  29.9 4.6 %collective-permute-start.10 = (bf16[2,104,256]{2,1,0:T(8,128)(2,1)S(1)}, bf16[2,104,256]{2,1,0:T(8,128)(2,1)S(1)}, u32[]{:S(2)}, u32[]{:S(2)}) collective-permute-start(bf16[2,104,256]{2,1,0:T(8,128)(2,1)S(1)} %get-tuple-element.43), channel_id=1, source_target_pairs={{0,1},{1,0},{2,3},{3,2},{4,5},{5,4},{6,7},{7,6},{8,9},{9,8},{10,11... | collective-permute-start | bytes 319496 | tf_op jit(solution)/shard_map/ppermute | solution.py:219
  30.7 8.5 %collective-permute-start.11 = (bf16[2,104,256]{2,1,0:T(8,128)(2,1)S(1)}, bf16[2,104,256]{2,1,0:T(8,128)(2,1)S(1)}, u32[]{:S(2)}, u32[]{:S(2)}) collective-permute-start(bf16[2,104,256]{2,1,0:T(8,128)(2,1)S(1)} %get-tuple-element.44), channel_id=1, source_target_pairs={{0,3},{1,2},{2,1},{3,0},{4,7},{5,6},{6,5},{7,4},{8,11},{9,10},{10,... | collective-permute-start | bytes 319496 | tf_op jit(solution)/shard_map/ppermute | solution.py:218
  32.0 10.7 %collective-permute-start.9 = (bf16[2,1,104,256]{3,2,1,0:T(8,128)(2,1)S(1)}, bf16[2,1,104,256]{3,2,1,0:T(8,128)(2,1)S(1)}, u32[]{:S(2)}, u32[]{:S(2)}) collective-permute-start(bf16[2,1,104,256]{3,2,1,0:T(8,128)(2,1)S(1)} %get-tuple-element.40.refs_0_.refs_1_.refs_4_), channel_id=1, source_target_pairs={{0,4},{4,8},{8,12},{12,16},{16,20},{20,24},{24,28},{28,0},{1,5},{5... | collective-permute-start | bytes 319496 | tf_op jit(solution)/shard_map/ppermute | solution.py:227
  33.4 13.7 %collective-permute-start.8 = (bf16[1,6,104,256]{3,2,1,0:T(8,128)(2,1)S(1)}, bf16[1,6,104,256]{3,2,1,0:T(8,128)(2,1)S(1)}, u32[]{:S(2)}, u32[]{:S(2)}) collective-permute-start(bf16[1,6,104,256]{3,2,1,0:T(8,128)(2,1)S(1)} %get-tuple-element.39), channel_id=1, source_target_pairs={{0,4},{4,8},{8,12},{12,16},{16,20},{20,24},{24,28},{28,0},{1,5},{5... | collective-permute-start | bytes 958472 | tf_op jit(solution)/shard_map/ppermute | solution.py:227
  38.2 5.9 %collective-permute-start.15 = (bf16[1,104,256]{2,1,0:T(8,128)(2,1)S(1)}, bf16[1,104,256]{2,1,0:T(8,128)(2,1)S(1)}, u32[]{:S(2)}, u32[]{:S(2)}) collective-permute-start(bf16[1,104,256]{2,1,0:T(8,128)(2,1)S(1)} %get-tuple-element.45._), channel_id=1, source_target_pairs={{0,1},{1,0},{2,3},{3,2},{4,5},{5,4},{6,7},{7,6},{8,9},{9,8},{10,11... | collective-permute-start | bytes 159752 | tf_op jit(solution)/shard_map/ppermute | solution.py:219
  38.3 5.9 %collective-permute-start.16 = (bf16[1,104,256]{2,1,0:T(8,128)(2,1)S(1)}, bf16[1,104,256]{2,1,0:T(8,128)(2,1)S(1)}, u32[]{:S(2)}, u32[]{:S(2)}) collective-permute-start(bf16[1,104,256]{2,1,0:T(8,128)(2,1)S(1)} %get-tuple-element.49), channel_id=1, source_target_pairs={{0,3},{1,2},{2,1},{3,0},{4,7},{5,6},{6,5},{7,4},{8,11},{9,10},{10,... | collective-permute-start | bytes 159752 | tf_op jit(solution)/shard_map/ppermute | solution.py:218
  39.2 4.9 %copy-start.7 = (bf16[256]{0:T(256)(128)(2,1)S(1)}, bf16[256]{0:T(256)(128)(2,1)}, u32[]{:S(2)}) copy-start(bf16[256]{0:T(256)(128)(2,1)} %refs_6_.5) | copy-start | bytes 1540
  42.7 4.4 %collective-permute-start.13 = (bf16[1,104,256]{2,1,0:T(8,128)(2,1)S(1)}, bf16[1,104,256]{2,1,0:T(8,128)(2,1)S(1)}, u32[]{:S(2)}, u32[]{:S(2)}) collective-permute-start(bf16[1,104,256]{2,1,0:T(8,128)(2,1)S(1)} %get-tuple-element.47), channel_id=1, source_target_pairs={{0,1},{1,0},{2,3},{3,2},{4,5},{5,4},{6,7},{7,6},{8,9},{9,8},{10,11... | collective-permute-start | bytes 159752 | tf_op jit(solution)/shard_map/ppermute | solution.py:219
  42.9 4.2 %collective-permute-start.14 = (bf16[1,104,256]{2,1,0:T(8,128)(2,1)S(1)}, bf16[1,104,256]{2,1,0:T(8,128)(2,1)S(1)}, u32[]{:S(2)}, u32[]{:S(2)}) collective-permute-start(bf16[1,104,256]{2,1,0:T(8,128)(2,1)S(1)} %get-tuple-element.48), channel_id=1, source_target_pairs={{0,3},{1,2},{2,1},{3,0},{4,7},{5,6},{6,5},{7,4},{8,11},{9,10},{10,... | collective-permute-start | bytes 159752 | tf_op jit(solution)/shard_map/ppermute | solution.py:218

commit v4 on v3

v4 whole, which is shorter than its diff:
```python
import functools

import jax
import jax.numpy as jnp
from jax import lax
from jax.experimental import pallas as pl
from jax.experimental.pallas import tpu as pltpu
from jax.sharding import PartitionSpec as P

EPSILON = 1e-06
BF16, F32 = jnp.bfloat16, jnp.float32
VMEM_LIMIT = 26 * 2**20


def ring(axis, step):
    peers = lax.axis_size(axis)
    return [(i, (i + step) % peers) for i in range(peers)]


def activate_rows(get_row, gain, shifts, rows, cells):
    for r in range(rows):
        values, mask = get_row(r)
        here = slice(r * cells, (r + 1) * cells)
        values = values.astype(F32)
        mean_power = jnp.mean(values * values, axis=-1, keepdims=True)
        normed = values * lax.rsqrt(mean_power + EPSILON) * gain
        act = normed / (1.0 + jnp.exp(-normed))
        if mask is not None:
            act = act * mask
        cell = lax.broadcasted_iota(jnp.int32, act.shape, 0)
        shifts[0, here, :] = jnp.where(cell == 0, 0.0, pltpu.roll(act, 1, 0))
        shifts[1, here, :] = act
        shifts[2, here, :] = jnp.where(cell == cells - 1, 0.0, pltpu.roll(act, cells - 1, 0))


def pack(shifts, even, odd, rows, cells):
    channels = shifts.shape[-1]
    pair = 2 * cells
    for buf, first, count in ((even, 0, rows // 2), (odd, cells, rows // 2 - 1)):
        for k in range(count):
            for l in range(3):
                buf[k * pair : (k + 1) * pair, l * channels : (l + 1) * channels] = shifts[
                    l, first + k * pair : first + (k + 1) * pair, :
                ].astype(BF16)


def taps(even, odd, kernel, start, length, cells):
    dot = functools.partial(jnp.dot, preferred_element_type=F32)
    lower = 2 * cells + start
    return (
        dot(even[start : start + length], kernel[0, 0])
        + dot(odd[start : start + length], kernel[0, 1])
        + dot(even[lower : lower + length], kernel[0, 2])
    )


def masks():
    row_id, rows = lax.axis_index("height"), lax.axis_size("height")
    above = (row_id > 0).astype(F32)
    below = (row_id < rows - 1).astype(F32)
    return above, below


def load_frame(frame, inward, outward, gain, bufs, edges=None):
    shifts, even, odd = bufs
    rows, cells = frame.shape[0], frame.shape[1]
    if edges is not None:
        rows += 2
    above, below = masks()

    lower = lax.axis_index("height") % 2 == 0

    def get_row(r):
        if r == 0:
            return jnp.where(lower, outward, inward), above
        if r == rows + 1:
            return jnp.where(lower, inward, outward), below
        if edges is None:
            return frame[r - 1], None
        if r in (1, rows):
            return edges[0 if r == 1 else 1], None
        return frame[r - 2], None

    activate_rows(get_row, gain[...].astype(F32)[None], shifts, rows + 2, cells)
    pack(shifts, even, odd, rows + 2, cells)


def chunks(rows, cells, fine=False):
    step = 4 * cells if rows % 4 == 0 and not fine else 2 * cells
    return [(s, step) for s in range(0, rows * cells, step)]


def own_kernel(last, first, up, down, gain, k1, k2, _, acc_first, acc_last, *bufs):
    rows, cells = last.shape[1], last.shape[2]
    even, odd = bufs[1:]
    load_frame(last.at[0], up[1], down[1], gain, bufs)
    for s, n in chunks(rows, cells):
        acc_last[s : s + n] = taps(even, odd, k2, s, n, cells)
    load_frame(first.at[0], up[0], down[0], gain, bufs)
    for s, n in chunks(rows, cells):
        acc_last[s : s + n] += taps(even, odd, k1, s, n, cells)
        acc_first[s : s + n] = taps(even, odd, k2, s, n, cells)


def own_last_kernel(last, up, down, gain, k2, _, acc_last, *bufs):
    rows, cells = last.shape[1], last.shape[2]
    even, odd = bufs[1:]
    load_frame(last.at[0], up[0], down[0], gain, bufs)
    for s, n in chunks(rows, cells):
        acc_last[s : s + n] = taps(even, odd, k2, s, n, cells)


def own_first_kernel(first, up, down, gain, k1, k2, acc_in, _, acc_first, acc_last, *bufs):
    rows, cells = first.shape[1], first.shape[2]
    even, odd = bufs[1:]
    load_frame(first.at[0], up[0], down[0], gain, bufs)
    for s, n in chunks(rows, cells):
        acc_last[s : s + n] = acc_in[s : s + n] + taps(even, odd, k1, s, n, cells)
        acc_first[s : s + n] = taps(even, odd, k2, s, n, cells)


def finish(total, bias, s, n, cells):
    value = (total + bias[...].astype(F32)[None]).reshape(n // cells, cells, -1)
    return slice(s // cells, (s + n) // cells), value


class Result:
    def __init__(self, latents, out, frame, rows, sems):
        self.residual, self.out, self.frame, self.rows, self.sems = latents.at[0], out, frame, rows, sems

    def copy(self, s, n, cells):
        r = pl.ds(s // cells, n // cells)
        return pltpu.make_async_copy(
            self.rows.at[r], self.out.at[self.frame, r], self.sems.at[s // n]
        )

    def finish(self, total, bias, s, n, cells):
        r, value = finish(total, bias, s, n, cells)
        self.rows[r] = (self.residual[r].astype(F32) + value).astype(BF16)
        self.copy(s, n, cells).start()

    def wait(self, parts):
        for s, n in parts:
            self.copy(s, n, self.rows.shape[1]).wait()


def frames_before(body):
    first = lax.axis_index("tm") == 0
    pl.when(first)(lambda: body(False))
    pl.when(jnp.logical_not(first))(lambda: body(True))


def before_kernel(residual, *refs):
    if residual:
        frame, up, down, gain, k0, k1, bias, acc_first, acc_last, latents, out, acc_out, *bufs, new, sems = refs
        frame, edges = frame.at[0], None
        result = Result(latents, out, 1, new, sems)
    else:
        frame, edges, up, down, gain, k0, k1, bias, acc_first, acc_last, out, acc_out, *bufs = refs
        frame = frame.at[0]
    cells = up.shape[1]
    rows = acc_first.shape[0] // cells
    even, odd = bufs[1:]

    @frames_before
    def _(there):
        if there:
            load_frame(frame, up[0], down[0], gain, bufs, edges)
        for s, n in chunks(rows, cells):
            total = acc_last[s : s + n]
            if there:
                total = total + taps(even, odd, k0, s, n, cells)
            if residual:
                result.finish(total, bias, s, n, cells)
            else:
                r, value = finish(total, bias, s, n, cells)
                out[0, r] = value.astype(BF16)
        for s, n in chunks(rows, cells):
            total = acc_first[s : s + n]
            if there:
                total = total + taps(even, odd, k1, s, n, cells)
            acc_out[s : s + n] = total

    if residual:
        result.wait(chunks(rows, cells))


def earliest_kernel(residual, *refs):
    if residual:
        frame, edges, up, down, gain, k0, bias, acc_first, latents, _, out, *bufs, new, sems = refs
        result = Result(latents, out, 0, new, sems)
    else:
        frame, edges, up, down, gain, k0, bias, acc_first, out, inner, edges_out, *bufs = refs
    cells = up.shape[1]
    rows = acc_first.shape[0] // cells
    even, odd = bufs[1:]

    @frames_before
    def _(there):
        if there:
            load_frame(frame.at[0], up[0], down[0], gain, bufs, edges)
        for s, n in chunks(rows, cells, residual):
            total = acc_first[s : s + n]
            if there:
                total = total + taps(even, odd, k0, s, n, cells)
            if residual:
                result.finish(total, bias, s, n, cells)
            else:
                r, value = finish(total, bias, s, n, cells)
                out[0, r] = value.astype(BF16)

    if residual:
        result.wait(chunks(rows, cells, True))
    else:
        edges_out[0] = out[0, 0]
        edges_out[1] = out[0, rows - 1]
        inner[0] = out[0, 1 : rows - 1]


def whole(shape):
    return pl.BlockSpec(tuple(shape), lambda i: (0,) * len(shape))


def part(shape, index):
    return pl.BlockSpec((1, *shape[1:]), lambda i: (index,) + (0,) * (len(shape) - 1))


def call(body, name, units, out_specs, out_shape, args, aliases=None, extra=()):
    rows, cells, channels = call.block
    flat = (rows + 2) * cells
    arrays = [a for a, _ in args]
    flops = units * 2 * rows * cells * 9 * channels * channels
    return pl.pallas_call(
        body,
        grid=(1,),
        in_specs=[s for _, s in args],
        out_specs=out_specs,
        out_shape=out_shape,
        scratch_shapes=[
            pltpu.VMEM((3, flat, channels), F32),
            pltpu.VMEM((flat, 3 * channels), BF16),
            pltpu.VMEM((flat - 2 * cells, 3 * channels), BF16),
            *extra,
        ],
        input_output_aliases=aliases or {},
        compiler_params=pltpu.CompilerParams(vmem_limit_bytes=VMEM_LIMIT),
        cost_estimate=pl.CostEstimate(
            flops=flops, bytes_accessed=units * 2**21, transcendentals=2 * flat * channels
        ),
        name=name,
    )(*arrays)


def exchange_rows(inward, outward):
    bands = lax.axis_size("height")
    pairs = [(i, i ^ 1) for i in range(bands)]
    others = [(i, (i + (1 if i % 2 else -1)) % bands) for i in range(bands)]
    outward = lax.ppermute(outward, "height", others)
    return lax.ppermute(inward, "height", pairs), outward


def w(array):
    return array, whole(array.shape)


def shift(array, closed=True):
    route = ring("tm", 1)
    return lax.ppermute(array, "tm", route if closed else route[:-1])


def shapes():
    rows, cells, channels = call.block
    acc = jax.ShapeDtypeStruct((rows * cells, channels), F32)
    frame = jax.ShapeDtypeStruct((1, rows, cells, channels), BF16)
    inner = jax.ShapeDtypeStruct((1, rows - 2, cells, channels), BF16)
    edge = jax.ShapeDtypeStruct((2, cells, channels), BF16)
    return acc, frame, inner, edge


def own(last, first, up, down, gain, k, token):
    acc = shapes()[0]
    args = [last, first, w(up), w(down), gain, k[1], k[2], (token, pl.BlockSpec(memory_space=pl.ANY))]
    return call(own_kernel, "own", 3, [whole(acc.shape)] * 2, [acc, acc], args)


def own_apart(last, first, up, down, gain, k, early, late):
    acc = shapes()[0]
    up, down = pairs(up, 1), pairs(down, 1)
    args = [last, up[1], down[1], gain, k[2], (early, pl.BlockSpec(memory_space=pl.ANY))]
    acc_last = call(own_last_kernel, "last", 1, [whole(acc.shape)], [acc], args)[0]
    args = [first, up[0], down[0], gain, k[1], k[2], w(acc_last), (late, pl.BlockSpec(memory_space=pl.ANY))]
    return call(own_first_kernel, "first", 2, [whole(acc.shape)] * 2, [acc, acc], args)


def inner_rows(latents, token):
    rows = latents.shape[1]
    inner = shapes()[2]

    def copy(last, first, _, last_out, first_out):
        last_out[...] = last[:, 1 : rows - 1]
        first_out[...] = first[:, 1 : rows - 1]

    return pl.pallas_call(
        copy,
        grid=(1,),
        in_specs=[part(latents.shape, 1), part(latents.shape, 0), pl.BlockSpec(memory_space=pl.ANY)],
        out_specs=[whole(inner.shape)] * 2,
        out_shape=[inner] * 2,
        compiler_params=pltpu.CompilerParams(vmem_limit_bytes=6 * 2**20),
        name="inner",
    )(latents, latents, token)


def rows_after(token, *sources, plain=False):
    count = len(sources)

    def copy(*refs):
        inward, outward, *rows = refs[2 * count + (token is not None) :]
        lower = lax.axis_index("height") % 2 == 0
        for n in range(count):
            top, bottom = (ref.reshape(inward.shape[1:])[...] for ref in refs[2 * n : 2 * n + 2])
            inward[n] = jnp.where(lower, bottom, top)
            outward[n] = jnp.where(lower, top, bottom)
            if plain:
                rows[0][2 * n] = top
                rows[0][2 * n + 1] = bottom

    args = []
    for array, *places in sources:
        for place in places:
            block = (1,) * len(place) + array.shape[len(place) :]
            tail = (0,) * (array.ndim - len(place))
            args.append((array, pl.BlockSpec(block, lambda i, p=place, t=tail: (*p, *t))))
    if token is not None:
        args.append((token, pl.BlockSpec(memory_space=pl.ANY)))
    row = sources[0][0].shape[-2:]
    outs = [jax.ShapeDtypeStruct((n, *row), BF16) for n in [count] * 2 + [2 * count] * plain]
    return pl.pallas_call(
        copy,
        grid=(1,),
        in_specs=[spec for _, spec in args],
        out_specs=[whole(o.shape) for o in outs],
        out_shape=outs,
        compiler_params=pltpu.CompilerParams(vmem_limit_bytes=4 * 2**20),
        name="edges",
    )(*[array for array, _ in args])


def pairs(array, size):
    block = (size, *array.shape[1:])
    return [
        (array, pl.BlockSpec(block, lambda i, n=n: (n,) + (0,) * (len(block) - 1)))
        for n in range(array.shape[0] // size)
    ]


def first_section(latents, gain, kernel, bias):
    bottom = latents.shape[1] - 1
    acc, frame, inner, edge = shapes()
    k = [(kernel, part(kernel.shape, i)) for i in range(3)]
    first, last = ((latents, part(latents.shape, i)) for i in range(2))
    sources = [(latents, (i, 0), (i, bottom)) for i in range(2)]
    *sides, edges = rows_after(None, *sources, plain=True)
    edges = shift(edges)
    up, down = exchange_rows(*sides)
    inner_last, inner_first = inner_rows(latents, sides[0])
    before, earliest = shift(inner_last), shift(inner_first, False)

    sides = rows_after(up, (edges, (2,), (3,)), (edges, (0,), (1,)))
    acc_first, acc_last = own(last, first, up, down, gain, k, sides[0])
    up, down = (pairs(a, 1) for a in exchange_rows(*sides))
    edges = pairs(edges, 2)
    outs = [frame, acc]
    y_last, acc_first = call(
        functools.partial(before_kernel, False),
        "before",
        2,
        [whole(o.shape) for o in outs],
        outs,
        [w(before), edges[1], up[0], down[0], gain, k[0], k[1], bias, w(acc_first), w(acc_last)],
    )
    outs = [frame, inner, edge]
    y_first, inner_first, edge_first = call(
        functools.partial(earliest_kernel, False),
        "earliest",
        1,
        [whole(o.shape) for o in outs],
        outs,
        [w(earliest), edges[0], up[1], down[1], gain, k[0], bias, w(acc_first)],
    )
    return y_last, y_first, inner_first, edge_first


def second_section(results, latents, gain, kernel, bias):
    y_last, y_first, inner_first, edge_first = results
    bottom = latents.shape[1] - 1
    acc = shapes()[0]
    k = [(kernel, part(kernel.shape, i)) for i in range(3)]
    before = shift(y_last)
    edges = shift(edge_first)
    earliest = shift(inner_first)
    up, down = exchange_rows(
        *rows_after(edge_first, (y_first, (0, 0), (0, bottom)), (y_last, (0, 0), (0, bottom)))
    )
    sides = rows_after(up, (before, (0, 0), (0, bottom)))
    acc_first, acc_last = own_apart(w(y_last), w(y_first), up, down, gain, k, up, sides[0])

    out = jax.ShapeDtypeStruct(latents.shape, BF16)
    anywhere = pl.BlockSpec(memory_space=pl.ANY)
    extra = [pltpu.VMEM(latents.shape[1:], BF16), pltpu.SemaphoreType.DMA((len(chunks(*latents.shape[1:3], True)),))]
    args = [w(before), *map(w, exchange_rows(*sides)), gain, k[0], k[1], bias, w(acc_first), w(acc_last)]
    args.append((latents, part(latents.shape, 1)))
    half, acc_first = call(
        functools.partial(before_kernel, True),
        "before",
        2,
        [anywhere, whole(acc.shape)],
        [out, acc],
        args,
        extra=extra,
    )
    sides = rows_after(acc_last, (edges, (0,), (1,)))
    args = [w(earliest), w(edges), *map(w, exchange_rows(*sides)), gain, k[0], bias, w(acc_first)]
    args += [(latents, part(latents.shape, 0)), (half, anywhere)]
    body = functools.partial(earliest_kernel, True)
    return call(body, "earliest", 1, anywhere, out, args, {len(args) - 1: 0}, extra)


def per_device(
    latents, first_gain, first_kernel, first_bias, second_gain, second_kernel, second_bias
):
    frames, rows, cells, channels = latents.shape
    call.block = (rows, cells, channels)

    def columns(kernel):
        return kernel.reshape(3, 3, 3 * channels, channels)

    first_gain, first_bias, second_gain, second_bias = map(w, (first_gain, first_bias, second_gain, second_bias))
    results = first_section(latents, first_gain, columns(first_kernel), first_bias)
    return second_section(results, latents, second_gain, columns(second_kernel), second_bias)


def solution(mesh):
    return jax.shard_map(
        per_device,
        mesh=mesh,
        in_specs=(P("tm", "height", None, None), P(), P(), P(), P(), P(), P()),
        out_specs=P("tm", "height", None, None),
        check_vma=False,
    )
```

time: 48.4 us -> 44.2 us (0.913)
  waiting for transfers between devices: 17.4 us -> 8.18 us
  starting transfers between devices: 18.2 us -> 24.8 us
  local copies, waits for them, and re-layouts: 2.96 us -> 1.19 us
    ppermute x5 -> x6, starting transfers between devices: 8.41 us -> 16.2 us  [shift(): return lax.ppermute(array, 'tm', route if closed else route[:-1])]
    ppermute x5 -> x6, waiting for transfers between devices: 15.4 us -> 7.84 us  [shift(): return lax.ppermute(array, 'tm', route if closed else route[:-1])]
    ppermute x6 -> x5, waiting for transfers between devices: 2 us -> 0.33 us  [exchange_rows(): outward = lax.ppermute(outward, 'height', others)]
    slice x1 -> x0, local copies, waits for them, and re-layouts: 1.11 us -> none  [first_section(): before = shift(latents[1:])]
    ppermute x6 -> x5, starting transfers between devices: 1.22 us -> 0.35 us  [exchange_rows(): return (lax.ppermute(inward, 'height', pairs), outward)]
    unnamed x18 -> x16, local copies, waits for them, and re-layouts: 1.85 us -> 1.19 us
    ppermute x6 -> x5, starting transfers between devices: 8.54 us -> 8.26 us  [exchange_rows(): outward = lax.ppermute(outward, 'height', others)]
    pallas_call x6 -> x7, Pallas kernels: 9.09 us -> 9.18 us  [call(): pl.pallas_call(body, grid=(1,), in_specs=[s for _, s in args], out_specs=...]
  transfers between devices with their start and end apart: 17 -> 16, of which waited for: 5 -> 6; matrix products, arithmetic and copies ran while one was open for 0% -> 0% of each run, Pallas kernels for 17% -> 19%
where the time goes in v4:
time: 44.2 us; the launch traced here: 43.9 us
  starting transfers between devices  24.8 us (56%)
  Pallas kernels  9.34 us (21%)
  waiting for transfers between devices  8.18 us (19%)
  local copies, waits for them, and re-layouts  1.19 us (3%)
    ppermute x6, starting transfers between devices, shift(): return lax.ppermute(array, 'tm', route if closed else route[:-1])  16.2 us
    pallas_call x7, Pallas kernels, call(): pl.pallas_call(body, grid=(1,), in_specs=[s for _, s in args], out_specs=...  9.18 us
    ppermute x5, starting transfers between devices, exchange_rows(): outward = lax.ppermute(outward, 'height', others)  8.26 us
    ppermute x6, waiting for transfers between devices, shift(): return lax.ppermute(array, 'tm', route if closed else route[:-1])  7.84 us
    unnamed x16, local copies, waits for them, and re-layouts  1.19 us
  transfers between devices with their start and end apart: 16, of which 6 were waited for; matrix products, arithmetic and copies ran while one was open for 0% of the time, Pallas kernels for 19%

profile of v4, /device:TPU:0, one launch (start us, length us, event | category | flops | bytes accessed | tf_op | source)
XLA Modules:
  0.0 43.9 jit_solution(12155151285281269903)
XLA Ops:
  0.0 0.0 copy-start.1
  0.0 1.2 %copy-done.1 = bf16[2,8,104,256]{3,2,1,0:T(8,128)(2,1)S(1)} copy-done((bf16[2,8,104,256]{3,2,1,0:T(8,128)(2,1)S(1)}, bf16[2,8,104,256]{3,2,1,0:T(8,128)(2,1)}, u32[]{:S(2)}) %copy-start.1) | copy-done | bytes 851992
  1.2 0.0 copy-start.2
  1.2 0.0 copy-start.3
  1.2 0.0 copy-start.5
  1.2 3.0 %collective-permute-start.1 = (bf16[4,104,256]{2,1,0:T(8,128)(2,1)S(1)}, bf16[4,104,256]{2,1,0:T(8,128)(2,1)S(1)}, u32[]{:S(2)}, u32[]{:S(2)}) collective-permute-start(bf16[4,104,256]{2,1,0:T(8,128)(2,1)S(1)} %get-tuple-element.31), channel_id=1, source_target_pairs={{0,4},{4,8},{8,12},{12,16},{16,20},{20,24},{24,28},{28,0},{1,5},{5... | collective-permute-start | bytes 638984 | tf_op jit(solution)/shard_map/ppermute | solution.py:268
  4.2 0.0 collective-permute-start.2
  4.2 1.6 %collective-permute-start.6 = (bf16[2,104,256]{2,1,0:T(8,128)(2,1)S(1)}, bf16[2,104,256]{2,1,0:T(8,128)(2,1)S(1)}, u32[]{:S(2)}, u32[]{:S(2)}) collective-permute-start(bf16[2,104,256]{2,1,0:T(8,128)(2,1)S(1)} %get-tuple-element.35), channel_id=1, source_target_pairs={{0,3},{1,2},{2,1},{3,0},{4,7},{5,6},{6,5},{7,4},{8,11},{9,10},{10,... | collective-permute-start | bytes 319496 | tf_op jit(solution)/shard_map/ppermute | solution.py:258
  5.8 0.0 copy-done.2
  5.9 1.6 %collective-permute-start.5 = (bf16[1,6,104,256]{3,2,1,0:T(8,128)(2,1)S(1)}, bf16[1,6,104,256]{3,2,1,0:T(8,128)(2,1)S(1)}, u32[]{:S(2)}, u32[]{:S(2)}) collective-permute-start(bf16[1,6,104,256]{3,2,1,0:T(8,128)(2,1)S(1)} %get-tuple-element.34), channel_id=1, source_target_pairs={{0,4},{4,8},{8,12},{12,16},{16,20},{20,24},{24,28},{28,0},{1,5},{5... | collective-permute-start | bytes 958472 | tf_op jit(solution)/shard_map/ppermute | solution.py:268
  7.5 3.4 %collective-permute-start = (bf16[1,6,104,256]{3,2,1,0:T(8,128)(2,1)S(1)}, bf16[1,6,104,256]{3,2,1,0:T(8,128)(2,1)S(1)}, u32[]{:S(2)}, u32[]{:S(2)}) collective-permute-start(bf16[1,6,104,256]{3,2,1,0:T(8,128)(2,1)S(1)} %get-tuple-element.30), channel_id=1, source_target_pairs={{0,4},{4,8},{8,12},{12,16},{16,20},{20,24},{24,28},{1,5},{5,9},{9,... | collective-permute-start | bytes 958472 | tf_op jit(solution)/shard_map/ppermute | solution.py:268
  10.9 0.0 collective-permute-done.2.refs_4_.up
  10.9 2.4 %collective-permute-done.1.refs_0_.refs_1_.refs_2_.refs_3_ = bf16[4,104,256]{2,1,0:T(8,128)(2,1)S(1)} collective-permute-done((bf16[4,104,256]{2,1,0:T(8,128)(2,1)S(1)}, bf16[4,104,256]{2,1,0:T(8,128)(2,1)S(1)}, u32[]{:S(2)}, u32[]{:S(2)}) %collective-permute-start.1) | collective-permute-done | bytes 213024 | tf_op jit(solution)/shard_map/ppermute | solution.py:268
  13.3 0.1 collective-permute-start.3
  13.4 1.9 %collective-permute-start.4 = (bf16[2,104,256]{2,1,0:T(8,128)(2,1)S(1)}, bf16[2,104,256]{2,1,0:T(8,128)(2,1)S(1)}, u32[]{:S(2)}, u32[]{:S(2)}) collective-permute-start(bf16[2,104,256]{2,1,0:T(8,128)(2,1)S(1)} %get-tuple-element.33), channel_id=1, source_target_pairs={{0,3},{1,2},{2,1},{3,0},{4,7},{5,6},{6,5},{7,4},{8,11},{9,10},{10,... | collective-permute-start | bytes 319496 | tf_op jit(solution)/shard_map/ppermute | solution.py:258
  15.3 0.0 collective-permute-done.6.down
  15.3 0.0 copy-done.3
  15.3 0.0 copy-done.5
  15.3 0.0 copy-start.6
  15.3 3.5 %own.1 = (f32[832,256]{1,0:T(8,128)S(1)}, f32[832,256]{1,0:T(8,128)S(1)}) custom-call(bf16[2,8,104,256]{3,2,1,0:T(8,128)(2,1)S(1)} %copy-done.2, bf16[2,8,104,256]{3,2,1,0:T(8,128)(2,1)S(1)} %copy-done.2, bf16[2,104,256]{2,1,0:T(8,128)(2,1)S(1)} %collective-permute-done.2.refs_4_.up, bf16[2,104,256]{2,1,0:T(8,128)(2,1)S(1)} %collective-permute-done.6.down, ...), custom_call_target="tpu_custom_call" | custom-call | flops 2944401408 | bytes 6291456 | tf_op jit(solution)/shard_map/own/pallas_call | solution.py:233
  18.8 0.0 collective-permute-done.3.refs_2_
  18.8 0.0 collective-permute-done.4.refs_3_
  18.8 0.5 %collective-permute-done.5.refs_0_ = bf16[1,6,104,256]{3,2,1,0:T(8,128)(2,1)S(1)} collective-permute-done((bf16[1,6,104,256]{3,2,1,0:T(8,128)(2,1)S(1)}, bf16[1,6,104,256]{3,2,1,0:T(8,128)(2,1)S(1)}, u32[]{:S(2)}, u32[]{:S(2)}) %collective-permute-start.5) | collective-permute-done | bytes 319520 | tf_op jit(solution)/shard_map/ppermute | solution.py:268
  19.3 0.0 copy-done.6
  19.3 0.1 before.2
  19.4 0.0 copy-start
  19.5 0.0 copy-start.4
  19.5 2.2 %collective-permute-start.11 = (bf16[1,8,104,256]{3,2,1,0:T(8,128)(2,1)S(1)}, bf16[1,8,104,256]{3,2,1,0:T(8,128)(2,1)S(1)}, u32[]{:S(2)}, u32[]{:S(2)}) collective-permute-start(bf16[1,8,104,256]{3,2,1,0:T(8,128)(2,1)S(1)} %get-tuple-element.42.refs_2_.refs_3_.last), channel_id=1, source_target_pairs={{0,4},{4,8},{8,12},{12,16},{16,20},{20,24},{24,28},{28,0},{1,5},{5... | collective-permute-start | bytes 1277960 | tf_op jit(solution)/shard_map/ppermute | solution.py:268
  21.6 1.8 %collective-permute-done.refs_0_ = bf16[1,6,104,256]{3,2,1,0:T(8,128)(2,1)S(1)} collective-permute-done((bf16[1,6,104,256]{3,2,1,0:T(8,128)(2,1)S(1)}, bf16[1,6,104,256]{3,2,1,0:T(8,128)(2,1)S(1)}, u32[]{:S(2)}, u32[]{:S(2)}) %collective-permute-start) | collective-permute-done | bytes 319520 | tf_op jit(solution)/shard_map/ppermute | solution.py:268
  23.4 0.1 earliest.2
  23.6 0.1 collective-permute-start.9
  23.6 1.7 %collective-permute-start.10 = (bf16[2,104,256]{2,1,0:T(8,128)(2,1)S(1)}, bf16[2,104,256]{2,1,0:T(8,128)(2,1)S(1)}, u32[]{:S(2)}, u32[]{:S(2)}) collective-permute-start(bf16[2,104,256]{2,1,0:T(8,128)(2,1)S(1)} %get-tuple-element.44), channel_id=1, source_target_pairs={{0,3},{1,2},{2,1},{3,0},{4,7},{5,6},{6,5},{7,4},{8,11},{9,10},{10,... | collective-permute-start | bytes 319496 | tf_op jit(solution)/shard_map/ppermute | solution.py:258
  25.4 3.9 %collective-permute-start.8 = (bf16[2,104,256]{2,1,0:T(8,128)(2,1)S(1)}, bf16[2,104,256]{2,1,0:T(8,128)(2,1)S(1)}, u32[]{:S(2)}, u32[]{:S(2)}) collective-permute-start(bf16[2,104,256]{2,1,0:T(8,128)(2,1)S(1)} %get-tuple-element.40.refs_4_), channel_id=1, source_target_pairs={{0,4},{4,8},{8,12},{12,16},{16,20},{20,24},{24,28},{28,0},{1,5},{5... | collective-permute-start | bytes 319496 | tf_op jit(solution)/shard_map/ppermute | solution.py:268
  29.3 2.1 %collective-permute-start.7 = (bf16[1,6,104,256]{3,2,1,0:T(8,128)(2,1)S(1)}, bf16[1,6,104,256]{3,2,1,0:T(8,128)(2,1)S(1)}, u32[]{:S(2)}, u32[]{:S(2)}) collective-permute-start(bf16[1,6,104,256]{3,2,1,0:T(8,128)(2,1)S(1)} %get-tuple-element.39), channel_id=1, source_target_pairs={{0,4},{4,8},{8,12},{12,16},{16,20},{20,24},{24,28},{28,0},{1,5},{5... | collective-permute-start | bytes 958472 | tf_op jit(solution)/shard_map/ppermute | solution.py:268
  31.4 0.0 collective-permute-done.9.up._.refs_2_
  31.4 0.0 collective-permute-done.10.down
  31.4 0.0 copy-done
  31.4 0.0 copy-done.4
  31.4 1.5 %last.5.acc_in = f32[832,256]{1,0:T(8,128)S(1)} custom-call(bf16[1,8,104,256]{3,2,1,0:T(8,128)(2,1)S(1)} %get-tuple-element.42.refs_2_.refs_3_.last, bf16[2,104,256]{2,1,0:T(8,128)(2,1)S(1)} %collective-permute-done.9.up._.refs_2_, bf16[2,104,256]{2,1,0:T(8,128)(2,1)S(1)} %collective-permute-done.10.down, bf16[256]{0:T(256)(128)(2,1)S(1)} %copy-done.4, ...), custom_call_target="tpu_custom_call" | custom-call | flops 981467136 | bytes 2097152 | tf_op jit(solution)/shard_map/last/pallas_call | solution.py:233
  32.9 0.8 %collective-permute-done.11.refs_0_.refs_1_ = bf16[1,8,104,256]{3,2,1,0:T(8,128)(2,1)S(1)} collective-permute-done((bf16[1,8,104,256]{3,2,1,0:T(8,128)(2,1)S(1)}, bf16[1,8,104,256]{3,2,1,0:T(8,128)(2,1)S(1)}, u32[]{:S(2)}, u32[]{:S(2)}) %collective-permute-start.11) | collective-permute-done | bytes 426016 | tf_op jit(solution)/shard_map/ppermute | solution.py:268
  33.7 0.1 collective-permute-start.14
  33.8 0.0 copy-start.7
  33.8 3.0 %collective-permute-start.15 = (bf16[1,104,256]{2,1,0:T(8,128)(2,1)S(1)}, bf16[1,104,256]{2,1,0:T(8,128)(2,1)S(1)}, u32[]{:S(2)}, u32[]{:S(2)}) collective-permute-start(bf16[1,104,256]{2,1,0:T(8,128)(2,1)S(1)} %get-tuple-element.49), channel_id=1, source_target_pairs={{0,3},{1,2},{2,1},{3,0},{4,7},{5,6},{6,5},{7,4},{8,11},{9,10},{10,... | collective-permute-start | bytes 159752 | tf_op jit(solution)/shard_map/ppermute | solution.py:258
  36.9 2.4 %first.5 = (f32[832,256]{1,0:T(8,128)S(1)}, f32[832,256]{1,0:T(8,128)S(1)}) custom-call(bf16[1,8,104,256]{3,2,1,0:T(8,128)(2,1)S(1)} %get-tuple-element.41.refs_0_.refs_1_.first, bf16[2,104,256]{2,1,0:T(8,128)(2,1)S(1)} %collective-permute-done.9.up._.refs_2_, bf16[2,104,256]{2,1,0:T(8,128)(2,1)S(1)} %collective-permute-done.10.down, ...), custom_call_target="tpu_custom_call" | custom-call | flops 1962934272 | bytes 4194304 | tf_op jit(solution)/shard_map/first/pallas_call | solution.py:233
  39.2 0.0 collective-permute-done.8.refs_0_.refs_1_
  39.3 0.1 collective-permute-start.12
  39.4 0.0 collective-permute-start.13
  39.4 0.0 collective-permute-done.14.refs_1_
  39.4 0.0 collective-permute-done.15.refs_2_
  39.4 0.0 copy-done.7
  39.4 0.9 %before.3 = (bf16[2,8,104,256]{3,2,1,0:T(8,128)(2,1)}, f32[832,256]{1,0:T(8,128)S(1)}) custom-call(bf16[1,8,104,256]{3,2,1,0:T(8,128)(2,1)S(1)} %collective-permute-done.11.refs_0_.refs_1_, bf16[1,104,256]{2,1,0:T(8,128)(2,1)S(1)} %collective-permute-done.14.refs_1_, bf16[1,104,256]{2,1,0:T(8,128)(2,1)S(1)} %collective-permute-done.15.refs_2_, ...), custom_call_target="tpu_custom_call" | custom-call | flops 1962934272 | bytes 4194304 | tf_op jit(solution)/shard_map/before/pallas_call | solution.py:233
  40.4 2.3 %collective-permute-done.7.refs_0_ = bf16[1,6,104,256]{3,2,1,0:T(8,128)(2,1)S(1)} collective-permute-done((bf16[1,6,104,256]{3,2,1,0:T(8,128)(2,1)S(1)}, bf16[1,6,104,256]{3,2,1,0:T(8,128)(2,1)S(1)}, u32[]{:S(2)}, u32[]{:S(2)}) %collective-permute-start.7) | collective-permute-done | bytes 319520 | tf_op jit(solution)/shard_map/ppermute | solution.py:268
  42.6 0.0 collective-permute-done.12.refs_2_
  42.6 0.3 collective-permute-done.13.refs_3_
  43.0 0.8 %earliest.3 = bf16[2,8,104,256]{3,2,1,0:T(8,128)(2,1)} custom-call(bf16[1,6,104,256]{3,2,1,0:T(8,128)(2,1)S(1)} %collective-permute-done.7.refs_0_, bf16[2,104,256]{2,1,0:T(8,128)(2,1)S(1)} %collective-permute-done.8.refs_0_.refs_1_, bf16[1,104,256]{2,1,0:T(8,128)(2,1)S(1)} %collective-permute-done.12.refs_2_, ...), custom_call_target="tpu_custom_call", output_to_operand_aliasing={{}: (9, {})} | custom-call | flops 981467136 | bytes 2097152 | tf_op jit(solution)/shard_map/earliest/pallas_call | solution.py:233
  (6 shorter events, 0.2 us)
Async XLA Ops:
  0.0 1.2 %copy-start.1 = (bf16[2,8,104,256]{3,2,1,0:T(8,128)(2,1)S(1)}, bf16[2,8,104,256]{3,2,1,0:T(8,128)(2,1)}, u32[]{:S(2)}) copy-start(bf16[2,8,104,256]{3,2,1,0:T(8,128)(2,1)} %refs_8_.1) | copy-start | bytes 2555908
  1.2 4.7 %copy-start.2 = (bf16[2,8,104,256]{3,2,1,0:T(8,128)(2,1)S(1)}, bf16[2,8,104,256]{3,2,1,0:T(8,128)(2,1)}, u32[]{:S(2)}) copy-start(bf16[2,8,104,256]{3,2,1,0:T(8,128)(2,1)} %refs_8_.1) | copy-start | bytes 2555908
  1.2 14.1 %copy-start.3 = (bf16[3,3,3,256,256]{4,3,2,1,0:T(8,128)(2,1)S(1)}, bf16[3,3,3,256,256]{4,3,2,1,0:T(8,128)(2,1)}, u32[]{:S(2)}) copy-start(bf16[3,3,3,256,256]{4,3,2,1,0:T(8,128)(2,1)} %param.9) | copy-start | bytes 10616836
  1.2 14.1 %copy-start.5 = (bf16[256]{0:T(256)(128)(2,1)S(1)}, bf16[256]{0:T(256)(128)(2,1)}, u32[]{:S(2)}) copy-start(bf16[256]{0:T(256)(128)(2,1)} %refs_4_.4) | copy-start | bytes 1540
  1.2 12.1 %collective-permute-start.1 = (bf16[4,104,256]{2,1,0:T(8,128)(2,1)S(1)}, bf16[4,104,256]{2,1,0:T(8,128)(2,1)S(1)}, u32[]{:S(2)}, u32[]{:S(2)}) collective-permute-start(bf16[4,104,256]{2,1,0:T(8,128)(2,1)S(1)} %get-tuple-element.31), channel_id=1, source_target_pairs={{0,4},{4,8},{8,12},{12,16},{16,20},{20,24},{24,28},{28,0},{1,5},{5... | collective-permute-start | bytes 638984 | tf_op jit(solution)/shard_map/ppermute | solution.py:268
  4.2 6.7 %collective-permute-start.2 = (bf16[2,104,256]{2,1,0:T(8,128)(2,1)S(1)}, bf16[2,104,256]{2,1,0:T(8,128)(2,1)S(1)}, u32[]{:S(2)}, u32[]{:S(2)}) collective-permute-start(bf16[2,104,256]{2,1,0:T(8,128)(2,1)S(1)} %get-tuple-element.29._), channel_id=1, source_target_pairs={{0,1},{1,0},{2,3},{3,2},{4,5},{5,4},{6,7},{7,6},{8,9},{9,8},{10,11... | collective-permute-start | bytes 319496 | tf_op jit(solution)/shard_map/ppermute | solution.py:259
  4.2 11.1 %collective-permute-start.6 = (bf16[2,104,256]{2,1,0:T(8,128)(2,1)S(1)}, bf16[2,104,256]{2,1,0:T(8,128)(2,1)S(1)}, u32[]{:S(2)}, u32[]{:S(2)}) collective-permute-start(bf16[2,104,256]{2,1,0:T(8,128)(2,1)S(1)} %get-tuple-element.35), channel_id=1, source_target_pairs={{0,3},{1,2},{2,1},{3,0},{4,7},{5,6},{6,5},{7,4},{8,11},{9,10},{10,... | collective-permute-start | bytes 319496 | tf_op jit(solution)/shard_map/ppermute | solution.py:258
  5.9 13.5 %collective-permute-start.5 = (bf16[1,6,104,256]{3,2,1,0:T(8,128)(2,1)S(1)}, bf16[1,6,104,256]{3,2,1,0:T(8,128)(2,1)S(1)}, u32[]{:S(2)}, u32[]{:S(2)}) collective-permute-start(bf16[1,6,104,256]{3,2,1,0:T(8,128)(2,1)S(1)} %get-tuple-element.34), channel_id=1, source_target_pairs={{0,4},{4,8},{8,12},{12,16},{16,20},{20,24},{24,28},{28,0},{1,5},{5... | collective-permute-start | bytes 958472 | tf_op jit(solution)/shard_map/ppermute | solution.py:268
  7.5 16.0 %collective-permute-start = (bf16[1,6,104,256]{3,2,1,0:T(8,128)(2,1)S(1)}, bf16[1,6,104,256]{3,2,1,0:T(8,128)(2,1)S(1)}, u32[]{:S(2)}, u32[]{:S(2)}) collective-permute-start(bf16[1,6,104,256]{3,2,1,0:T(8,128)(2,1)S(1)} %get-tuple-element.30), channel_id=1, source_target_pairs={{0,4},{4,8},{8,12},{12,16},{16,20},{20,24},{24,28},{1,5},{5,9},{9,... | collective-permute-start | bytes 958472 | tf_op jit(solution)/shard_map/ppermute | solution.py:268
  13.3 5.4 %collective-permute-start.3 = (bf16[2,104,256]{2,1,0:T(8,128)(2,1)S(1)}, bf16[2,104,256]{2,1,0:T(8,128)(2,1)S(1)}, u32[]{:S(2)}, u32[]{:S(2)}) collective-permute-start(bf16[2,104,256]{2,1,0:T(8,128)(2,1)S(1)} %get-tuple-element.32._), channel_id=1, source_target_pairs={{0,1},{1,0},{2,3},{3,2},{4,5},{5,4},{6,7},{7,6},{8,9},{9,8},{10,11... | collective-permute-start | bytes 319496 | tf_op jit(solution)/shard_map/ppermute | solution.py:259
  13.4 5.4 %collective-permute-start.4 = (bf16[2,104,256]{2,1,0:T(8,128)(2,1)S(1)}, bf16[2,104,256]{2,1,0:T(8,128)(2,1)S(1)}, u32[]{:S(2)}, u32[]{:S(2)}) collective-permute-start(bf16[2,104,256]{2,1,0:T(8,128)(2,1)S(1)} %get-tuple-element.33), channel_id=1, source_target_pairs={{0,3},{1,2},{2,1},{3,0},{4,7},{5,6},{6,5},{7,4},{8,11},{9,10},{10,... | collective-permute-start | bytes 319496 | tf_op jit(solution)/shard_map/ppermute | solution.py:258
  15.3 4.0 %copy-start.6 = (bf16[256]{0:T(256)(128)(2,1)S(1)}, bf16[256]{0:T(256)(128)(2,1)}, u32[]{:S(2)}) copy-start(bf16[256]{0:T(256)(128)(2,1)} %refs_6_.3) | copy-start | bytes 1540
  19.4 12.0 %copy-start = (bf16[3,3,3,256,256]{4,3,2,1,0:T(8,128)(2,1)S(1)}, bf16[3,3,3,256,256]{4,3,2,1,0:T(8,128)(2,1)}, u32[]{:S(2)}) copy-start(bf16[3,3,3,256,256]{4,3,2,1,0:T(8,128)(2,1)} %param.12) | copy-start | bytes 10616836
  19.5 12.0 %copy-start.4 = (bf16[256]{0:T(256)(128)(2,1)S(1)}, bf16[256]{0:T(256)(128)(2,1)}, u32[]{:S(2)}) copy-start(bf16[256]{0:T(256)(128)(2,1)} %refs_4_.5) | copy-start | bytes 1540
  19.5 14.3 %collective-permute-start.11 = (bf16[1,8,104,256]{3,2,1,0:T(8,128)(2,1)S(1)}, bf16[1,8,104,256]{3,2,1,0:T(8,128)(2,1)S(1)}, u32[]{:S(2)}, u32[]{:S(2)}) collective-permute-start(bf16[1,8,104,256]{3,2,1,0:T(8,128)(2,1)S(1)} %get-tuple-element.42.refs_2_.refs_3_.last), channel_id=1, source_target_pairs={{0,4},{4,8},{8,12},{12,16},{16,20},{20,24},{24,28},{28,0},{1,5},{5... | collective-permute-start | bytes 1277960 | tf_op jit(solution)/shard_map/ppermute | solution.py:268
  23.6 7.9 %collective-permute-start.9 = (bf16[2,104,256]{2,1,0:T(8,128)(2,1)S(1)}, bf16[2,104,256]{2,1,0:T(8,128)(2,1)S(1)}, u32[]{:S(2)}, u32[]{:S(2)}) collective-permute-start(bf16[2,104,256]{2,1,0:T(8,128)(2,1)S(1)} %get-tuple-element.43), channel_id=1, source_target_pairs={{0,1},{1,0},{2,3},{3,2},{4,5},{5,4},{6,7},{7,6},{8,9},{9,8},{10,11... | collective-permute-start | bytes 319496 | tf_op jit(solution)/shard_map/ppermute | solution.py:259
  23.6 7.8 %collective-permute-start.10 = (bf16[2,104,256]{2,1,0:T(8,128)(2,1)S(1)}, bf16[2,104,256]{2,1,0:T(8,128)(2,1)S(1)}, u32[]{:S(2)}, u32[]{:S(2)}) collective-permute-start(bf16[2,104,256]{2,1,0:T(8,128)(2,1)S(1)} %get-tuple-element.44), channel_id=1, source_target_pairs={{0,3},{1,2},{2,1},{3,0},{4,7},{5,6},{6,5},{7,4},{8,11},{9,10},{10,... | collective-permute-start | bytes 319496 | tf_op jit(solution)/shard_map/ppermute | solution.py:258
  25.4 13.8 %collective-permute-start.8 = (bf16[2,104,256]{2,1,0:T(8,128)(2,1)S(1)}, bf16[2,104,256]{2,1,0:T(8,128)(2,1)S(1)}, u32[]{:S(2)}, u32[]{:S(2)}) collective-permute-start(bf16[2,104,256]{2,1,0:T(8,128)(2,1)S(1)} %get-tuple-element.40.refs_4_), channel_id=1, source_target_pairs={{0,4},{4,8},{8,12},{12,16},{16,20},{20,24},{24,28},{28,0},{1,5},{5... | collective-permute-start | bytes 319496 | tf_op jit(solution)/shard_map/ppermute | solution.py:268
  29.3 13.4 %collective-permute-start.7 = (bf16[1,6,104,256]{3,2,1,0:T(8,128)(2,1)S(1)}, bf16[1,6,104,256]{3,2,1,0:T(8,128)(2,1)S(1)}, u32[]{:S(2)}, u32[]{:S(2)}) collective-permute-start(bf16[1,6,104,256]{3,2,1,0:T(8,128)(2,1)S(1)} %get-tuple-element.39), channel_id=1, source_target_pairs={{0,4},{4,8},{8,12},{12,16},{16,20},{20,24},{24,28},{28,0},{1,5},{5... | collective-permute-start | bytes 958472 | tf_op jit(solution)/shard_map/ppermute | solution.py:268
  33.7 5.7 %collective-permute-start.14 = (bf16[1,104,256]{2,1,0:T(8,128)(2,1)S(1)}, bf16[1,104,256]{2,1,0:T(8,128)(2,1)S(1)}, u32[]{:S(2)}, u32[]{:S(2)}) collective-permute-start(bf16[1,104,256]{2,1,0:T(8,128)(2,1)S(1)} %get-tuple-element.45._), channel_id=1, source_target_pairs={{0,1},{1,0},{2,3},{3,2},{4,5},{5,4},{6,7},{7,6},{8,9},{9,8},{10,11... | collective-permute-start | bytes 159752 | tf_op jit(solution)/shard_map/ppermute | solution.py:259
  33.8 5.6 %copy-start.7 = (bf16[256]{0:T(256)(128)(2,1)S(1)}, bf16[256]{0:T(256)(128)(2,1)}, u32[]{:S(2)}) copy-start(bf16[256]{0:T(256)(128)(2,1)} %refs_6_.5) | copy-start | bytes 1540
  33.8 5.6 %collective-permute-start.15 = (bf16[1,104,256]{2,1,0:T(8,128)(2,1)S(1)}, bf16[1,104,256]{2,1,0:T(8,128)(2,1)S(1)}, u32[]{:S(2)}, u32[]{:S(2)}) collective-permute-start(bf16[1,104,256]{2,1,0:T(8,128)(2,1)S(1)} %get-tuple-element.49), channel_id=1, source_target_pairs={{0,3},{1,2},{2,1},{3,0},{4,7},{5,6},{6,5},{7,4},{8,11},{9,10},{10,... | collective-permute-start | bytes 159752 | tf_op jit(solution)/shard_map/ppermute | solution.py:258
  39.3 3.4 %collective-permute-start.12 = (bf16[1,104,256]{2,1,0:T(8,128)(2,1)S(1)}, bf16[1,104,256]{2,1,0:T(8,128)(2,1)S(1)}, u32[]{:S(2)}, u32[]{:S(2)}) collective-permute-start(bf16[1,104,256]{2,1,0:T(8,128)(2,1)S(1)} %get-tuple-element.47), channel_id=1, source_target_pairs={{0,1},{1,0},{2,3},{3,2},{4,5},{5,4},{6,7},{7,6},{8,9},{9,8},{10,11... | collective-permute-start | bytes 159752 | tf_op jit(solution)/shard_map/ppermute | solution.py:259
  39.4 3.6 %collective-permute-start.13 = (bf16[1,104,256]{2,1,0:T(8,128)(2,1)S(1)}, bf16[1,104,256]{2,1,0:T(8,128)(2,1)S(1)}, u32[]{:S(2)}, u32[]{:S(2)}) collective-permute-start(bf16[1,104,256]{2,1,0:T(8,128)(2,1)S(1)} %get-tuple-element.48), channel_id=1, source_target_pairs={{0,3},{1,2},{2,1},{3,0},{4,7},{5,6},{6,5},{7,4},{8,11},{9,10},{10,... | collective-permute-start | bytes 159752 | tf_op jit(solution)/shard_map/ppermute | solution.py:258

commit v5 on v4

--- a/solution.py
+++ b/solution.py
@@ -360,7 +360,8 @@
     k = [(kernel, part(kernel.shape, i)) for i in range(3)]
     first, last = ((latents, part(latents.shape, i)) for i in range(2))
     sources = [(latents, (i, 0), (i, bottom)) for i in range(2)]
-    *sides, edges = rows_after(None, *sources, plain=True)
+    edges = latents[:, ::bottom].reshape(4, *latents.shape[2:])
+    sides = rows_after(None, *sources)
     edges = shift(edges)
     up, down = exchange_rows(*sides)
     inner_last, inner_first = inner_rows(latents, sides[0])

time: 44.2 us -> 43.7 us (0.989)
  waiting for transfers between devices: 8.18 us -> 5.73 us
  starting transfers between devices: 24.8 us -> 25.9 us
  local copies, waits for them, and re-layouts: 1.19 us -> 2.15 us
    ppermute x6, waiting for transfers between devices: 7.84 us -> 5.39 us  [shift(): return lax.ppermute(array, 'tm', route if closed else route[:-1])]
    slice x0 -> x1, local copies, waits for them, and re-layouts: none -> 0.96 us  [first_section(): edges = latents[:, ::bottom].reshape(4, *latents.shape[2:])]
    ppermute x5, starting transfers between devices: 8.26 us -> 8.91 us  [exchange_rows(): outward = lax.ppermute(outward, 'height', others)]
  transfers between devices with their start and end apart: 16 -> 16, of which waited for: 6 -> 6; matrix products, arithmetic and copies ran while one was open for 0% -> 0% of each run, Pallas kernels for 19% -> 20%
where the time goes in v5:
time: 43.7 us; the launch traced here: 43.5 us
  starting transfers between devices  25.9 us (59%)
  Pallas kernels  9.34 us (21%)
  waiting for transfers between devices  5.73 us (13%)
  local copies, waits for them, and re-layouts  2.15 us (5%)
    ppermute x6, starting transfers between devices, shift(): return lax.ppermute(array, 'tm', route if closed else route[:-1])  16.6 us
    pallas_call x7, Pallas kernels, call(): pl.pallas_call(body, grid=(1,), in_specs=[s for _, s in args], out_specs=...  9.18 us
    ppermute x5, starting transfers between devices, exchange_rows(): outward = lax.ppermute(outward, 'height', others)  8.91 us
    ppermute x6, waiting for transfers between devices, shift(): return lax.ppermute(array, 'tm', route if closed else route[:-1])  5.39 us
    unnamed x16, local copies, waits for them, and re-layouts  1.19 us
    slice x1, local copies, waits for them, and re-layouts, first_section(): edges = latents[:, ::bottom].reshape(4, *latents.shape[2:])  0.96 us
  transfers between devices with their start and end apart: 16, of which 6 were waited for; matrix products, arithmetic and copies ran while one was open for 0% of the time, Pallas kernels for 20%

profile of v5, /device:TPU:0, one launch (start us, length us, event | category | flops | bytes accessed | tf_op | source)
XLA Modules:
  0.0 43.5 jit_solution(10722873522006067983)
XLA Ops:
  0.0 0.0 copy-start.5
  0.0 1.0 %slice.3 = bf16[2,2,104,256]{3,2,1,0:T(8,128)(2,1)S(1)} slice(bf16[2,8,104,256]{3,2,1,0:T(8,128)(2,1)} %refs_8_.1), slice={[0:2:1], [0:8:7], [0:104:1], [0:256:1]} | slice | bytes 425984 | tf_op jit(solution)/shard_map/slice | solution.py:363
  1.0 3.0 %collective-permute-start.1 = (bf16[4,104,256]{2,1,0:T(8,128)(2,1)S(1)}, bf16[4,104,256]{2,1,0:T(8,128)(2,1)S(1)}, u32[]{:S(2)}, u32[]{:S(2)}) collective-permute-start(bf16[4,104,256]{2,1,0:T(8,128)(2,1)S(1)} %bitcast.14), channel_id=1, source_target_pairs={{0,4},{4,8},{8,12},{12,16},{16,20},{20,24},{24,28},{28,0},{1,5},{5... | collective-permute-start | bytes 638984 | tf_op jit(solution)/shard_map/ppermute | solution.py:268
  4.0 0.0 copy-start.1
  4.0 1.2 %copy-done.1 = bf16[2,8,104,256]{3,2,1,0:T(8,128)(2,1)S(1)} copy-done((bf16[2,8,104,256]{3,2,1,0:T(8,128)(2,1)S(1)}, bf16[2,8,104,256]{3,2,1,0:T(8,128)(2,1)}, u32[]{:S(2)}) %copy-start.1) | copy-done | bytes 851992
  5.1 0.0 copy-start.2
  5.1 0.0 copy-start.3
  5.1 0.1 collective-permute-start.2
  5.2 1.6 %collective-permute-start.6 = (bf16[2,104,256]{2,1,0:T(8,128)(2,1)S(1)}, bf16[2,104,256]{2,1,0:T(8,128)(2,1)S(1)}, u32[]{:S(2)}, u32[]{:S(2)}) collective-permute-start(bf16[2,104,256]{2,1,0:T(8,128)(2,1)S(1)} %get-tuple-element.33), channel_id=1, source_target_pairs={{0,3},{1,2},{2,1},{3,0},{4,7},{5,6},{6,5},{7,4},{8,11},{9,10},{10,... | collective-permute-start | bytes 319496 | tf_op jit(solution)/shard_map/ppermute | solution.py:258
  6.9 0.0 copy-done.2
  6.9 1.6 %collective-permute-start.5 = (bf16[1,6,104,256]{3,2,1,0:T(8,128)(2,1)S(1)}, bf16[1,6,104,256]{3,2,1,0:T(8,128)(2,1)S(1)}, u32[]{:S(2)}, u32[]{:S(2)}) collective-permute-start(bf16[1,6,104,256]{3,2,1,0:T(8,128)(2,1)S(1)} %get-tuple-element.32), channel_id=1, source_target_pairs={{0,4},{4,8},{8,12},{12,16},{16,20},{20,24},{24,28},{28,0},{1,5},{5... | collective-permute-start | bytes 958472 | tf_op jit(solution)/shard_map/ppermute | solution.py:268
  8.5 3.4 %collective-permute-start = (bf16[1,6,104,256]{3,2,1,0:T(8,128)(2,1)S(1)}, bf16[1,6,104,256]{3,2,1,0:T(8,128)(2,1)S(1)}, u32[]{:S(2)}, u32[]{:S(2)}) collective-permute-start(bf16[1,6,104,256]{3,2,1,0:T(8,128)(2,1)S(1)} %get-tuple-element.29), channel_id=1, source_target_pairs={{0,4},{4,8},{8,12},{12,16},{16,20},{20,24},{24,28},{1,5},{5,9},{9,... | collective-permute-start | bytes 958472 | tf_op jit(solution)/shard_map/ppermute | solution.py:268
  11.9 0.0 collective-permute-done.2.refs_4_.up
  11.9 0.3 collective-permute-done.1.refs_0_.refs_1_.refs_2_.refs_3_
  12.3 0.1 collective-permute-start.3
  12.4 2.5 %collective-permute-start.4 = (bf16[2,104,256]{2,1,0:T(8,128)(2,1)S(1)}, bf16[2,104,256]{2,1,0:T(8,128)(2,1)S(1)}, u32[]{:S(2)}, u32[]{:S(2)}) collective-permute-start(bf16[2,104,256]{2,1,0:T(8,128)(2,1)S(1)} %get-tuple-element.31), channel_id=1, source_target_pairs={{0,3},{1,2},{2,1},{3,0},{4,7},{5,6},{6,5},{7,4},{8,11},{9,10},{10,... | collective-permute-start | bytes 319496 | tf_op jit(solution)/shard_map/ppermute | solution.py:258
  14.9 0.0 collective-permute-done.6.down
  14.9 0.0 copy-done.5
  14.9 0.0 copy-done.3
  14.9 0.0 copy-start.6
  14.9 3.5 %own.1 = (f32[832,256]{1,0:T(8,128)S(1)}, f32[832,256]{1,0:T(8,128)S(1)}) custom-call(bf16[2,8,104,256]{3,2,1,0:T(8,128)(2,1)S(1)} %copy-done.2, bf16[2,8,104,256]{3,2,1,0:T(8,128)(2,1)S(1)} %copy-done.2, bf16[2,104,256]{2,1,0:T(8,128)(2,1)S(1)} %collective-permute-done.2.refs_4_.up, bf16[2,104,256]{2,1,0:T(8,128)(2,1)S(1)} %collective-permute-done.6.down, ...), custom_call_target="tpu_custom_call" | custom-call | flops 2944401408 | bytes 6291456 | tf_op jit(solution)/shard_map/own/pallas_call | solution.py:233
  18.4 0.0 collective-permute-done.3.refs_2_
  18.4 0.0 collective-permute-done.4.refs_3_
  18.4 0.8 %collective-permute-done.5.refs_0_ = bf16[1,6,104,256]{3,2,1,0:T(8,128)(2,1)S(1)} collective-permute-done((bf16[1,6,104,256]{3,2,1,0:T(8,128)(2,1)S(1)}, bf16[1,6,104,256]{3,2,1,0:T(8,128)(2,1)S(1)}, u32[]{:S(2)}, u32[]{:S(2)}) %collective-permute-start.5) | collective-permute-done | bytes 319520 | tf_op jit(solution)/shard_map/ppermute | solution.py:268
  19.2 0.0 copy-done.6
  19.2 0.1 before.2
  19.3 0.0 copy-start
  19.3 0.0 copy-start.4
  19.3 2.2 %collective-permute-start.11 = (bf16[1,8,104,256]{3,2,1,0:T(8,128)(2,1)S(1)}, bf16[1,8,104,256]{3,2,1,0:T(8,128)(2,1)S(1)}, u32[]{:S(2)}, u32[]{:S(2)}) collective-permute-start(bf16[1,8,104,256]{3,2,1,0:T(8,128)(2,1)S(1)} %get-tuple-element.40.refs_2_.refs_3_.last), channel_id=1, source_target_pairs={{0,4},{4,8},{8,12},{12,16},{16,20},{20,24},{24,28},{28,0},{1,5},{5... | collective-permute-start | bytes 1277960 | tf_op jit(solution)/shard_map/ppermute | solution.py:268
  21.5 1.5 %collective-permute-done.refs_0_ = bf16[1,6,104,256]{3,2,1,0:T(8,128)(2,1)S(1)} collective-permute-done((bf16[1,6,104,256]{3,2,1,0:T(8,128)(2,1)S(1)}, bf16[1,6,104,256]{3,2,1,0:T(8,128)(2,1)S(1)}, u32[]{:S(2)}, u32[]{:S(2)}) %collective-permute-start) | collective-permute-done | bytes 319520 | tf_op jit(solution)/shard_map/ppermute | solution.py:268
  23.0 0.1 earliest.2
  23.1 0.1 collective-permute-start.9
  23.2 1.6 %collective-permute-start.10 = (bf16[2,104,256]{2,1,0:T(8,128)(2,1)S(1)}, bf16[2,104,256]{2,1,0:T(8,128)(2,1)S(1)}, u32[]{:S(2)}, u32[]{:S(2)}) collective-permute-start(bf16[2,104,256]{2,1,0:T(8,128)(2,1)S(1)} %get-tuple-element.42), channel_id=1, source_target_pairs={{0,3},{1,2},{2,1},{3,0},{4,7},{5,6},{6,5},{7,4},{8,11},{9,10},{10,... | collective-permute-start | bytes 319496 | tf_op jit(solution)/shard_map/ppermute | solution.py:258
  24.7 3.9 %collective-permute-start.8 = (bf16[2,104,256]{2,1,0:T(8,128)(2,1)S(1)}, bf16[2,104,256]{2,1,0:T(8,128)(2,1)S(1)}, u32[]{:S(2)}, u32[]{:S(2)}) collective-permute-start(bf16[2,104,256]{2,1,0:T(8,128)(2,1)S(1)} %get-tuple-element.38.refs_4_), channel_id=1, source_target_pairs={{0,4},{4,8},{8,12},{12,16},{16,20},{20,24},{24,28},{28,0},{1,5},{5... | collective-permute-start | bytes 319496 | tf_op jit(solution)/shard_map/ppermute | solution.py:268
  28.6 2.5 %collective-permute-start.7 = (bf16[1,6,104,256]{3,2,1,0:T(8,128)(2,1)S(1)}, bf16[1,6,104,256]{3,2,1,0:T(8,128)(2,1)S(1)}, u32[]{:S(2)}, u32[]{:S(2)}) collective-permute-start(bf16[1,6,104,256]{3,2,1,0:T(8,128)(2,1)S(1)} %get-tuple-element.37), channel_id=1, source_target_pairs={{0,4},{4,8},{8,12},{12,16},{16,20},{20,24},{24,28},{28,0},{1,5},{5... | collective-permute-start | bytes 958472 | tf_op jit(solution)/shard_map/ppermute | solution.py:268
  31.1 0.0 collective-permute-done.9.up._.refs_2_
  31.1 0.0 collective-permute-done.10.down
  31.1 0.0 copy-done
  31.1 0.0 copy-done.4
  31.2 1.5 %last.5.acc_in = f32[832,256]{1,0:T(8,128)S(1)} custom-call(bf16[1,8,104,256]{3,2,1,0:T(8,128)(2,1)S(1)} %get-tuple-element.40.refs_2_.refs_3_.last, bf16[2,104,256]{2,1,0:T(8,128)(2,1)S(1)} %collective-permute-done.9.up._.refs_2_, bf16[2,104,256]{2,1,0:T(8,128)(2,1)S(1)} %collective-permute-done.10.down, bf16[256]{0:T(256)(128)(2,1)S(1)} %copy-done.4, ...), custom_call_target="tpu_custom_call" | custom-call | flops 981467136 | bytes 2097152 | tf_op jit(solution)/shard_map/last/pallas_call | solution.py:233
  32.6 0.5 %collective-permute-done.11.refs_0_.refs_1_ = bf16[1,8,104,256]{3,2,1,0:T(8,128)(2,1)S(1)} collective-permute-done((bf16[1,8,104,256]{3,2,1,0:T(8,128)(2,1)S(1)}, bf16[1,8,104,256]{3,2,1,0:T(8,128)(2,1)S(1)}, u32[]{:S(2)}, u32[]{:S(2)}) %collective-permute-start.11) | collective-permute-done | bytes 426016 | tf_op jit(solution)/shard_map/ppermute | solution.py:268
  33.2 0.1 collective-permute-start.14
  33.2 0.0 copy-start.7
  33.3 3.2 %collective-permute-start.15 = (bf16[1,104,256]{2,1,0:T(8,128)(2,1)S(1)}, bf16[1,104,256]{2,1,0:T(8,128)(2,1)S(1)}, u32[]{:S(2)}, u32[]{:S(2)}) collective-permute-start(bf16[1,104,256]{2,1,0:T(8,128)(2,1)S(1)} %get-tuple-element.47), channel_id=1, source_target_pairs={{0,3},{1,2},{2,1},{3,0},{4,7},{5,6},{6,5},{7,4},{8,11},{9,10},{10,... | collective-permute-start | bytes 159752 | tf_op jit(solution)/shard_map/ppermute | solution.py:258
  36.4 2.4 %first.5 = (f32[832,256]{1,0:T(8,128)S(1)}, f32[832,256]{1,0:T(8,128)S(1)}) custom-call(bf16[1,8,104,256]{3,2,1,0:T(8,128)(2,1)S(1)} %get-tuple-element.39.refs_0_.refs_1_.first, bf16[2,104,256]{2,1,0:T(8,128)(2,1)S(1)} %collective-permute-done.9.up._.refs_2_, bf16[2,104,256]{2,1,0:T(8,128)(2,1)S(1)} %collective-permute-done.10.down, ...), custom_call_target="tpu_custom_call" | custom-call | flops 1962934272 | bytes 4194304 | tf_op jit(solution)/shard_map/first/pallas_call | solution.py:233
  38.8 0.0 collective-permute-done.8.refs_0_.refs_1_
  38.9 0.1 collective-permute-start.12
  39.0 0.0 collective-permute-start.13
  39.0 0.0 collective-permute-done.14.refs_1_
  39.0 0.0 collective-permute-done.15.refs_2_
  39.0 0.0 copy-done.7
  39.0 0.9 %before.3 = (bf16[2,8,104,256]{3,2,1,0:T(8,128)(2,1)}, f32[832,256]{1,0:T(8,128)S(1)}) custom-call(bf16[1,8,104,256]{3,2,1,0:T(8,128)(2,1)S(1)} %collective-permute-done.11.refs_0_.refs_1_, bf16[1,104,256]{2,1,0:T(8,128)(2,1)S(1)} %collective-permute-done.14.refs_1_, bf16[1,104,256]{2,1,0:T(8,128)(2,1)S(1)} %collective-permute-done.15.refs_2_, ...), custom_call_target="tpu_custom_call" | custom-call | flops 1962934272 | bytes 4194304 | tf_op jit(solution)/shard_map/before/pallas_call | solution.py:233
  40.0 2.3 %collective-permute-done.7.refs_0_ = bf16[1,6,104,256]{3,2,1,0:T(8,128)(2,1)S(1)} collective-permute-done((bf16[1,6,104,256]{3,2,1,0:T(8,128)(2,1)S(1)}, bf16[1,6,104,256]{3,2,1,0:T(8,128)(2,1)S(1)}, u32[]{:S(2)}, u32[]{:S(2)}) %collective-permute-start.7) | collective-permute-done | bytes 319520 | tf_op jit(solution)/shard_map/ppermute | solution.py:268
  42.2 0.0 collective-permute-done.12.refs_2_
  42.2 0.3 collective-permute-done.13.refs_3_
  42.6 0.8 %earliest.3 = bf16[2,8,104,256]{3,2,1,0:T(8,128)(2,1)} custom-call(bf16[1,6,104,256]{3,2,1,0:T(8,128)(2,1)S(1)} %collective-permute-done.7.refs_0_, bf16[2,104,256]{2,1,0:T(8,128)(2,1)S(1)} %collective-permute-done.8.refs_0_.refs_1_, bf16[1,104,256]{2,1,0:T(8,128)(2,1)S(1)} %collective-permute-done.12.refs_2_, ...), custom_call_target="tpu_custom_call", output_to_operand_aliasing={{}: (9, {})} | custom-call | flops 981467136 | bytes 2097152 | tf_op jit(solution)/shard_map/earliest/pallas_call | solution.py:233
  (6 shorter events, 0.2 us)
Async XLA Ops:
  0.0 14.9 %copy-start.5 = (bf16[256]{0:T(256)(128)(2,1)S(1)}, bf16[256]{0:T(256)(128)(2,1)}, u32[]{:S(2)}) copy-start(bf16[256]{0:T(256)(128)(2,1)} %refs_4_.4) | copy-start | bytes 1540
  1.0 11.3 %collective-permute-start.1 = (bf16[4,104,256]{2,1,0:T(8,128)(2,1)S(1)}, bf16[4,104,256]{2,1,0:T(8,128)(2,1)S(1)}, u32[]{:S(2)}, u32[]{:S(2)}) collective-permute-start(bf16[4,104,256]{2,1,0:T(8,128)(2,1)S(1)} %bitcast.14), channel_id=1, source_target_pairs={{0,4},{4,8},{8,12},{12,16},{16,20},{20,24},{24,28},{28,0},{1,5},{5... | collective-permute-start | bytes 638984 | tf_op jit(solution)/shard_map/ppermute | solution.py:268
  4.0 1.2 %copy-start.1 = (bf16[2,8,104,256]{3,2,1,0:T(8,128)(2,1)S(1)}, bf16[2,8,104,256]{3,2,1,0:T(8,128)(2,1)}, u32[]{:S(2)}) copy-start(bf16[2,8,104,256]{3,2,1,0:T(8,128)(2,1)} %refs_8_.1) | copy-start | bytes 2555908
  5.1 1.8 %copy-start.2 = (bf16[2,8,104,256]{3,2,1,0:T(8,128)(2,1)S(1)}, bf16[2,8,104,256]{3,2,1,0:T(8,128)(2,1)}, u32[]{:S(2)}) copy-start(bf16[2,8,104,256]{3,2,1,0:T(8,128)(2,1)} %refs_8_.1) | copy-start | bytes 2555908
  5.1 9.8 %copy-start.3 = (bf16[3,3,3,256,256]{4,3,2,1,0:T(8,128)(2,1)S(1)}, bf16[3,3,3,256,256]{4,3,2,1,0:T(8,128)(2,1)}, u32[]{:S(2)}) copy-start(bf16[3,3,3,256,256]{4,3,2,1,0:T(8,128)(2,1)} %param.9) | copy-start | bytes 10616836
  5.1 6.8 %collective-permute-start.2 = (bf16[2,104,256]{2,1,0:T(8,128)(2,1)S(1)}, bf16[2,104,256]{2,1,0:T(8,128)(2,1)S(1)}, u32[]{:S(2)}, u32[]{:S(2)}) collective-permute-start(bf16[2,104,256]{2,1,0:T(8,128)(2,1)S(1)} %get-tuple-element.28._), channel_id=1, source_target_pairs={{0,1},{1,0},{2,3},{3,2},{4,5},{5,4},{6,7},{7,6},{8,9},{9,8},{10,11... | collective-permute-start | bytes 319496 | tf_op jit(solution)/shard_map/ppermute | solution.py:259
  5.2 9.6 %collective-permute-start.6 = (bf16[2,104,256]{2,1,0:T(8,128)(2,1)S(1)}, bf16[2,104,256]{2,1,0:T(8,128)(2,1)S(1)}, u32[]{:S(2)}, u32[]{:S(2)}) collective-permute-start(bf16[2,104,256]{2,1,0:T(8,128)(2,1)S(1)} %get-tuple-element.33), channel_id=1, source_target_pairs={{0,3},{1,2},{2,1},{3,0},{4,7},{5,6},{6,5},{7,4},{8,11},{9,10},{10,... | collective-permute-start | bytes 319496 | tf_op jit(solution)/shard_map/ppermute | solution.py:258
  6.9 12.3 %collective-permute-start.5 = (bf16[1,6,104,256]{3,2,1,0:T(8,128)(2,1)S(1)}, bf16[1,6,104,256]{3,2,1,0:T(8,128)(2,1)S(1)}, u32[]{:S(2)}, u32[]{:S(2)}) collective-permute-start(bf16[1,6,104,256]{3,2,1,0:T(8,128)(2,1)S(1)} %get-tuple-element.32), channel_id=1, source_target_pairs={{0,4},{4,8},{8,12},{12,16},{16,20},{20,24},{24,28},{28,0},{1,5},{5... | collective-permute-start | bytes 958472 | tf_op jit(solution)/shard_map/ppermute | solution.py:268
  8.5 14.4 %collective-permute-start = (bf16[1,6,104,256]{3,2,1,0:T(8,128)(2,1)S(1)}, bf16[1,6,104,256]{3,2,1,0:T(8,128)(2,1)S(1)}, u32[]{:S(2)}, u32[]{:S(2)}) collective-permute-start(bf16[1,6,104,256]{3,2,1,0:T(8,128)(2,1)S(1)} %get-tuple-element.29), channel_id=1, source_target_pairs={{0,4},{4,8},{8,12},{12,16},{16,20},{20,24},{24,28},{1,5},{5,9},{9,... | collective-permute-start | bytes 958472 | tf_op jit(solution)/shard_map/ppermute | solution.py:268
  12.3 6.1 %collective-permute-start.3 = (bf16[2,104,256]{2,1,0:T(8,128)(2,1)S(1)}, bf16[2,104,256]{2,1,0:T(8,128)(2,1)S(1)}, u32[]{:S(2)}, u32[]{:S(2)}) collective-permute-start(bf16[2,104,256]{2,1,0:T(8,128)(2,1)S(1)} %get-tuple-element.30._), channel_id=1, source_target_pairs={{0,1},{1,0},{2,3},{3,2},{4,5},{5,4},{6,7},{7,6},{8,9},{9,8},{10,11... | collective-permute-start | bytes 319496 | tf_op jit(solution)/shard_map/ppermute | solution.py:259
  12.4 6.0 %collective-permute-start.4 = (bf16[2,104,256]{2,1,0:T(8,128)(2,1)S(1)}, bf16[2,104,256]{2,1,0:T(8,128)(2,1)S(1)}, u32[]{:S(2)}, u32[]{:S(2)}) collective-permute-start(bf16[2,104,256]{2,1,0:T(8,128)(2,1)S(1)} %get-tuple-element.31), channel_id=1, source_target_pairs={{0,3},{1,2},{2,1},{3,0},{4,7},{5,6},{6,5},{7,4},{8,11},{9,10},{10,... | collective-permute-start | bytes 319496 | tf_op jit(solution)/shard_map/ppermute | solution.py:258
  14.9 4.3 %copy-start.6 = (bf16[256]{0:T(256)(128)(2,1)S(1)}, bf16[256]{0:T(256)(128)(2,1)}, u32[]{:S(2)}) copy-start(bf16[256]{0:T(256)(128)(2,1)} %refs_6_.3) | copy-start | bytes 1540
  19.3 11.9 %copy-start = (bf16[3,3,3,256,256]{4,3,2,1,0:T(8,128)(2,1)S(1)}, bf16[3,3,3,256,256]{4,3,2,1,0:T(8,128)(2,1)}, u32[]{:S(2)}) copy-start(bf16[3,3,3,256,256]{4,3,2,1,0:T(8,128)(2,1)} %param.12) | copy-start | bytes 10616836
  19.3 11.9 %copy-start.4 = (bf16[256]{0:T(256)(128)(2,1)S(1)}, bf16[256]{0:T(256)(128)(2,1)}, u32[]{:S(2)}) copy-start(bf16[256]{0:T(256)(128)(2,1)} %refs_4_.5) | copy-start | bytes 1540
  19.3 13.8 %collective-permute-start.11 = (bf16[1,8,104,256]{3,2,1,0:T(8,128)(2,1)S(1)}, bf16[1,8,104,256]{3,2,1,0:T(8,128)(2,1)S(1)}, u32[]{:S(2)}, u32[]{:S(2)}) collective-permute-start(bf16[1,8,104,256]{3,2,1,0:T(8,128)(2,1)S(1)} %get-tuple-element.40.refs_2_.refs_3_.last), channel_id=1, source_target_pairs={{0,4},{4,8},{8,12},{12,16},{16,20},{20,24},{24,28},{28,0},{1,5},{5... | collective-permute-start | bytes 1277960 | tf_op jit(solution)/shard_map/ppermute | solution.py:268
  23.1 8.0 %collective-permute-start.9 = (bf16[2,104,256]{2,1,0:T(8,128)(2,1)S(1)}, bf16[2,104,256]{2,1,0:T(8,128)(2,1)S(1)}, u32[]{:S(2)}, u32[]{:S(2)}) collective-permute-start(bf16[2,104,256]{2,1,0:T(8,128)(2,1)S(1)} %get-tuple-element.41), channel_id=1, source_target_pairs={{0,1},{1,0},{2,3},{3,2},{4,5},{5,4},{6,7},{7,6},{8,9},{9,8},{10,11... | collective-permute-start | bytes 319496 | tf_op jit(solution)/shard_map/ppermute | solution.py:259
  23.2 8.0 %collective-permute-start.10 = (bf16[2,104,256]{2,1,0:T(8,128)(2,1)S(1)}, bf16[2,104,256]{2,1,0:T(8,128)(2,1)S(1)}, u32[]{:S(2)}, u32[]{:S(2)}) collective-permute-start(bf16[2,104,256]{2,1,0:T(8,128)(2,1)S(1)} %get-tuple-element.42), channel_id=1, source_target_pairs={{0,3},{1,2},{2,1},{3,0},{4,7},{5,6},{6,5},{7,4},{8,11},{9,10},{10,... | collective-permute-start | bytes 319496 | tf_op jit(solution)/shard_map/ppermute | solution.py:258
  24.7 14.1 %collective-permute-start.8 = (bf16[2,104,256]{2,1,0:T(8,128)(2,1)S(1)}, bf16[2,104,256]{2,1,0:T(8,128)(2,1)S(1)}, u32[]{:S(2)}, u32[]{:S(2)}) collective-permute-start(bf16[2,104,256]{2,1,0:T(8,128)(2,1)S(1)} %get-tuple-element.38.refs_4_), channel_id=1, source_target_pairs={{0,4},{4,8},{8,12},{12,16},{16,20},{20,24},{24,28},{28,0},{1,5},{5... | collective-permute-start | bytes 319496 | tf_op jit(solution)/shard_map/ppermute | solution.py:268
  28.6 13.6 %collective-permute-start.7 = (bf16[1,6,104,256]{3,2,1,0:T(8,128)(2,1)S(1)}, bf16[1,6,104,256]{3,2,1,0:T(8,128)(2,1)S(1)}, u32[]{:S(2)}, u32[]{:S(2)}) collective-permute-start(bf16[1,6,104,256]{3,2,1,0:T(8,128)(2,1)S(1)} %get-tuple-element.37), channel_id=1, source_target_pairs={{0,4},{4,8},{8,12},{12,16},{16,20},{20,24},{24,28},{28,0},{1,5},{5... | collective-permute-start | bytes 958472 | tf_op jit(solution)/shard_map/ppermute | solution.py:268
  33.2 5.8 %collective-permute-start.14 = (bf16[1,104,256]{2,1,0:T(8,128)(2,1)S(1)}, bf16[1,104,256]{2,1,0:T(8,128)(2,1)S(1)}, u32[]{:S(2)}, u32[]{:S(2)}) collective-permute-start(bf16[1,104,256]{2,1,0:T(8,128)(2,1)S(1)} %get-tuple-element.43._), channel_id=1, source_target_pairs={{0,1},{1,0},{2,3},{3,2},{4,5},{5,4},{6,7},{7,6},{8,9},{9,8},{10,11... | collective-permute-start | bytes 159752 | tf_op jit(solution)/shard_map/ppermute | solution.py:259
  33.2 5.8 %copy-start.7 = (bf16[256]{0:T(256)(128)(2,1)S(1)}, bf16[256]{0:T(256)(128)(2,1)}, u32[]{:S(2)}) copy-start(bf16[256]{0:T(256)(128)(2,1)} %refs_6_.5) | copy-start | bytes 1540
  33.3 5.8 %collective-permute-start.15 = (bf16[1,104,256]{2,1,0:T(8,128)(2,1)S(1)}, bf16[1,104,256]{2,1,0:T(8,128)(2,1)S(1)}, u32[]{:S(2)}, u32[]{:S(2)}) collective-permute-start(bf16[1,104,256]{2,1,0:T(8,128)(2,1)S(1)} %get-tuple-element.47), channel_id=1, source_target_pairs={{0,3},{1,2},{2,1},{3,0},{4,7},{5,6},{6,5},{7,4},{8,11},{9,10},{10,... | collective-permute-start | bytes 159752 | tf_op jit(solution)/shard_map/ppermute | solution.py:258
  38.9 3.4 %collective-permute-start.12 = (bf16[1,104,256]{2,1,0:T(8,128)(2,1)S(1)}, bf16[1,104,256]{2,1,0:T(8,128)(2,1)S(1)}, u32[]{:S(2)}, u32[]{:S(2)}) collective-permute-start(bf16[1,104,256]{2,1,0:T(8,128)(2,1)S(1)} %get-tuple-element.45), channel_id=1, source_target_pairs={{0,1},{1,0},{2,3},{3,2},{4,5},{5,4},{6,7},{7,6},{8,9},{9,8},{10,11... | collective-permute-start | bytes 159752 | tf_op jit(solution)/shard_map/ppermute | solution.py:259
  39.0 3.6 %collective-permute-start.13 = (bf16[1,104,256]{2,1,0:T(8,128)(2,1)S(1)}, bf16[1,104,256]{2,1,0:T(8,128)(2,1)S(1)}, u32[]{:S(2)}, u32[]{:S(2)}) collective-permute-start(bf16[1,104,256]{2,1,0:T(8,128)(2,1)S(1)} %get-tuple-element.46), channel_id=1, source_target_pairs={{0,3},{1,2},{2,1},{3,0},{4,7},{5,6},{6,5},{7,4},{8,11},{9,10},{10,... | collective-permute-start | bytes 159752 | tf_op jit(solution)/shard_map/ppermute | solution.py:258

commit v6 on v5

--- a/solution.py
+++ b/solution.py
@@ -17,20 +17,29 @@
     return [(i, (i + step) % peers) for i in range(peers)]
 
 
+def activate(row, gain, mask):
+    cells = row.shape[0]
+    values = row.astype(F32)
+    mean_power = jnp.mean(values * values, axis=-1, keepdims=True)
+    normed = values * lax.rsqrt(mean_power + EPSILON) * gain
+    act = normed / (1.0 + jnp.exp(-normed))
+    if mask is not None:
+        act = act * mask
+    cell = lax.broadcasted_iota(jnp.int32, act.shape, 0)
+    left = jnp.where(cell == 0, 0.0, pltpu.roll(act, 1, 0))
+    right = jnp.where(cell == cells - 1, 0.0, pltpu.roll(act, cells - 1, 0))
+    return left, act, right
+
+
 def activate_rows(get_row, gain, shifts, rows, cells):
     for r in range(rows):
         values, mask = get_row(r)
         here = slice(r * cells, (r + 1) * cells)
-        values = values.astype(F32)
-        mean_power = jnp.mean(values * values, axis=-1, keepdims=True)
-        normed = values * lax.rsqrt(mean_power + EPSILON) * gain
-        act = normed / (1.0 + jnp.exp(-normed))
-        if mask is not None:
-            act = act * mask
-        cell = lax.broadcasted_iota(jnp.int32, act.shape, 0)
-        shifts[0, here, :] = jnp.where(cell == 0, 0.0, pltpu.roll(act, 1, 0))
-        shifts[1, here, :] = act
-        shifts[2, here, :] = jnp.where(cell == cells - 1, 0.0, pltpu.roll(act, cells - 1, 0))
+        if values is None:
+            shifts[:, here, :] = jnp.zeros((3, cells, shifts.shape[-1]), F32)
+            continue
+        for l, value in enumerate(activate(values, gain, mask)):
+            shifts[l, here, :] = value
 
 
 def pack(shifts, even, odd, rows, cells):
@@ -71,6 +80,8 @@
     lower = lax.axis_index("height") % 2 == 0
 
     def get_row(r):
+        if inward is None and r in (0, rows + 1):
+            return None, None
         if r == 0:
             return jnp.where(lower, outward, inward), above
         if r == rows + 1:
@@ -102,21 +113,28 @@
         acc_first[s : s + n] = taps(even, odd, k2, s, n, cells)
 
 
-def own_last_kernel(last, up, down, gain, k2, _, acc_last, *bufs):
+def own_last_kernel(last, gain, k2, acc_last, *bufs):
     rows, cells = last.shape[1], last.shape[2]
     even, odd = bufs[1:]
-    load_frame(last.at[0], up[0], down[0], gain, bufs)
+    load_frame(last.at[0], None, None, gain, bufs)
     for s, n in chunks(rows, cells):
         acc_last[s : s + n] = taps(even, odd, k2, s, n, cells)
 
 
-def own_first_kernel(first, up, down, gain, k1, k2, acc_in, _, acc_first, acc_last, *bufs):
+def own_first_kernel(first, up, down, last_up, last_down, gain, k1, k2, acc_in, _, acc_first, acc_last, *bufs):
     rows, cells = first.shape[1], first.shape[2]
     even, odd = bufs[1:]
     load_frame(first.at[0], up[0], down[0], gain, bufs)
     for s, n in chunks(rows, cells):
         acc_last[s : s + n] = acc_in[s : s + n] + taps(even, odd, k1, s, n, cells)
         acc_first[s : s + n] = taps(even, odd, k2, s, n, cells)
+    lower = lax.axis_index("height") % 2 == 0
+    weight = gain[...].astype(F32)[None]
+    for edge, mask in enumerate(masks()):
+        pair = (last_down[0], last_up[0]) if edge == 0 else (last_up[0], last_down[0])
+        row = jnp.concatenate(activate(jnp.where(lower, *pair), weight, mask), axis=1).astype(BF16)
+        here = slice(0, cells) if edge == 0 else slice((rows - 1) * cells, rows * cells)
+        acc_last[here] += jnp.dot(row, k2[0, 2 * edge], preferred_element_type=F32)
 
 
 def finish(total, bias, s, n, cells):
@@ -185,12 +203,7 @@
         result.wait(chunks(rows, cells))
 
 
-def earliest_kernel(residual, *refs):
-    if residual:
-        frame, edges, up, down, gain, k0, bias, acc_first, latents, _, out, *bufs, new, sems = refs
-        result = Result(latents, out, 0, new, sems)
-    else:
-        frame, edges, up, down, gain, k0, bias, acc_first, out, inner, edges_out, *bufs = refs
+def earliest_kernel(frame, edges, up, down, gain, k0, bias, acc_first, _, out, *bufs):
     cells = up.shape[1]
     rows = acc_first.shape[0] // cells
     even, odd = bufs[1:]
@@ -199,22 +212,60 @@
     def _(there):
         if there:
             load_frame(frame.at[0], up[0], down[0], gain, bufs, edges)
-        for s, n in chunks(rows, cells, residual):
+        for s, n in chunks(rows, cells):
             total = acc_first[s : s + n]
             if there:
                 total = total + taps(even, odd, k0, s, n, cells)
-            if residual:
-                result.finish(total, bias, s, n, cells)
-            else:
-                r, value = finish(total, bias, s, n, cells)
-                out[0, r] = value.astype(BF16)
-
-    if residual:
-        result.wait(chunks(rows, cells, True))
-    else:
-        edges_out[0] = out[0, 0]
-        edges_out[1] = out[0, rows - 1]
-        inner[0] = out[0, 1 : rows - 1]
+            r, value = finish(total, bias, s, n, cells)
+            out[0, r] = value.astype(BF16)
+
+
+def ahead_kernel(frame, gain, k0, inner, edge_acc, *bufs):
+    rows, cells = frame.shape[1], frame.shape[2]
+    even, odd = bufs[1:]
+    load_frame(frame.at[0], None, None, gain, bufs)
+    for s, n in chunks(rows, cells):
+        total = taps(even, odd, k0, s, n, cells)
+        value = total.reshape(n // cells, cells, -1).astype(BF16)
+        first = s // cells
+        low, high = max(first, 1), min(first + n // cells, rows - 1)
+        inner[0, low - 1 : high - 1] = value[low - first : high - first]
+        if s == 0:
+            edge_acc[0] = total[:cells]
+        if s + n == rows * cells:
+            edge_acc[1] = total[n - cells :]
+
+
+def edges_kernel(inward, outward, gain, k0, edge_acc, _, edges, columns):
+    lower = lax.axis_index("height") % 2 == 0
+    weight = gain[...].astype(F32)[None]
+    for edge, mask in enumerate(masks()):
+        pair = (outward[0], inward[0]) if edge == 0 else (inward[0], outward[0])
+        for l, value in enumerate(activate(jnp.where(lower, *pair), weight, mask)):
+            size = value.shape[-1]
+            columns[:, l * size : (l + 1) * size] = value.astype(BF16)
+        add = jnp.dot(columns[...], k0[0, 2 * edge], preferred_element_type=F32)
+        edges[edge] = (edge_acc[edge] + add).astype(BF16)
+
+
+def received(value):
+    return jnp.where(lax.axis_index("tm") > 0, value.astype(F32), 0.0)
+
+
+def sum_kernel(inner, edges, acc_first, bias, residual, _, out, rows, sems):
+    count, cells = residual.shape[1], residual.shape[2]
+    copies = []
+    for n in range(2):
+        low, high = n * (count // 2), (n + 1) * (count // 2)
+        for r in range(low, high):
+            ahead = edges[0 if r == 0 else 1] if r in (0, count - 1) else inner[0, r - 1]
+            total = acc_first[r * cells : (r + 1) * cells] + bias[...].astype(F32)[None] + received(ahead)
+            rows[r] = (residual[0, r].astype(F32) + total).astype(BF16)
+        half = pl.ds(low, count // 2)
+        copies.append(pltpu.make_async_copy(rows.at[half], out.at[0, half], sems.at[n]))
+        copies[-1].start()
+    for copy in copies:
+        copy.wait()
 
 
 def whole(shape):
@@ -225,27 +276,27 @@
     return pl.BlockSpec((1, *shape[1:]), lambda i: (index,) + (0,) * (len(shape) - 1))
 
 
-def call(body, name, units, out_specs, out_shape, args, aliases=None, extra=()):
+def call(body, name, units, out_specs, out_shape, args, aliases=None, scratch=None, limit=VMEM_LIMIT):
     rows, cells, channels = call.block
     flat = (rows + 2) * cells
     arrays = [a for a, _ in args]
-    flops = units * 2 * rows * cells * 9 * channels * channels
+    flops = int(units * 2 * rows * cells * 9 * channels * channels)
     return pl.pallas_call(
         body,
         grid=(1,),
         in_specs=[s for _, s in args],
         out_specs=out_specs,
         out_shape=out_shape,
-        scratch_shapes=[
+        scratch_shapes=scratch
+        or [
             pltpu.VMEM((3, flat, channels), F32),
             pltpu.VMEM((flat, 3 * channels), BF16),
             pltpu.VMEM((flat - 2 * cells, 3 * channels), BF16),
-            *extra,
         ],
         input_output_aliases=aliases or {},
-        compiler_params=pltpu.CompilerParams(vmem_limit_bytes=VMEM_LIMIT),
+        compiler_params=pltpu.CompilerParams(vmem_limit_bytes=limit),
         cost_estimate=pl.CostEstimate(
-            flops=flops, bytes_accessed=units * 2**21, transcendentals=2 * flat * channels
+            flops=flops, bytes_accessed=int(units * 2**21), transcendentals=2 * flat * channels
         ),
         name=name,
     )(*arrays)
@@ -266,6 +317,10 @@
 def shift(array, closed=True):
     route = ring("tm", 1)
     return lax.ppermute(array, "tm", route if closed else route[:-1])
+
+
+def rest(array):
+    return array, pl.BlockSpec(memory_space=pl.ANY)
 
 
 def shapes():
@@ -283,12 +338,15 @@
     return call(own_kernel, "own", 3, [whole(acc.shape)] * 2, [acc, acc], args)
 
 
-def own_apart(last, first, up, down, gain, k, early, late):
+def own_last(last, gain, k):
+    acc = shapes()[0]
+    return call(own_last_kernel, "last", 1, [whole(acc.shape)], [acc], [last, gain, k[2]])[0]
+
+
+def own_first(first, up, down, gain, k, acc_last, token):
     acc = shapes()[0]
     up, down = pairs(up, 1), pairs(down, 1)
-    args = [last, up[1], down[1], gain, k[2], (early, pl.BlockSpec(memory_space=pl.ANY))]
-    acc_last = call(own_last_kernel, "last", 1, [whole(acc.shape)], [acc], args)[0]
-    args = [first, up[0], down[0], gain, k[1], k[2], w(acc_last), (late, pl.BlockSpec(memory_space=pl.ANY))]
+    args = [first, up[0], down[0], up[1], down[1], gain, k[1], k[2], w(acc_last), rest(token)]
     return call(own_first_kernel, "first", 2, [whole(acc.shape)] * 2, [acc, acc], args)
 
 
@@ -354,7 +412,7 @@
     ]
 
 
-def first_section(latents, gain, kernel, bias):
+def first_section(latents, gain, kernel, bias, ahead):
     bottom = latents.shape[1] - 1
     acc, frame, inner, edge = shapes()
     k = [(kernel, part(kernel.shape, i)) for i in range(3)]
@@ -380,35 +438,49 @@
         outs,
         [w(before), edges[1], up[0], down[0], gain, k[0], k[1], bias, w(acc_first), w(acc_last)],
     )
-    outs = [frame, inner, edge]
-    y_first, inner_first, edge_first = call(
-        functools.partial(earliest_kernel, False),
+    second_last = ahead(y_last)
+    outs = [frame]
+    (y_first,) = call(
+        earliest_kernel,
         "earliest",
         1,
         [whole(o.shape) for o in outs],
         outs,
-        [w(earliest), edges[0], up[1], down[1], gain, k[0], bias, w(acc_first)],
+        [w(earliest), edges[0], up[1], down[1], gain, k[0], bias, w(acc_first), rest(second_last)],
     )
-    return y_last, y_first, inner_first, edge_first
+    return y_last, y_first, second_last
 
 
 def second_section(results, latents, gain, kernel, bias):
-    y_last, y_first, inner_first, edge_first = results
-    bottom = latents.shape[1] - 1
-    acc = shapes()[0]
+    y_last, y_first, acc_last = results
+    rows, cells, channels = latents.shape[1:]
+    bottom = rows - 1
+    acc, _, inner, edge = shapes()
     k = [(kernel, part(kernel.shape, i)) for i in range(3)]
     before = shift(y_last)
-    edges = shift(edge_first)
-    earliest = shift(inner_first)
-    up, down = exchange_rows(
-        *rows_after(edge_first, (y_first, (0, 0), (0, bottom)), (y_last, (0, 0), (0, bottom)))
+    frames = [(y, (0, 0), (0, bottom)) for y in (y_first, y_last)]
+    up, down = exchange_rows(*rows_after(None, *frames))
+    outs = [inner, jax.ShapeDtypeStruct(edge.shape, F32)]
+    inner_ahead, edge_acc = call(
+        ahead_kernel, "ahead", 1, [whole(o.shape) for o in outs], outs, [w(y_first), gain, k[0]]
     )
+    inner_ahead = shift(inner_ahead)
+    args = [pairs(up, 1)[0], pairs(down, 1)[0], gain, k[0], w(edge_acc), rest(acc_last)]
+    columns = [pltpu.VMEM((cells, 3 * channels), BF16)]
+    (edges_ahead,) = call(edges_kernel, "ends", 0, [whole(edge.shape)], [edge], args, scratch=columns)
+    edges_ahead = shift(edges_ahead, False)
     sides = rows_after(up, (before, (0, 0), (0, bottom)))
-    acc_first, acc_last = own_apart(w(y_last), w(y_first), up, down, gain, k, up, sides[0])
+    acc_first, acc_last = own_first(w(y_first), up, down, gain, k, acc_last, sides[0])
 
     out = jax.ShapeDtypeStruct(latents.shape, BF16)
     anywhere = pl.BlockSpec(memory_space=pl.ANY)
-    extra = [pltpu.VMEM(latents.shape[1:], BF16), pltpu.SemaphoreType.DMA((len(chunks(*latents.shape[1:3], True)),))]
+    extra = [pltpu.VMEM(latents.shape[1:], BF16), pltpu.SemaphoreType.DMA((2,))]
+    flat = (rows + 2) * cells
+    scratch = [
+        pltpu.VMEM((3, flat, channels), F32),
+        pltpu.VMEM((flat, 3 * channels), BF16),
+        pltpu.VMEM((flat - 2 * cells, 3 * channels), BF16),
+    ]
     args = [w(before), *map(w, exchange_rows(*sides)), gain, k[0], k[1], bias, w(acc_first), w(acc_last)]
     args.append((latents, part(latents.shape, 1)))
     half, acc_first = call(
@@ -418,13 +490,10 @@
         [anywhere, whole(acc.shape)],
         [out, acc],
         args,
-        extra=extra,
+        scratch=scratch + extra,
     )
-    sides = rows_after(acc_last, (edges, (0,), (1,)))
-    args = [w(earliest), w(edges), *map(w, exchange_rows(*sides)), gain, k[0], bias, w(acc_first)]
-    args += [(latents, part(latents.shape, 0)), (half, anywhere)]
-    body = functools.partial(earliest_kernel, True)
-    return call(body, "earliest", 1, anywhere, out, args, {len(args) - 1: 0}, extra)
+    args = [w(inner_ahead), w(edges_ahead), w(acc_first), bias, (latents, part(latents.shape, 0)), rest(half)]
+    return call(sum_kernel, "sum", 0, anywhere, out, args, {len(args) - 1: 0}, extra, 12 * 2**20)
 
 
 def per_device(
@@ -437,8 +506,14 @@
         return kernel.reshape(3, 3, 3 * channels, channels)
 
     first_gain, first_bias, second_gain, second_bias = map(w, (first_gain, first_bias, second_gain, second_bias))
-    results = first_section(latents, first_gain, columns(first_kernel), first_bias)
-    return second_section(results, latents, second_gain, columns(second_kernel), second_bias)
+    second_kernel = columns(second_kernel)
+    k = [(second_kernel, part(second_kernel.shape, i)) for i in range(3)]
+
+    def ahead(y_last):
+        return own_last(w(y_last), second_gain, k)
+
+    results = first_section(latents, first_gain, columns(first_kernel), first_bias, ahead)
+    return second_section(results, latents, second_gain, second_kernel, second_bias)
 
 
 def solution(mesh):

time: 43.7 us -> 42.6 us (0.975)
  waiting for transfers between devices: 5.73 us -> 3.37 us
  Pallas kernels: 9.34 us -> 11.2 us
  starting transfers between devices: 25.9 us -> 25.3 us
    ppermute x5 -> x4, starting transfers between devices: 8.91 us -> 3.85 us  [exchange_rows(): outward = lax.ppermute(outward, 'height', others)]
    ppermute x6, waiting for transfers between devices: 5.39 us -> 2.68 us  [shift(): return lax.ppermute(array, 'tm', route if closed else route[:-1])]
    ppermute x5 -> x4, starting transfers between devices: 0.42 us -> 2.71 us  [exchange_rows(): return (lax.ppermute(inward, 'height', pairs), outward)]
    ppermute x6, starting transfers between devices: 16.6 us -> 18.7 us  [shift(): return lax.ppermute(array, 'tm', route if closed else route[:-1])]
    pallas_call x7 -> x9, Pallas kernels: 9.18 us -> 11.1 us  [call(): pl.pallas_call(body, grid=(1,), in_specs=[s for _, s in args], out_specs=...]
  transfers between devices with their start and end apart: 16 -> 14, of which waited for: 6 -> 6; matrix products, arithmetic and copies ran while one was open for 0% -> 0% of each run, Pallas kernels for 20% -> 24%
where the time goes in v6:
time: 42.6 us; the launch traced here: 42.4 us
  starting transfers between devices  25.3 us (59%)
  Pallas kernels  11.2 us (26%)
  waiting for transfers between devices  3.37 us (8%)
  local copies, waits for them, and re-layouts  2.14 us (5%)
    ppermute x6, starting transfers between devices, shift(): return lax.ppermute(array, 'tm', route if closed else route[:-1])  18.7 us
    pallas_call x9, Pallas kernels, call(): pl.pallas_call(body, grid=(1,), in_specs=[s for _, s in args], out_specs=...  11.1 us
    ppermute x4, starting transfers between devices, exchange_rows(): outward = lax.ppermute(outward, 'height', others)  3.85 us
    ppermute x4, starting transfers between devices, exchange_rows(): return (lax.ppermute(inward, 'height', pairs), outward)  2.71 us
    ppermute x6, waiting for transfers between devices, shift(): return lax.ppermute(array, 'tm', route if closed else route[:-1])  2.68 us
    unnamed x16, local copies, waits for them, and re-layouts  1.18 us
    slice x1, local copies, waits for them, and re-layouts, first_section(): edges = latents[:, ::bottom].reshape(4, *latents.shape[2:])  0.96 us
  transfers between devices with their start and end apart: 14, of which 6 were waited for; matrix products, arithmetic and copies ran while one was open for 0% of the time, Pallas kernels for 24%

profile of v6, /device:TPU:0, one launch (start us, length us, event | category | flops | bytes accessed | tf_op | source)
XLA Modules:
  0.0 42.4 jit_solution(2754592975655329381)
XLA Ops:
  0.0 0.0 copy-start.6
  0.0 1.0 %slice.3 = bf16[2,2,104,256]{3,2,1,0:T(8,128)(2,1)S(1)} slice(bf16[2,8,104,256]{3,2,1,0:T(8,128)(2,1)} %residual.1), slice={[0:2:1], [0:8:7], [0:104:1], [0:256:1]} | slice | bytes 425984 | tf_op jit(solution)/shard_map/slice | solution.py:421
  1.0 3.0 %collective-permute-start.1 = (bf16[4,104,256]{2,1,0:T(8,128)(2,1)S(1)}, bf16[4,104,256]{2,1,0:T(8,128)(2,1)S(1)}, u32[]{:S(2)}, u32[]{:S(2)}) collective-permute-start(bf16[4,104,256]{2,1,0:T(8,128)(2,1)S(1)} %bitcast.15), channel_id=1, source_target_pairs={{0,4},{4,8},{8,12},{12,16},{16,20},{20,24},{24,28},{28,0},{1,5},{5... | collective-permute-start | bytes 638984 | tf_op jit(solution)/shard_map/ppermute | solution.py:319
  4.0 0.0 copy-start.1
  4.0 1.2 %copy-done.1 = bf16[2,8,104,256]{3,2,1,0:T(8,128)(2,1)S(1)} copy-done((bf16[2,8,104,256]{3,2,1,0:T(8,128)(2,1)S(1)}, bf16[2,8,104,256]{3,2,1,0:T(8,128)(2,1)}, u32[]{:S(2)}) %copy-start.1) | copy-done | bytes 851992
  5.1 0.0 copy-start.2
  5.1 0.0 copy-start.3
  5.1 0.1 collective-permute-start.2
  5.2 1.6 %collective-permute-start.6 = (bf16[2,104,256]{2,1,0:T(8,128)(2,1)S(1)}, bf16[2,104,256]{2,1,0:T(8,128)(2,1)S(1)}, u32[]{:S(2)}, u32[]{:S(2)}) collective-permute-start(bf16[2,104,256]{2,1,0:T(8,128)(2,1)S(1)} %get-tuple-element.30), channel_id=1, source_target_pairs={{0,3},{1,2},{2,1},{3,0},{4,7},{5,6},{6,5},{7,4},{8,11},{9,10},{10,... | collective-permute-start | bytes 319496 | tf_op jit(solution)/shard_map/ppermute | solution.py:309
  6.9 0.0 copy-done.2
  6.9 1.6 %collective-permute-start.5 = (bf16[1,6,104,256]{3,2,1,0:T(8,128)(2,1)S(1)}, bf16[1,6,104,256]{3,2,1,0:T(8,128)(2,1)S(1)}, u32[]{:S(2)}, u32[]{:S(2)}) collective-permute-start(bf16[1,6,104,256]{3,2,1,0:T(8,128)(2,1)S(1)} %get-tuple-element.29), channel_id=1, source_target_pairs={{0,4},{4,8},{8,12},{12,16},{16,20},{20,24},{24,28},{28,0},{1,5},{5... | collective-permute-start | bytes 958472 | tf_op jit(solution)/shard_map/ppermute | solution.py:319
  8.5 3.4 %collective-permute-start = (bf16[1,6,104,256]{3,2,1,0:T(8,128)(2,1)S(1)}, bf16[1,6,104,256]{3,2,1,0:T(8,128)(2,1)S(1)}, u32[]{:S(2)}, u32[]{:S(2)}) collective-permute-start(bf16[1,6,104,256]{3,2,1,0:T(8,128)(2,1)S(1)} %get-tuple-element.26), channel_id=1, source_target_pairs={{0,4},{4,8},{8,12},{12,16},{16,20},{20,24},{24,28},{1,5},{5,9},{9,... | collective-permute-start | bytes 958472 | tf_op jit(solution)/shard_map/ppermute | solution.py:319
  11.9 0.0 collective-permute-done.2.refs_4_.up
  11.9 0.3 collective-permute-done.1.refs_0_.refs_1_.refs_2_.refs_3_.edges
  12.3 0.3 collective-permute-start.4
  12.5 2.3 %collective-permute-start.3 = (bf16[2,104,256]{2,1,0:T(8,128)(2,1)S(1)}, bf16[2,104,256]{2,1,0:T(8,128)(2,1)S(1)}, u32[]{:S(2)}, u32[]{:S(2)}) collective-permute-start(bf16[2,104,256]{2,1,0:T(8,128)(2,1)S(1)} %get-tuple-element.27._), channel_id=1, source_target_pairs={{0,1},{1,0},{2,3},{3,2},{4,5},{5,4},{6,7},{7,6},{8,9},{9,8},{10,11... | collective-permute-start | bytes 319496 | tf_op jit(solution)/shard_map/ppermute | solution.py:310
  14.9 0.0 collective-permute-done.6.down
  14.9 0.0 copy-done.6
  14.9 0.0 copy-done.3
  14.9 0.0 copy-start.7
  14.9 3.5 %own.1 = (f32[832,256]{1,0:T(8,128)S(1)}, f32[832,256]{1,0:T(8,128)S(1)}) custom-call(bf16[2,8,104,256]{3,2,1,0:T(8,128)(2,1)S(1)} %copy-done.2, bf16[2,8,104,256]{3,2,1,0:T(8,128)(2,1)S(1)} %copy-done.2, bf16[2,104,256]{2,1,0:T(8,128)(2,1)S(1)} %collective-permute-done.2.refs_4_.up, bf16[2,104,256]{2,1,0:T(8,128)(2,1)S(1)} %collective-permute-done.6.down, ...), custom_call_target="tpu_custom_call" | custom-call | flops 2944401408 | bytes 6291456 | tf_op jit(solution)/shard_map/own/pallas_call | solution.py:284
  18.3 0.0 collective-permute-done.4.refs_3_.down
  18.4 0.0 collective-permute-done.3.refs_2_.up
  18.4 0.8 %collective-permute-done.5.refs_0_ = bf16[1,6,104,256]{3,2,1,0:T(8,128)(2,1)S(1)} collective-permute-done((bf16[1,6,104,256]{3,2,1,0:T(8,128)(2,1)S(1)}, bf16[1,6,104,256]{3,2,1,0:T(8,128)(2,1)S(1)}, u32[]{:S(2)}, u32[]{:S(2)}) %collective-permute-start.5) | collective-permute-done | bytes 319520 | tf_op jit(solution)/shard_map/ppermute | solution.py:319
  19.2 0.0 copy-done.7
  19.2 0.0 copy-start
  19.2 0.0 copy-start.4
  19.2 0.1 before.2
  19.3 2.2 %collective-permute-start.11 = (bf16[1,8,104,256]{3,2,1,0:T(8,128)(2,1)S(1)}, bf16[1,8,104,256]{3,2,1,0:T(8,128)(2,1)S(1)}, u32[]{:S(2)}, u32[]{:S(2)}) collective-permute-start(bf16[1,8,104,256]{3,2,1,0:T(8,128)(2,1)S(1)} %get-tuple-element.34.last.refs_2_.refs_3_), channel_id=1, source_target_pairs={{0,4},{4,8},{8,12},{12,16},{16,20},{20,24},{24,28},{28,0},{1,5},{5... | collective-permute-start | bytes 1277960 | tf_op jit(solution)/shard_map/ppermute | solution.py:319
  21.5 0.0 copy-done
  21.5 0.0 copy-done.4
  21.5 1.4 %last.5._.acc_in = f32[832,256]{1,0:T(8,128)S(1)} custom-call(bf16[1,8,104,256]{3,2,1,0:T(8,128)(2,1)S(1)} %get-tuple-element.34.last.refs_2_.refs_3_, bf16[256]{0:T(256)(128)(2,1)S(1)} %copy-done.4, bf16[3,3,768,256]{3,2,1,0:T(8,128)(2,1)S(1)} %bitcast.3), custom_call_target="tpu_custom_call" | custom-call | flops 981467136 | bytes 2097152 | tf_op jit(solution)/shard_map/last/pallas_call | solution.py:284
  22.9 0.4 collective-permute-done.frame
  23.3 0.1 earliest.1.frame.refs_0_.refs_1_.first
  23.4 0.1 collective-permute-start.8
  23.5 1.2 %collective-permute-start.9 = (bf16[2,104,256]{2,1,0:T(8,128)(2,1)S(1)}, bf16[2,104,256]{2,1,0:T(8,128)(2,1)S(1)}, u32[]{:S(2)}, u32[]{:S(2)}) collective-permute-start(bf16[2,104,256]{2,1,0:T(8,128)(2,1)S(1)} %get-tuple-element.37), channel_id=1, source_target_pairs={{0,3},{1,2},{2,1},{3,0},{4,7},{5,6},{6,5},{7,4},{8,11},{9,10},{10,... | collective-permute-start | bytes 319496 | tf_op jit(solution)/shard_map/ppermute | solution.py:309
  24.7 1.4 %ahead.1 = (bf16[1,6,104,256]{3,2,1,0:T(8,128)(2,1)S(1)}, f32[2,104,256]{2,1,0:T(8,128)S(1)}) custom-call(bf16[1,8,104,256]{3,2,1,0:T(8,128)(2,1)S(1)} %earliest.1.frame.refs_0_.refs_1_.first, bf16[256]{0:T(256)(128)(2,1)S(1)} %copy-done.4, bf16[3,3,768,256]{3,2,1,0:T(8,128)(2,1)S(1)} %bitcast.4), custom_call_target="tpu_custom_call" | custom-call | flops 981467136 | bytes 2097152 | tf_op jit(solution)/shard_map/ahead/pallas_call | solution.py:284
  26.1 4.0 %collective-permute-start.7 = (bf16[1,6,104,256]{3,2,1,0:T(8,128)(2,1)S(1)}, bf16[1,6,104,256]{3,2,1,0:T(8,128)(2,1)S(1)}, u32[]{:S(2)}, u32[]{:S(2)}) collective-permute-start(bf16[1,6,104,256]{3,2,1,0:T(8,128)(2,1)S(1)} %get-tuple-element.35), channel_id=1, source_target_pairs={{0,4},{4,8},{8,12},{12,16},{16,20},{20,24},{24,28},{28,0},{1,5},{5... | collective-permute-start | bytes 958472 | tf_op jit(solution)/shard_map/ppermute | solution.py:319
  30.1 0.0 collective-permute-done.8.inward.refs_2_.up.last_up
  30.1 0.0 collective-permute-done.9.outward.down.last_down
  30.1 0.4 ends.1
  30.5 4.6 %collective-permute-start.10 = (bf16[2,104,256]{2,1,0:T(8,128)(2,1)S(1)}, bf16[2,104,256]{2,1,0:T(8,128)(2,1)S(1)}, u32[]{:S(2)}, u32[]{:S(2)}) collective-permute-start(bf16[2,104,256]{2,1,0:T(8,128)(2,1)S(1)} %ends.1), channel_id=1, source_target_pairs={{0,4},{4,8},{8,12},{12,16},{16,20},{20,24},{24,28},{1,5},{5,9},{9,... | collective-permute-start | bytes 319496 | tf_op jit(solution)/shard_map/ppermute | solution.py:319
  35.1 0.0 collective-permute-done.11.refs_0_.refs_1_
  35.1 0.7 %collective-permute-start.13 = (bf16[1,104,256]{2,1,0:T(8,128)(2,1)S(1)}, bf16[1,104,256]{2,1,0:T(8,128)(2,1)S(1)}, u32[]{:S(2)}, u32[]{:S(2)}) collective-permute-start(bf16[1,104,256]{2,1,0:T(8,128)(2,1)S(1)} %get-tuple-element.40), channel_id=1, source_target_pairs={{0,3},{1,2},{2,1},{3,0},{4,7},{5,6},{6,5},{7,4},{8,11},{9,10},{10,... | collective-permute-start | bytes 159752 | tf_op jit(solution)/shard_map/ppermute | solution.py:309
  35.9 0.0 copy-start.5
  35.9 0.2 collective-permute-start.12
  36.1 2.5 %first.5 = (f32[832,256]{1,0:T(8,128)S(1)}, f32[832,256]{1,0:T(8,128)S(1)}) custom-call(bf16[1,8,104,256]{3,2,1,0:T(8,128)(2,1)S(1)} %earliest.1.frame.refs_0_.refs_1_.first, bf16[2,104,256]{2,1,0:T(8,128)(2,1)S(1)} %collective-permute-done.8.inward.refs_2_.up.last_up, bf16[2,104,256]{2,1,0:T(8,128)(2,1)S(1)} %collective-permute-done.9.outward.down.last_down, ...), custom_call_target="tpu_custom_call" | custom-call | flops 1962934272 | bytes 4194304 | tf_op jit(solution)/shard_map/first/pallas_call | solution.py:284
  38.6 0.7 %collective-permute-done.13.refs_2_ = bf16[1,104,256]{2,1,0:T(8,128)(2,1)S(1)} collective-permute-done((bf16[1,104,256]{2,1,0:T(8,128)(2,1)S(1)}, bf16[1,104,256]{2,1,0:T(8,128)(2,1)S(1)}, u32[]{:S(2)}, u32[]{:S(2)}) %collective-permute-start.13) | collective-permute-done | bytes 53280 | tf_op jit(solution)/shard_map/ppermute | solution.py:309
  39.2 0.0 collective-permute-done.12.refs_1_
  39.2 0.0 copy-done.5
  39.2 0.9 %before.3 = (bf16[2,8,104,256]{3,2,1,0:T(8,128)(2,1)}, f32[832,256]{1,0:T(8,128)S(1)}) custom-call(bf16[1,8,104,256]{3,2,1,0:T(8,128)(2,1)S(1)} %collective-permute-done.11.refs_0_.refs_1_, bf16[1,104,256]{2,1,0:T(8,128)(2,1)S(1)} %collective-permute-done.12.refs_1_, bf16[1,104,256]{2,1,0:T(8,128)(2,1)S(1)} %collective-permute-done.13.refs_2_, ...), custom_call_target="tpu_custom_call" | custom-call | flops 1962934272 | bytes 4194304 | tf_op jit(solution)/shard_map/before/pallas_call | solution.py:284
  40.1 0.5 %collective-permute-done.10.edges = bf16[2,104,256]{2,1,0:T(8,128)(2,1)S(1)} collective-permute-done((bf16[2,104,256]{2,1,0:T(8,128)(2,1)S(1)}, bf16[2,104,256]{2,1,0:T(8,128)(2,1)S(1)}, u32[]{:S(2)}, u32[]{:S(2)}) %collective-permute-start.10) | collective-permute-done | bytes 106528 | tf_op jit(solution)/shard_map/ppermute | solution.py:319
  40.6 0.7 %collective-permute-done.7.inner = bf16[1,6,104,256]{3,2,1,0:T(8,128)(2,1)S(1)} collective-permute-done((bf16[1,6,104,256]{3,2,1,0:T(8,128)(2,1)S(1)}, bf16[1,6,104,256]{3,2,1,0:T(8,128)(2,1)S(1)}, u32[]{:S(2)}, u32[]{:S(2)}) %collective-permute-start.7) | collective-permute-done | bytes 319520 | tf_op jit(solution)/shard_map/ppermute | solution.py:319
  41.3 0.9 %sum.1 = bf16[2,8,104,256]{3,2,1,0:T(8,128)(2,1)} custom-call(bf16[1,6,104,256]{3,2,1,0:T(8,128)(2,1)S(1)} %collective-permute-done.7.inner, bf16[2,104,256]{2,1,0:T(8,128)(2,1)S(1)} %collective-permute-done.10.edges, f32[832,256]{1,0:T(8,128)S(1)} %get-tuple-element.43.acc_first, bf16[256]{0:T(256)(128)(2,1)S(1)} %copy-done.5, ...), custom_call_target="tpu_custom_call", output_to_operand_aliasing={{}: (5, {})} | custom-call | tf_op jit(solution)/shard_map/sum/pallas_call | solution.py:284
  (5 shorter events, 0.1 us)
Async XLA Ops:
  0.0 14.9 %copy-start.6 = (bf16[256]{0:T(256)(128)(2,1)S(1)}, bf16[256]{0:T(256)(128)(2,1)}, u32[]{:S(2)}) copy-start(bf16[256]{0:T(256)(128)(2,1)} %gain.8) | copy-start | bytes 1540
  1.0 11.3 %collective-permute-start.1 = (bf16[4,104,256]{2,1,0:T(8,128)(2,1)S(1)}, bf16[4,104,256]{2,1,0:T(8,128)(2,1)S(1)}, u32[]{:S(2)}, u32[]{:S(2)}) collective-permute-start(bf16[4,104,256]{2,1,0:T(8,128)(2,1)S(1)} %bitcast.15), channel_id=1, source_target_pairs={{0,4},{4,8},{8,12},{12,16},{16,20},{20,24},{24,28},{28,0},{1,5},{5... | collective-permute-start | bytes 638984 | tf_op jit(solution)/shard_map/ppermute | solution.py:319
  4.0 1.2 %copy-start.1 = (bf16[2,8,104,256]{3,2,1,0:T(8,128)(2,1)S(1)}, bf16[2,8,104,256]{3,2,1,0:T(8,128)(2,1)}, u32[]{:S(2)}) copy-start(bf16[2,8,104,256]{3,2,1,0:T(8,128)(2,1)} %residual.1) | copy-start | bytes 2555908
  5.1 1.8 %copy-start.2 = (bf16[2,8,104,256]{3,2,1,0:T(8,128)(2,1)S(1)}, bf16[2,8,104,256]{3,2,1,0:T(8,128)(2,1)}, u32[]{:S(2)}) copy-start(bf16[2,8,104,256]{3,2,1,0:T(8,128)(2,1)} %residual.1) | copy-start | bytes 2555908
  5.1 9.7 %copy-start.3 = (bf16[3,3,3,256,256]{4,3,2,1,0:T(8,128)(2,1)S(1)}, bf16[3,3,3,256,256]{4,3,2,1,0:T(8,128)(2,1)}, u32[]{:S(2)}) copy-start(bf16[3,3,3,256,256]{4,3,2,1,0:T(8,128)(2,1)} %param.9) | copy-start | bytes 10616836
  5.1 6.8 %collective-permute-start.2 = (bf16[2,104,256]{2,1,0:T(8,128)(2,1)S(1)}, bf16[2,104,256]{2,1,0:T(8,128)(2,1)S(1)}, u32[]{:S(2)}, u32[]{:S(2)}) collective-permute-start(bf16[2,104,256]{2,1,0:T(8,128)(2,1)S(1)} %get-tuple-element.25._), channel_id=1, source_target_pairs={{0,1},{1,0},{2,3},{3,2},{4,5},{5,4},{6,7},{7,6},{8,9},{9,8},{10,11... | collective-permute-start | bytes 319496 | tf_op jit(solution)/shard_map/ppermute | solution.py:310
  5.2 9.6 %collective-permute-start.6 = (bf16[2,104,256]{2,1,0:T(8,128)(2,1)S(1)}, bf16[2,104,256]{2,1,0:T(8,128)(2,1)S(1)}, u32[]{:S(2)}, u32[]{:S(2)}) collective-permute-start(bf16[2,104,256]{2,1,0:T(8,128)(2,1)S(1)} %get-tuple-element.30), channel_id=1, source_target_pairs={{0,3},{1,2},{2,1},{3,0},{4,7},{5,6},{6,5},{7,4},{8,11},{9,10},{10,... | collective-permute-start | bytes 319496 | tf_op jit(solution)/shard_map/ppermute | solution.py:309
  6.9 12.3 %collective-permute-start.5 = (bf16[1,6,104,256]{3,2,1,0:T(8,128)(2,1)S(1)}, bf16[1,6,104,256]{3,2,1,0:T(8,128)(2,1)S(1)}, u32[]{:S(2)}, u32[]{:S(2)}) collective-permute-start(bf16[1,6,104,256]{3,2,1,0:T(8,128)(2,1)S(1)} %get-tuple-element.29), channel_id=1, source_target_pairs={{0,4},{4,8},{8,12},{12,16},{16,20},{20,24},{24,28},{28,0},{1,5},{5... | collective-permute-start | bytes 958472 | tf_op jit(solution)/shard_map/ppermute | solution.py:319
  8.5 14.8 %collective-permute-start = (bf16[1,6,104,256]{3,2,1,0:T(8,128)(2,1)S(1)}, bf16[1,6,104,256]{3,2,1,0:T(8,128)(2,1)S(1)}, u32[]{:S(2)}, u32[]{:S(2)}) collective-permute-start(bf16[1,6,104,256]{3,2,1,0:T(8,128)(2,1)S(1)} %get-tuple-element.26), channel_id=1, source_target_pairs={{0,4},{4,8},{8,12},{12,16},{16,20},{20,24},{24,28},{1,5},{5,9},{9,... | collective-permute-start | bytes 958472 | tf_op jit(solution)/shard_map/ppermute | solution.py:319
  12.3 6.1 %collective-permute-start.4 = (bf16[2,104,256]{2,1,0:T(8,128)(2,1)S(1)}, bf16[2,104,256]{2,1,0:T(8,128)(2,1)S(1)}, u32[]{:S(2)}, u32[]{:S(2)}) collective-permute-start(bf16[2,104,256]{2,1,0:T(8,128)(2,1)S(1)} %get-tuple-element.28), channel_id=1, source_target_pairs={{0,3},{1,2},{2,1},{3,0},{4,7},{5,6},{6,5},{7,4},{8,11},{9,10},{10,... | collective-permute-start | bytes 319496 | tf_op jit(solution)/shard_map/ppermute | solution.py:309
  12.5 5.8 %collective-permute-start.3 = (bf16[2,104,256]{2,1,0:T(8,128)(2,1)S(1)}, bf16[2,104,256]{2,1,0:T(8,128)(2,1)S(1)}, u32[]{:S(2)}, u32[]{:S(2)}) collective-permute-start(bf16[2,104,256]{2,1,0:T(8,128)(2,1)S(1)} %get-tuple-element.27._), channel_id=1, source_target_pairs={{0,1},{1,0},{2,3},{3,2},{4,5},{5,4},{6,7},{7,6},{8,9},{9,8},{10,11... | collective-permute-start | bytes 319496 | tf_op jit(solution)/shard_map/ppermute | solution.py:310
  14.9 4.3 %copy-start.7 = (bf16[256]{0:T(256)(128)(2,1)S(1)}, bf16[256]{0:T(256)(128)(2,1)}, u32[]{:S(2)}) copy-start(bf16[256]{0:T(256)(128)(2,1)} %bias.2) | copy-start | bytes 1540
  19.2 2.3 %copy-start = (bf16[3,3,3,256,256]{4,3,2,1,0:T(8,128)(2,1)S(1)}, bf16[3,3,3,256,256]{4,3,2,1,0:T(8,128)(2,1)}, u32[]{:S(2)}) copy-start(bf16[3,3,3,256,256]{4,3,2,1,0:T(8,128)(2,1)} %param.12) | copy-start | bytes 10616836
  19.2 2.3 %copy-start.4 = (bf16[256]{0:T(256)(128)(2,1)S(1)}, bf16[256]{0:T(256)(128)(2,1)}, u32[]{:S(2)}) copy-start(bf16[256]{0:T(256)(128)(2,1)} %refs_3_.3) | copy-start | bytes 1540
  19.3 15.8 %collective-permute-start.11 = (bf16[1,8,104,256]{3,2,1,0:T(8,128)(2,1)S(1)}, bf16[1,8,104,256]{3,2,1,0:T(8,128)(2,1)S(1)}, u32[]{:S(2)}, u32[]{:S(2)}) collective-permute-start(bf16[1,8,104,256]{3,2,1,0:T(8,128)(2,1)S(1)} %get-tuple-element.34.last.refs_2_.refs_3_), channel_id=1, source_target_pairs={{0,4},{4,8},{8,12},{12,16},{16,20},{20,24},{24,28},{28,0},{1,5},{5... | collective-permute-start | bytes 1277960 | tf_op jit(solution)/shard_map/ppermute | solution.py:319
  23.4 6.7 %collective-permute-start.8 = (bf16[2,104,256]{2,1,0:T(8,128)(2,1)S(1)}, bf16[2,104,256]{2,1,0:T(8,128)(2,1)S(1)}, u32[]{:S(2)}, u32[]{:S(2)}) collective-permute-start(bf16[2,104,256]{2,1,0:T(8,128)(2,1)S(1)} %get-tuple-element.36), channel_id=1, source_target_pairs={{0,1},{1,0},{2,3},{3,2},{4,5},{5,4},{6,7},{7,6},{8,9},{9,8},{10,11... | collective-permute-start | bytes 319496 | tf_op jit(solution)/shard_map/ppermute | solution.py:310
  23.5 6.7 %collective-permute-start.9 = (bf16[2,104,256]{2,1,0:T(8,128)(2,1)S(1)}, bf16[2,104,256]{2,1,0:T(8,128)(2,1)S(1)}, u32[]{:S(2)}, u32[]{:S(2)}) collective-permute-start(bf16[2,104,256]{2,1,0:T(8,128)(2,1)S(1)} %get-tuple-element.37), channel_id=1, source_target_pairs={{0,3},{1,2},{2,1},{3,0},{4,7},{5,6},{6,5},{7,4},{8,11},{9,10},{10,... | collective-permute-start | bytes 319496 | tf_op jit(solution)/shard_map/ppermute | solution.py:309
  26.1 15.2 %collective-permute-start.7 = (bf16[1,6,104,256]{3,2,1,0:T(8,128)(2,1)S(1)}, bf16[1,6,104,256]{3,2,1,0:T(8,128)(2,1)S(1)}, u32[]{:S(2)}, u32[]{:S(2)}) collective-permute-start(bf16[1,6,104,256]{3,2,1,0:T(8,128)(2,1)S(1)} %get-tuple-element.35), channel_id=1, source_target_pairs={{0,4},{4,8},{8,12},{12,16},{16,20},{20,24},{24,28},{28,0},{1,5},{5... | collective-permute-start | bytes 958472 | tf_op jit(solution)/shard_map/ppermute | solution.py:319
  30.5 10.1 %collective-permute-start.10 = (bf16[2,104,256]{2,1,0:T(8,128)(2,1)S(1)}, bf16[2,104,256]{2,1,0:T(8,128)(2,1)S(1)}, u32[]{:S(2)}, u32[]{:S(2)}) collective-permute-start(bf16[2,104,256]{2,1,0:T(8,128)(2,1)S(1)} %ends.1), channel_id=1, source_target_pairs={{0,4},{4,8},{8,12},{12,16},{16,20},{20,24},{24,28},{1,5},{5,9},{9,... | collective-permute-start | bytes 319496 | tf_op jit(solution)/shard_map/ppermute | solution.py:319
  35.1 4.1 %collective-permute-start.13 = (bf16[1,104,256]{2,1,0:T(8,128)(2,1)S(1)}, bf16[1,104,256]{2,1,0:T(8,128)(2,1)S(1)}, u32[]{:S(2)}, u32[]{:S(2)}) collective-permute-start(bf16[1,104,256]{2,1,0:T(8,128)(2,1)S(1)} %get-tuple-element.40), channel_id=1, source_target_pairs={{0,3},{1,2},{2,1},{3,0},{4,7},{5,6},{6,5},{7,4},{8,11},{9,10},{10,... | collective-permute-start | bytes 159752 | tf_op jit(solution)/shard_map/ppermute | solution.py:309
  35.9 3.4 %copy-start.5 = (bf16[256]{0:T(256)(128)(2,1)S(1)}, bf16[256]{0:T(256)(128)(2,1)}, u32[]{:S(2)}) copy-start(bf16[256]{0:T(256)(128)(2,1)} %bias.3) | copy-start | bytes 1540
  35.9 3.4 %collective-permute-start.12 = (bf16[1,104,256]{2,1,0:T(8,128)(2,1)S(1)}, bf16[1,104,256]{2,1,0:T(8,128)(2,1)S(1)}, u32[]{:S(2)}, u32[]{:S(2)}) collective-permute-start(bf16[1,104,256]{2,1,0:T(8,128)(2,1)S(1)} %get-tuple-element.39._), channel_id=1, source_target_pairs={{0,1},{1,0},{2,3},{3,2},{4,5},{5,4},{6,7},{7,6},{8,9},{9,8},{10,11... | collective-permute-start | bytes 159752 | tf_op jit(solution)/shard_map/ppermute | solution.py:310

commit v7 on v6

--- a/solution.py
+++ b/solution.py
@@ -121,13 +121,14 @@
         acc_last[s : s + n] = taps(even, odd, k2, s, n, cells)
 
 
-def own_first_kernel(first, up, down, last_up, last_down, gain, k1, k2, acc_in, _, acc_first, acc_last, *bufs):
+def own_first_kernel(first, up, down, last_up, last_down, gain, k1, k2, bias, residual, acc_in, _, acc_first, acc_last, *bufs):
     rows, cells = first.shape[1], first.shape[2]
     even, odd = bufs[1:]
     load_frame(first.at[0], up[0], down[0], gain, bufs)
     for s, n in chunks(rows, cells):
         acc_last[s : s + n] = acc_in[s : s + n] + taps(even, odd, k1, s, n, cells)
-        acc_first[s : s + n] = taps(even, odd, k2, s, n, cells)
+        share = residual[0, s // cells : (s + n) // cells].astype(F32).reshape(n, -1) + bias[...].astype(F32)[None]
+        acc_first[s : s + n] = share + taps(even, odd, k2, s, n, cells)
     lower = lax.axis_index("height") % 2 == 0
     weight = gain[...].astype(F32)[None]
     for edge, mask in enumerate(masks()):
@@ -252,15 +253,14 @@
     return jnp.where(lax.axis_index("tm") > 0, value.astype(F32), 0.0)
 
 
-def sum_kernel(inner, edges, acc_first, bias, residual, _, out, rows, sems):
-    count, cells = residual.shape[1], residual.shape[2]
+def sum_kernel(inner, edges, acc_first, _, out, rows, sems):
+    count, cells = rows.shape[0], rows.shape[1]
     copies = []
     for n in range(2):
         low, high = n * (count // 2), (n + 1) * (count // 2)
         for r in range(low, high):
             ahead = edges[0 if r == 0 else 1] if r in (0, count - 1) else inner[0, r - 1]
-            total = acc_first[r * cells : (r + 1) * cells] + bias[...].astype(F32)[None] + received(ahead)
-            rows[r] = (residual[0, r].astype(F32) + total).astype(BF16)
+            rows[r] = (acc_first[r * cells : (r + 1) * cells] + received(ahead)).astype(BF16)
         half = pl.ds(low, count // 2)
         copies.append(pltpu.make_async_copy(rows.at[half], out.at[0, half], sems.at[n]))
         copies[-1].start()
@@ -343,10 +343,11 @@
     return call(own_last_kernel, "last", 1, [whole(acc.shape)], [acc], [last, gain, k[2]])[0]
 
 
-def own_first(first, up, down, gain, k, acc_last, token):
+def own_first(first, up, down, gain, k, bias, latents, acc_last, token):
     acc = shapes()[0]
     up, down = pairs(up, 1), pairs(down, 1)
-    args = [first, up[0], down[0], up[1], down[1], gain, k[1], k[2], w(acc_last), rest(token)]
+    args = [first, up[0], down[0], up[1], down[1], gain, k[1], k[2], bias]
+    args += [(latents, part(latents.shape, 0)), w(acc_last), rest(token)]
     return call(own_first_kernel, "first", 2, [whole(acc.shape)] * 2, [acc, acc], args)
 
 
@@ -470,7 +471,7 @@
     (edges_ahead,) = call(edges_kernel, "ends", 0, [whole(edge.shape)], [edge], args, scratch=columns)
     edges_ahead = shift(edges_ahead, False)
     sides = rows_after(up, (before, (0, 0), (0, bottom)))
-    acc_first, acc_last = own_first(w(y_first), up, down, gain, k, acc_last, sides[0])
+    acc_first, acc_last = own_first(w(y_first), up, down, gain, k, bias, latents, acc_last, sides[0])
 
     out = jax.ShapeDtypeStruct(latents.shape, BF16)
     anywhere = pl.BlockSpec(memory_space=pl.ANY)
@@ -492,7 +493,7 @@
         args,
         scratch=scratch + extra,
     )
-    args = [w(inner_ahead), w(edges_ahead), w(acc_first), bias, (latents, part(latents.shape, 0)), rest(half)]
+    args = [w(inner_ahead), w(edges_ahead), w(acc_first), rest(half)]
     return call(sum_kernel, "sum", 0, anywhere, out, args, {len(args) - 1: 0}, extra, 12 * 2**20)
 
 

time: 42.6 us -> 42.6 us (level)
  transfers between devices with their start and end apart: 14 -> 14, of which waited for: 6 -> 6; matrix products, arithmetic and copies ran while one was open for 0% -> 0% of each run, Pallas kernels for 24% -> 25%
where the time goes in v7:
time: 42.6 us; the launch traced here: 42.4 us
  starting transfers between devices  25.3 us (59%)
  Pallas kernels  11.3 us (27%)
  waiting for transfers between devices  3.2 us (8%)
  local copies, waits for them, and re-layouts  2.15 us (5%)
    ppermute x6, starting transfers between devices, shift(): return lax.ppermute(array, 'tm', route if closed else route[:-1])  18.8 us
    pallas_call x9, Pallas kernels, call(): pl.pallas_call(body, grid=(1,), in_specs=[s for _, s in args], out_specs=...  11.2 us
    ppermute x4, starting transfers between devices, exchange_rows(): outward = lax.ppermute(outward, 'height', others)  3.83 us
    ppermute x4, starting transfers between devices, exchange_rows(): return (lax.ppermute(inward, 'height', pairs), outward)  2.73 us
    ppermute x6, waiting for transfers between devices, shift(): return lax.ppermute(array, 'tm', route if closed else route[:-1])  2.55 us
    unnamed x16, local copies, waits for them, and re-layouts  1.19 us
    slice x1, local copies, waits for them, and re-layouts, first_section(): edges = latents[:, ::bottom].reshape(4, *latents.shape[2:])  0.96 us
  transfers between devices with their start and end apart: 14, of which 6 were waited for; matrix products, arithmetic and copies ran while one was open for 0% of the time, Pallas kernels for 25%

profile of v7, /device:TPU:0, one launch (start us, length us, event | category | flops | bytes accessed | tf_op | source)
XLA Modules:
  0.0 42.4 jit_solution(15265266549952946747)
XLA Ops:
  0.0 0.0 copy-start.6
  0.0 1.0 %slice.3 = bf16[2,2,104,256]{3,2,1,0:T(8,128)(2,1)S(1)} slice(bf16[2,8,104,256]{3,2,1,0:T(8,128)(2,1)} %refs_9_.1), slice={[0:2:1], [0:8:7], [0:104:1], [0:256:1]} | slice | bytes 425984 | tf_op jit(solution)/shard_map/slice | solution.py:422
  1.0 3.0 %collective-permute-start.1 = (bf16[4,104,256]{2,1,0:T(8,128)(2,1)S(1)}, bf16[4,104,256]{2,1,0:T(8,128)(2,1)S(1)}, u32[]{:S(2)}, u32[]{:S(2)}) collective-permute-start(bf16[4,104,256]{2,1,0:T(8,128)(2,1)S(1)} %bitcast.15), channel_id=1, source_target_pairs={{0,4},{4,8},{8,12},{12,16},{16,20},{20,24},{24,28},{28,0},{1,5},{5... | collective-permute-start | bytes 638984 | tf_op jit(solution)/shard_map/ppermute | solution.py:319
  4.0 0.0 copy-start.1
  4.0 1.2 %copy-done.1 = bf16[2,8,104,256]{3,2,1,0:T(8,128)(2,1)S(1)} copy-done((bf16[2,8,104,256]{3,2,1,0:T(8,128)(2,1)S(1)}, bf16[2,8,104,256]{3,2,1,0:T(8,128)(2,1)}, u32[]{:S(2)}) %copy-start.1) | copy-done | bytes 851992
  5.1 0.0 copy-start.2
  5.1 0.0 copy-start.3
  5.1 0.1 collective-permute-start.2
  5.2 1.6 %collective-permute-start.6 = (bf16[2,104,256]{2,1,0:T(8,128)(2,1)S(1)}, bf16[2,104,256]{2,1,0:T(8,128)(2,1)S(1)}, u32[]{:S(2)}, u32[]{:S(2)}) collective-permute-start(bf16[2,104,256]{2,1,0:T(8,128)(2,1)S(1)} %get-tuple-element.30), channel_id=1, source_target_pairs={{0,3},{1,2},{2,1},{3,0},{4,7},{5,6},{6,5},{7,4},{8,11},{9,10},{10,... | collective-permute-start | bytes 319496 | tf_op jit(solution)/shard_map/ppermute | solution.py:309
  6.9 0.0 copy-done.2
  6.9 1.6 %collective-permute-start.5 = (bf16[1,6,104,256]{3,2,1,0:T(8,128)(2,1)S(1)}, bf16[1,6,104,256]{3,2,1,0:T(8,128)(2,1)S(1)}, u32[]{:S(2)}, u32[]{:S(2)}) collective-permute-start(bf16[1,6,104,256]{3,2,1,0:T(8,128)(2,1)S(1)} %get-tuple-element.29), channel_id=1, source_target_pairs={{0,4},{4,8},{8,12},{12,16},{16,20},{20,24},{24,28},{28,0},{1,5},{5... | collective-permute-start | bytes 958472 | tf_op jit(solution)/shard_map/ppermute | solution.py:319
  8.5 3.4 %collective-permute-start = (bf16[1,6,104,256]{3,2,1,0:T(8,128)(2,1)S(1)}, bf16[1,6,104,256]{3,2,1,0:T(8,128)(2,1)S(1)}, u32[]{:S(2)}, u32[]{:S(2)}) collective-permute-start(bf16[1,6,104,256]{3,2,1,0:T(8,128)(2,1)S(1)} %get-tuple-element.26), channel_id=1, source_target_pairs={{0,4},{4,8},{8,12},{12,16},{16,20},{20,24},{24,28},{1,5},{5,9},{9,... | collective-permute-start | bytes 958472 | tf_op jit(solution)/shard_map/ppermute | solution.py:319
  11.9 0.0 collective-permute-done.2.refs_4_.up
  11.9 0.3 collective-permute-done.1.refs_0_.refs_1_.refs_2_.refs_3_.edges
  12.3 0.3 collective-permute-start.4
  12.5 2.3 %collective-permute-start.3 = (bf16[2,104,256]{2,1,0:T(8,128)(2,1)S(1)}, bf16[2,104,256]{2,1,0:T(8,128)(2,1)S(1)}, u32[]{:S(2)}, u32[]{:S(2)}) collective-permute-start(bf16[2,104,256]{2,1,0:T(8,128)(2,1)S(1)} %get-tuple-element.27._), channel_id=1, source_target_pairs={{0,1},{1,0},{2,3},{3,2},{4,5},{5,4},{6,7},{7,6},{8,9},{9,8},{10,11... | collective-permute-start | bytes 319496 | tf_op jit(solution)/shard_map/ppermute | solution.py:310
  14.9 0.0 collective-permute-done.6.down
  14.9 0.0 copy-done.6
  14.9 0.0 copy-done.3
  14.9 0.0 copy-start.7
  14.9 3.5 %own.1 = (f32[832,256]{1,0:T(8,128)S(1)}, f32[832,256]{1,0:T(8,128)S(1)}) custom-call(bf16[2,8,104,256]{3,2,1,0:T(8,128)(2,1)S(1)} %copy-done.2, bf16[2,8,104,256]{3,2,1,0:T(8,128)(2,1)S(1)} %copy-done.2, bf16[2,104,256]{2,1,0:T(8,128)(2,1)S(1)} %collective-permute-done.2.refs_4_.up, bf16[2,104,256]{2,1,0:T(8,128)(2,1)S(1)} %collective-permute-done.6.down, ...), custom_call_target="tpu_custom_call" | custom-call | flops 2944401408 | bytes 6291456 | tf_op jit(solution)/shard_map/own/pallas_call | solution.py:284
  18.4 0.0 collective-permute-done.4.refs_3_.down
  18.4 0.0 collective-permute-done.3.refs_2_.up
  18.4 0.7 %collective-permute-done.5.refs_0_ = bf16[1,6,104,256]{3,2,1,0:T(8,128)(2,1)S(1)} collective-permute-done((bf16[1,6,104,256]{3,2,1,0:T(8,128)(2,1)S(1)}, bf16[1,6,104,256]{3,2,1,0:T(8,128)(2,1)S(1)}, u32[]{:S(2)}, u32[]{:S(2)}) %collective-permute-start.5) | collective-permute-done | bytes 319520 | tf_op jit(solution)/shard_map/ppermute | solution.py:319
  19.2 0.0 copy-done.7
  19.2 0.0 copy-start
  19.2 0.0 copy-start.4
  19.2 0.1 before.2
  19.3 2.2 %collective-permute-start.11 = (bf16[1,8,104,256]{3,2,1,0:T(8,128)(2,1)S(1)}, bf16[1,8,104,256]{3,2,1,0:T(8,128)(2,1)S(1)}, u32[]{:S(2)}, u32[]{:S(2)}) collective-permute-start(bf16[1,8,104,256]{3,2,1,0:T(8,128)(2,1)S(1)} %get-tuple-element.34.last.refs_2_.refs_3_), channel_id=1, source_target_pairs={{0,4},{4,8},{8,12},{12,16},{16,20},{20,24},{24,28},{28,0},{1,5},{5... | collective-permute-start | bytes 1277960 | tf_op jit(solution)/shard_map/ppermute | solution.py:319
  21.5 0.0 copy-done
  21.5 0.0 copy-done.4
  21.5 1.5 %last.5._.acc_in = f32[832,256]{1,0:T(8,128)S(1)} custom-call(bf16[1,8,104,256]{3,2,1,0:T(8,128)(2,1)S(1)} %get-tuple-element.34.last.refs_2_.refs_3_, bf16[256]{0:T(256)(128)(2,1)S(1)} %copy-done.4, bf16[3,3,768,256]{3,2,1,0:T(8,128)(2,1)S(1)} %bitcast.3), custom_call_target="tpu_custom_call" | custom-call | flops 981467136 | bytes 2097152 | tf_op jit(solution)/shard_map/last/pallas_call | solution.py:284
  23.0 0.3 collective-permute-done.frame
  23.3 0.1 earliest.1.frame.refs_0_.refs_1_.first
  23.4 0.1 collective-permute-start.8
  23.5 1.2 %collective-permute-start.9 = (bf16[2,104,256]{2,1,0:T(8,128)(2,1)S(1)}, bf16[2,104,256]{2,1,0:T(8,128)(2,1)S(1)}, u32[]{:S(2)}, u32[]{:S(2)}) collective-permute-start(bf16[2,104,256]{2,1,0:T(8,128)(2,1)S(1)} %get-tuple-element.37), channel_id=1, source_target_pairs={{0,3},{1,2},{2,1},{3,0},{4,7},{5,6},{6,5},{7,4},{8,11},{9,10},{10,... | collective-permute-start | bytes 319496 | tf_op jit(solution)/shard_map/ppermute | solution.py:309
  24.7 1.5 %ahead.1 = (bf16[1,6,104,256]{3,2,1,0:T(8,128)(2,1)S(1)}, f32[2,104,256]{2,1,0:T(8,128)S(1)}) custom-call(bf16[1,8,104,256]{3,2,1,0:T(8,128)(2,1)S(1)} %earliest.1.frame.refs_0_.refs_1_.first, bf16[256]{0:T(256)(128)(2,1)S(1)} %copy-done.4, bf16[3,3,768,256]{3,2,1,0:T(8,128)(2,1)S(1)} %bitcast.4), custom_call_target="tpu_custom_call" | custom-call | flops 981467136 | bytes 2097152 | tf_op jit(solution)/shard_map/ahead/pallas_call | solution.py:284
  26.2 0.0 copy-start.5
  26.2 4.0 %collective-permute-start.7 = (bf16[1,6,104,256]{3,2,1,0:T(8,128)(2,1)S(1)}, bf16[1,6,104,256]{3,2,1,0:T(8,128)(2,1)S(1)}, u32[]{:S(2)}, u32[]{:S(2)}) collective-permute-start(bf16[1,6,104,256]{3,2,1,0:T(8,128)(2,1)S(1)} %get-tuple-element.35), channel_id=1, source_target_pairs={{0,4},{4,8},{8,12},{12,16},{16,20},{20,24},{24,28},{28,0},{1,5},{5... | collective-permute-start | bytes 958472 | tf_op jit(solution)/shard_map/ppermute | solution.py:319
  30.1 0.0 collective-permute-done.8.inward.refs_2_.up.last_up
  30.2 0.0 collective-permute-done.9.outward.down.last_down
  30.2 0.4 ends.1
  30.5 4.6 %collective-permute-start.10 = (bf16[2,104,256]{2,1,0:T(8,128)(2,1)S(1)}, bf16[2,104,256]{2,1,0:T(8,128)(2,1)S(1)}, u32[]{:S(2)}, u32[]{:S(2)}) collective-permute-start(bf16[2,104,256]{2,1,0:T(8,128)(2,1)S(1)} %ends.1), channel_id=1, source_target_pairs={{0,4},{4,8},{8,12},{12,16},{16,20},{20,24},{24,28},{1,5},{5,9},{9,... | collective-permute-start | bytes 319496 | tf_op jit(solution)/shard_map/ppermute | solution.py:319
  35.1 0.0 collective-permute-done.11.refs_0_.refs_1_
  35.2 0.7 %collective-permute-start.13 = (bf16[1,104,256]{2,1,0:T(8,128)(2,1)S(1)}, bf16[1,104,256]{2,1,0:T(8,128)(2,1)S(1)}, u32[]{:S(2)}, u32[]{:S(2)}) collective-permute-start(bf16[1,104,256]{2,1,0:T(8,128)(2,1)S(1)} %get-tuple-element.40), channel_id=1, source_target_pairs={{0,3},{1,2},{2,1},{3,0},{4,7},{5,6},{6,5},{7,4},{8,11},{9,10},{10,... | collective-permute-start | bytes 159752 | tf_op jit(solution)/shard_map/ppermute | solution.py:309
  35.9 0.3 collective-permute-start.12
  36.1 0.0 copy-done.5
  36.2 2.5 %first.5 = (f32[832,256]{1,0:T(8,128)S(1)}, f32[832,256]{1,0:T(8,128)S(1)}) custom-call(bf16[1,8,104,256]{3,2,1,0:T(8,128)(2,1)S(1)} %earliest.1.frame.refs_0_.refs_1_.first, bf16[2,104,256]{2,1,0:T(8,128)(2,1)S(1)} %collective-permute-done.8.inward.refs_2_.up.last_up, bf16[2,104,256]{2,1,0:T(8,128)(2,1)S(1)} %collective-permute-done.9.outward.down.last_down, ...), custom_call_target="tpu_custom_call" | custom-call | flops 1962934272 | bytes 4194304 | tf_op jit(solution)/shard_map/first/pallas_call | solution.py:284
  38.7 0.6 %collective-permute-done.13.refs_2_ = bf16[1,104,256]{2,1,0:T(8,128)(2,1)S(1)} collective-permute-done((bf16[1,104,256]{2,1,0:T(8,128)(2,1)S(1)}, bf16[1,104,256]{2,1,0:T(8,128)(2,1)S(1)}, u32[]{:S(2)}, u32[]{:S(2)}) %collective-permute-start.13) | collective-permute-done | bytes 53280 | tf_op jit(solution)/shard_map/ppermute | solution.py:309
  39.3 0.0 collective-permute-done.12.refs_1_
  39.3 0.9 %before.3 = (bf16[2,8,104,256]{3,2,1,0:T(8,128)(2,1)}, f32[832,256]{1,0:T(8,128)S(1)}) custom-call(bf16[1,8,104,256]{3,2,1,0:T(8,128)(2,1)S(1)} %collective-permute-done.11.refs_0_.refs_1_, bf16[1,104,256]{2,1,0:T(8,128)(2,1)S(1)} %collective-permute-done.12.refs_1_, bf16[1,104,256]{2,1,0:T(8,128)(2,1)S(1)} %collective-permute-done.13.refs_2_, ...), custom_call_target="tpu_custom_call" | custom-call | flops 1962934272 | bytes 4194304 | tf_op jit(solution)/shard_map/before/pallas_call | solution.py:284
  40.2 0.5 %collective-permute-done.10.edges = bf16[2,104,256]{2,1,0:T(8,128)(2,1)S(1)} collective-permute-done((bf16[2,104,256]{2,1,0:T(8,128)(2,1)S(1)}, bf16[2,104,256]{2,1,0:T(8,128)(2,1)S(1)}, u32[]{:S(2)}, u32[]{:S(2)}) %collective-permute-start.10) | collective-permute-done | bytes 106528 | tf_op jit(solution)/shard_map/ppermute | solution.py:319
  40.6 0.7 %collective-permute-done.7.inner = bf16[1,6,104,256]{3,2,1,0:T(8,128)(2,1)S(1)} collective-permute-done((bf16[1,6,104,256]{3,2,1,0:T(8,128)(2,1)S(1)}, bf16[1,6,104,256]{3,2,1,0:T(8,128)(2,1)S(1)}, u32[]{:S(2)}, u32[]{:S(2)}) %collective-permute-start.7) | collective-permute-done | bytes 319520 | tf_op jit(solution)/shard_map/ppermute | solution.py:319
  41.4 0.8 %sum.1 = bf16[2,8,104,256]{3,2,1,0:T(8,128)(2,1)} custom-call(bf16[1,6,104,256]{3,2,1,0:T(8,128)(2,1)S(1)} %collective-permute-done.7.inner, bf16[2,104,256]{2,1,0:T(8,128)(2,1)S(1)} %collective-permute-done.10.edges, f32[832,256]{1,0:T(8,128)S(1)} %get-tuple-element.43.acc_first, ...), custom_call_target="tpu_custom_call", output_to_operand_aliasing={{}: (3, {})} | custom-call | tf_op jit(solution)/shard_map/sum/pallas_call | solution.py:284
  (5 shorter events, 0.1 us)
Async XLA Ops:
  0.0 14.9 %copy-start.6 = (bf16[256]{0:T(256)(128)(2,1)S(1)}, bf16[256]{0:T(256)(128)(2,1)}, u32[]{:S(2)}) copy-start(bf16[256]{0:T(256)(128)(2,1)} %gain.8) | copy-start | bytes 1540
  1.0 11.3 %collective-permute-start.1 = (bf16[4,104,256]{2,1,0:T(8,128)(2,1)S(1)}, bf16[4,104,256]{2,1,0:T(8,128)(2,1)S(1)}, u32[]{:S(2)}, u32[]{:S(2)}) collective-permute-start(bf16[4,104,256]{2,1,0:T(8,128)(2,1)S(1)} %bitcast.15), channel_id=1, source_target_pairs={{0,4},{4,8},{8,12},{12,16},{16,20},{20,24},{24,28},{28,0},{1,5},{5... | collective-permute-start | bytes 638984 | tf_op jit(solution)/shard_map/ppermute | solution.py:319
  4.0 1.2 %copy-start.1 = (bf16[2,8,104,256]{3,2,1,0:T(8,128)(2,1)S(1)}, bf16[2,8,104,256]{3,2,1,0:T(8,128)(2,1)}, u32[]{:S(2)}) copy-start(bf16[2,8,104,256]{3,2,1,0:T(8,128)(2,1)} %refs_9_.1) | copy-start | bytes 2555908
  5.1 1.8 %copy-start.2 = (bf16[2,8,104,256]{3,2,1,0:T(8,128)(2,1)S(1)}, bf16[2,8,104,256]{3,2,1,0:T(8,128)(2,1)}, u32[]{:S(2)}) copy-start(bf16[2,8,104,256]{3,2,1,0:T(8,128)(2,1)} %refs_9_.1) | copy-start | bytes 2555908
  5.1 9.7 %copy-start.3 = (bf16[3,3,3,256,256]{4,3,2,1,0:T(8,128)(2,1)S(1)}, bf16[3,3,3,256,256]{4,3,2,1,0:T(8,128)(2,1)}, u32[]{:S(2)}) copy-start(bf16[3,3,3,256,256]{4,3,2,1,0:T(8,128)(2,1)} %param.9) | copy-start | bytes 10616836
  5.1 6.8 %collective-permute-start.2 = (bf16[2,104,256]{2,1,0:T(8,128)(2,1)S(1)}, bf16[2,104,256]{2,1,0:T(8,128)(2,1)S(1)}, u32[]{:S(2)}, u32[]{:S(2)}) collective-permute-start(bf16[2,104,256]{2,1,0:T(8,128)(2,1)S(1)} %get-tuple-element.25._), channel_id=1, source_target_pairs={{0,1},{1,0},{2,3},{3,2},{4,5},{5,4},{6,7},{7,6},{8,9},{9,8},{10,11... | collective-permute-start | bytes 319496 | tf_op jit(solution)/shard_map/ppermute | solution.py:310
  5.2 9.6 %collective-permute-start.6 = (bf16[2,104,256]{2,1,0:T(8,128)(2,1)S(1)}, bf16[2,104,256]{2,1,0:T(8,128)(2,1)S(1)}, u32[]{:S(2)}, u32[]{:S(2)}) collective-permute-start(bf16[2,104,256]{2,1,0:T(8,128)(2,1)S(1)} %get-tuple-element.30), channel_id=1, source_target_pairs={{0,3},{1,2},{2,1},{3,0},{4,7},{5,6},{6,5},{7,4},{8,11},{9,10},{10,... | collective-permute-start | bytes 319496 | tf_op jit(solution)/shard_map/ppermute | solution.py:309
  6.9 12.3 %collective-permute-start.5 = (bf16[1,6,104,256]{3,2,1,0:T(8,128)(2,1)S(1)}, bf16[1,6,104,256]{3,2,1,0:T(8,128)(2,1)S(1)}, u32[]{:S(2)}, u32[]{:S(2)}) collective-permute-start(bf16[1,6,104,256]{3,2,1,0:T(8,128)(2,1)S(1)} %get-tuple-element.29), channel_id=1, source_target_pairs={{0,4},{4,8},{8,12},{12,16},{16,20},{20,24},{24,28},{28,0},{1,5},{5... | collective-permute-start | bytes 958472 | tf_op jit(solution)/shard_map/ppermute | solution.py:319
  8.5 14.8 %collective-permute-start = (bf16[1,6,104,256]{3,2,1,0:T(8,128)(2,1)S(1)}, bf16[1,6,104,256]{3,2,1,0:T(8,128)(2,1)S(1)}, u32[]{:S(2)}, u32[]{:S(2)}) collective-permute-start(bf16[1,6,104,256]{3,2,1,0:T(8,128)(2,1)S(1)} %get-tuple-element.26), channel_id=1, source_target_pairs={{0,4},{4,8},{8,12},{12,16},{16,20},{20,24},{24,28},{1,5},{5,9},{9,... | collective-permute-start | bytes 958472 | tf_op jit(solution)/shard_map/ppermute | solution.py:319
  12.3 6.1 %collective-permute-start.4 = (bf16[2,104,256]{2,1,0:T(8,128)(2,1)S(1)}, bf16[2,104,256]{2,1,0:T(8,128)(2,1)S(1)}, u32[]{:S(2)}, u32[]{:S(2)}) collective-permute-start(bf16[2,104,256]{2,1,0:T(8,128)(2,1)S(1)} %get-tuple-element.28), channel_id=1, source_target_pairs={{0,3},{1,2},{2,1},{3,0},{4,7},{5,6},{6,5},{7,4},{8,11},{9,10},{10,... | collective-permute-start | bytes 319496 | tf_op jit(solution)/shard_map/ppermute | solution.py:309
  12.5 5.9 %collective-permute-start.3 = (bf16[2,104,256]{2,1,0:T(8,128)(2,1)S(1)}, bf16[2,104,256]{2,1,0:T(8,128)(2,1)S(1)}, u32[]{:S(2)}, u32[]{:S(2)}) collective-permute-start(bf16[2,104,256]{2,1,0:T(8,128)(2,1)S(1)} %get-tuple-element.27._), channel_id=1, source_target_pairs={{0,1},{1,0},{2,3},{3,2},{4,5},{5,4},{6,7},{7,6},{8,9},{9,8},{10,11... | collective-permute-start | bytes 319496 | tf_op jit(solution)/shard_map/ppermute | solution.py:310
  14.9 4.3 %copy-start.7 = (bf16[256]{0:T(256)(128)(2,1)S(1)}, bf16[256]{0:T(256)(128)(2,1)}, u32[]{:S(2)}) copy-start(bf16[256]{0:T(256)(128)(2,1)} %bias.2) | copy-start | bytes 1540
  19.2 2.3 %copy-start = (bf16[3,3,3,256,256]{4,3,2,1,0:T(8,128)(2,1)S(1)}, bf16[3,3,3,256,256]{4,3,2,1,0:T(8,128)(2,1)}, u32[]{:S(2)}) copy-start(bf16[3,3,3,256,256]{4,3,2,1,0:T(8,128)(2,1)} %param.12) | copy-start | bytes 10616836
  19.2 2.3 %copy-start.4 = (bf16[256]{0:T(256)(128)(2,1)S(1)}, bf16[256]{0:T(256)(128)(2,1)}, u32[]{:S(2)}) copy-start(bf16[256]{0:T(256)(128)(2,1)} %refs_3_.3) | copy-start | bytes 1540
  19.3 15.9 %collective-permute-start.11 = (bf16[1,8,104,256]{3,2,1,0:T(8,128)(2,1)S(1)}, bf16[1,8,104,256]{3,2,1,0:T(8,128)(2,1)S(1)}, u32[]{:S(2)}, u32[]{:S(2)}) collective-permute-start(bf16[1,8,104,256]{3,2,1,0:T(8,128)(2,1)S(1)} %get-tuple-element.34.last.refs_2_.refs_3_), channel_id=1, source_target_pairs={{0,4},{4,8},{8,12},{12,16},{16,20},{20,24},{24,28},{28,0},{1,5},{5... | collective-permute-start | bytes 1277960 | tf_op jit(solution)/shard_map/ppermute | solution.py:319
  23.4 6.8 %collective-permute-start.8 = (bf16[2,104,256]{2,1,0:T(8,128)(2,1)S(1)}, bf16[2,104,256]{2,1,0:T(8,128)(2,1)S(1)}, u32[]{:S(2)}, u32[]{:S(2)}) collective-permute-start(bf16[2,104,256]{2,1,0:T(8,128)(2,1)S(1)} %get-tuple-element.36), channel_id=1, source_target_pairs={{0,1},{1,0},{2,3},{3,2},{4,5},{5,4},{6,7},{7,6},{8,9},{9,8},{10,11... | collective-permute-start | bytes 319496 | tf_op jit(solution)/shard_map/ppermute | solution.py:310
  23.5 6.7 %collective-permute-start.9 = (bf16[2,104,256]{2,1,0:T(8,128)(2,1)S(1)}, bf16[2,104,256]{2,1,0:T(8,128)(2,1)S(1)}, u32[]{:S(2)}, u32[]{:S(2)}) collective-permute-start(bf16[2,104,256]{2,1,0:T(8,128)(2,1)S(1)} %get-tuple-element.37), channel_id=1, source_target_pairs={{0,3},{1,2},{2,1},{3,0},{4,7},{5,6},{6,5},{7,4},{8,11},{9,10},{10,... | collective-permute-start | bytes 319496 | tf_op jit(solution)/shard_map/ppermute | solution.py:309
  26.2 10.0 %copy-start.5 = (bf16[256]{0:T(256)(128)(2,1)S(1)}, bf16[256]{0:T(256)(128)(2,1)}, u32[]{:S(2)}) copy-start(bf16[256]{0:T(256)(128)(2,1)} %refs_6_.1) | copy-start | bytes 1540
  26.2 15.2 %collective-permute-start.7 = (bf16[1,6,104,256]{3,2,1,0:T(8,128)(2,1)S(1)}, bf16[1,6,104,256]{3,2,1,0:T(8,128)(2,1)S(1)}, u32[]{:S(2)}, u32[]{:S(2)}) collective-permute-start(bf16[1,6,104,256]{3,2,1,0:T(8,128)(2,1)S(1)} %get-tuple-element.35), channel_id=1, source_target_pairs={{0,4},{4,8},{8,12},{12,16},{16,20},{20,24},{24,28},{28,0},{1,5},{5... | collective-permute-start | bytes 958472 | tf_op jit(solution)/shard_map/ppermute | solution.py:319
  30.5 10.1 %collective-permute-start.10 = (bf16[2,104,256]{2,1,0:T(8,128)(2,1)S(1)}, bf16[2,104,256]{2,1,0:T(8,128)(2,1)S(1)}, u32[]{:S(2)}, u32[]{:S(2)}) collective-permute-start(bf16[2,104,256]{2,1,0:T(8,128)(2,1)S(1)} %ends.1), channel_id=1, source_target_pairs={{0,4},{4,8},{8,12},{12,16},{16,20},{20,24},{24,28},{1,5},{5,9},{9,... | collective-permute-start | bytes 319496 | tf_op jit(solution)/shard_map/ppermute | solution.py:319
  35.2 4.1 %collective-permute-start.13 = (bf16[1,104,256]{2,1,0:T(8,128)(2,1)S(1)}, bf16[1,104,256]{2,1,0:T(8,128)(2,1)S(1)}, u32[]{:S(2)}, u32[]{:S(2)}) collective-permute-start(bf16[1,104,256]{2,1,0:T(8,128)(2,1)S(1)} %get-tuple-element.40), channel_id=1, source_target_pairs={{0,3},{1,2},{2,1},{3,0},{4,7},{5,6},{6,5},{7,4},{8,11},{9,10},{10,... | collective-permute-start | bytes 159752 | tf_op jit(solution)/shard_map/ppermute | solution.py:309
  35.9 3.4 %collective-permute-start.12 = (bf16[1,104,256]{2,1,0:T(8,128)(2,1)S(1)}, bf16[1,104,256]{2,1,0:T(8,128)(2,1)S(1)}, u32[]{:S(2)}, u32[]{:S(2)}) collective-permute-start(bf16[1,104,256]{2,1,0:T(8,128)(2,1)S(1)} %get-tuple-element.39._), channel_id=1, source_target_pairs={{0,1},{1,0},{2,3},{3,2},{4,5},{5,4},{6,7},{7,6},{8,9},{9,8},{10,11... | collective-permute-start | bytes 159752 | tf_op jit(solution)/shard_map/ppermute | solution.py:310
